TPU v7x, 32 devices: a whole 2x2x4 slice. The times are simulated.
32 devices in a mesh: grp: 2 (over y), row: 4 (over x, core), col: 4 (over z).
Axes of the slice: x: 2, y: 2, z: 4, core: 2. Of those that a mesh axis runs over, the one named last changes fastest.
Arguments:
- counts: int32 [16384, 32768], P(('grp', 'row'), 'col'), parts along dimension 0, may hold values from 0 to 255, as said below
- ctx_counts: int32 [65536], P(('grp', 'col')), parts along dimension 0, may hold values from 1000 to 119531
- omega: bfloat16 [32768, 512], P('col'), may hold values from -6 to 6
Outputs:
- basis: float32 [16384, 512], P(('grp', 'row', 'col')), parts along dimension 0
- projected: float32 [65536, 512], P(('grp', 'col'), 'row'), parts along dimension 0
There are 2 independent parts, one for each index of `grp`. A program takes and returns all parts, laid end to end along the dimension named above; an argument that names none is the same for every part. Nothing has to cross between parts.
Inputs may be any that keep to these rules, and one draw needn't show every extreme that they name: `counts`: every slab row has at least one positive count.
All inputs are finite; a program needn't handle non-finite values.
Results may differ from a plain program's by a relative error of at most 0.008.
Values may be sent and summed in bfloat16 or wider, within the bound.
No kernel may reach another device: no remote copies, remote signals or barrier semaphores. Data moves between devices by JAX's collectives and lax.ppermute only.
A program may use at most 256 MiB of HBM per device.

v0:
```python
import functools

import jax
import jax.numpy as jnp
from jax import lax
from jax.experimental import pallas as pl
from jax.experimental.pallas import tpu as pltpu
from jax.sharding import PartitionSpec as P

HIGHEST = lax.Precision.HIGHEST
F32 = jnp.float32
BF16 = jnp.bfloat16
NB = 128
ROWS = ((0,), (0,))
COLS = ((1,), (1,))
VMEM = pl.BlockSpec(memory_space=pltpu.VMEM)
SMEM = pl.BlockSpec(memory_space=pltpu.SMEM)
ANY = pl.BlockSpec(memory_space=pl.ANY)
HBM = pl.BlockSpec(memory_space=pltpu.HBM)


def limit(mib):
    return pltpu.CompilerParams(vmem_limit_bytes=mib * 1024 * 1024)


def cost(flops, nbytes):
    return pl.CostEstimate(flops=int(flops), bytes_accessed=int(nbytes), transcendentals=0)


def whole(*shape):
    return pl.BlockSpec(shape, lambda *_: (0,) * len(shape))


def dot(a, b, contract, precision=None):
    return lax.dot_general(a, b, (contract, ((), ())), precision=precision, preferred_element_type=F32)


def eye(n):
    return lax.broadcasted_iota(jnp.int32, (n, n), 0) == lax.broadcasted_iota(jnp.int32, (n, n), 1)


def totals_body(counts, out, small):
    tile, width = counts.shape
    for at in range(tile // NB):
        parts = []
        for r in range(at * NB, (at + 1) * NB, 32):
            acc = None
            for c in range(0, width, NB):
                value = counts[r : r + 32, c : c + NB]
                small[r : r + 32, c : c + NB] = (value - 128).astype(jnp.int8)
                acc = value if acc is None else acc + value
            parts.append(jnp.sum(acc.astype(F32), axis=1, keepdims=True))
        column = jnp.concatenate(parts, 0)
        out[at] = jnp.sum(jnp.where(eye(NB), column, 0.0), axis=0, keepdims=True)


def row_sums(counts):
    rows, width = counts.shape
    tile = 2 * NB
    return pl.pallas_call(
        totals_body,
        grid=(rows // tile,),
        in_specs=[pl.BlockSpec((tile, width), lambda g: (g, 0))],
        out_specs=[
            pl.BlockSpec((tile // NB, 1, NB), lambda g: (g, 0, 0)),
            pl.BlockSpec((tile, width), lambda g: (g, 0)),
        ],
        out_shape=[
            jax.ShapeDtypeStruct((rows // NB, 1, NB), F32),
            jax.ShapeDtypeStruct((rows, width), jnp.int8),
        ],
        name="row_sums",
        cost_estimate=cost(2000 * rows * width, 1),
        compiler_params=limit(50),
    )(counts)


def weigh_body(order, small, base, log_ctx, omega, *refs):
    w, send, keep = refs[-3:]
    tile, width = w.shape
    step = min(2048, width)
    column = jnp.concatenate(
        [jnp.sum(jnp.where(eye(NB), base[i], 0.0), axis=1, keepdims=True) for i in range(tile // NB)]
    )
    acc = jnp.zeros((tile, omega.shape[1]), F32)
    for c in range(0, width, step):
        here = slice(c, c + step)
        for r in range(0, tile, 32):
            rows = slice(r, r + 32)
            count = small[rows, here].astype(F32) + 128.0
            value = jnp.log(count) + (column[rows] - log_ctx[:, here])
            w[rows, here] = jnp.maximum(value, 0.0).astype(BF16)
        acc = acc + jnp.dot(w[:, here], omega[here, :], preferred_element_type=F32)

    @pl.when(pl.program_id(0) < 2)
    def _():
        send[0] = acc.astype(BF16)

    @pl.when(pl.program_id(0) >= 2)
    def _():
        keep[0] = acc


def weigh(small, base, log_ctx, omega, w, order, offset, tile, tokens):
    n = order.shape[0]
    rows, width = small.shape
    size = omega.shape[1]
    share = rows // n
    place = lambda g, o: (o[g] * (share // tile) + offset // tile, 0)
    held = ([] if w is None else [w]) + tokens
    return pl.pallas_call(
        weigh_body,
        grid_spec=pltpu.PrefetchScalarGridSpec(
            num_scalar_prefetch=1,
            grid=(n,),
            in_specs=[
                pl.BlockSpec((tile, width), place),
                pl.BlockSpec((tile // NB, 1, NB), lambda g, o: place(g, o) + (0,)),
                pl.BlockSpec((1, width), lambda g, o: (0, 0)),
                VMEM,
            ]
            + [ANY] * len(held),
            out_specs=[
                pl.BlockSpec((tile, width), place),
                pl.BlockSpec((1, tile, size), lambda g, o: (jnp.minimum(g, 1), 0, 0)),
                pl.BlockSpec((1, tile, size), lambda g, o: (jnp.maximum(g - 2, 0), 0, 0)),
            ],
        ),
        out_shape=[
            jax.ShapeDtypeStruct((rows, width), BF16),
            jax.ShapeDtypeStruct((2, tile, size), BF16),
            jax.ShapeDtypeStruct((2, tile, size), F32),
        ],
        input_output_aliases={} if w is None else {5: 0},
        name="weigh_and_sketch",
        cost_estimate=cost(40 * n * tile * width * size, 6 * n * tile * width),
        compiler_params=limit(44),
    )(order, small, base, log_ctx, omega, *held)


PACKED = (((0, 0), (0, 1), (0, 2), (0, 3), (3, 3)), ((1, 1), (1, 2), (1, 3), (2, 2), (2, 3)))


def gram_body(parts_of, core, *refs):
    n = sum(len(parts) for parts in parts_of)
    terms, (sketch, sketch_b, own, send) = refs[:n], refs[n : n + 4]
    held, arrival = refs[n + 4 : -1], refs[-1]
    which = [at for parts in parts_of for at in parts]
    copies = [
        pltpu.make_async_copy(terms[i] if at is None else terms[i].at[at], held[i], arrival.at[i])
        for i, at in enumerate(which)
    ]
    for copy in copies:
        copy.start()
    at, i = 0, 0
    for parts in parts_of:
        total = None
        for _ in parts:
            copies[i].wait()
            value = held[i][...].astype(F32)
            total = value if total is None else total + value
            i += 1
        sketch[at : at + total.shape[0], :] = total
        at += total.shape[0]
    sketch_b[...] = sketch[...].astype(BF16)
    size = sketch.shape[1] // 4
    col = lambda i, j: sketch[:, i * size : j * size]
    upper = lambda i, j: dot(col(i, i + 1), col(i, j), ROWS, HIGHEST)
    halves = [
        jnp.concatenate([upper(0, 4), upper(3, 4)], axis=1),
        jnp.concatenate([upper(1, 4), upper(2, 4)], axis=1),
    ]
    for which in range(2):

        @pl.when(core[0] == which)
        def _(which=which):
            own[...] = halves[which]
            send[...] = halves[1 - which]


def gram_of(core, pieces):
    terms = [array for piece in pieces for array, _ in piece]
    parts_of = [[which for _, which in piece] for piece in pieces]
    size = terms[0].shape[-1]
    rows = sum(piece[0][0].shape[-2] for piece in pieces)
    return pl.pallas_call(
        functools.partial(gram_body, parts_of),
        grid=(1,),
        in_specs=[SMEM] + [HBM] * len(terms),
        out_specs=[whole(rows, size)] * 2 + [whole(size // 4, size // 4 * 5)] * 2,
        out_shape=[
            jax.ShapeDtypeStruct((rows, size), F32),
            jax.ShapeDtypeStruct((rows, size), BF16),
            jax.ShapeDtypeStruct((size // 4, size // 4 * 5), F32),
            jax.ShapeDtypeStruct((size // 4, size // 4 * 5), F32),
        ],
        scratch_shapes=[pltpu.VMEM(x.shape[-2:], x.dtype) for x in terms]
        + [pltpu.SemaphoreType.DMA((len(terms),))],
        name="gram",
        cost_estimate=cost(12 * rows * size * size, 8 * rows * size),
        compiler_params=limit(60),
    )(core, *terms)


def small_inverse(g):
    n = len(g)
    g = [list(r) for r in g]
    m = [[None] * n for _ in range(n)]
    out = [[None] * n for _ in range(n)]
    for j in range(0, n, 2):
        k = j + 1
        a, b, c = g[j][j], g[k][j], g[k][k]
        over = 1.0 / (a * c - b * b)
        ca, cb, cc = a * over, b * over, c * over
        ra, rb = lax.rsqrt(a), lax.rsqrt(ca)
        for l in range(j):
            out[j][l] = m[j][l] * ra
            out[k][l] = (ca * m[k][l] - cb * m[j][l]) * rb
        out[j][j], out[k][j], out[k][k] = ra, -cb * rb, ca * rb
        for i in range(k + 1, n):
            f = cc * g[i][j] - cb * g[i][k]
            h = ca * g[i][k] - cb * g[i][j]
            for l in range(k + 1, i + 1):
                g[i][l] = g[i][l] - (f * g[l][j] + h * g[l][k])
            for l in range(j):
                m[i][l] = m[i][l] - (f * m[j][l] + h * m[k][l])
            m[i][j], m[i][k] = -f, -h
    return out


def total(terms):
    while len(terms) > 1:
        terms = [x + y for x, y in zip(terms[::2], terms[1::2])] + terms[len(terms) // 2 * 2 :]
    return terms[0]


def eliminate(tiles, done):
    shape, n, group = tiles[0].shape, len(tiles), 2
    lane = lax.broadcasted_iota(jnp.int32, shape, 1)
    sub = lax.broadcasted_iota(jnp.int32, shape, 0)
    spread = lambda x: jnp.broadcast_to(x, shape)
    columns = lambda x: tuple(spread(x[:, m : m + 1]) for m in range(8))
    pivots = lane < 8

    def turn(t, carry):
        here, tiles = carry
        g = [[spread(here[l][i : i + 1]) for l in range(i + 1)] for i in range(8)]
        rows = [
            jnp.where(pivots, jnp.where(lane == k, 1.0, 0.0), spread(tiles[0][k : k + 1])) for k in range(8)
        ]
        low = small_inverse(g)
        y = [total([low[r][k] * rows[k] for k in range(r + 1)]) for r in range(8)]
        z = [total([low[r][m] * y[r] for r in range(m, 8)]) for m in range(8)]
        new = []
        for x in tiles[1:]:
            x = jnp.where(pivots, 0.0, x) - total([c * w for c, w in zip(columns(x), z)])
            new.append(pltpu.roll(x, NB - 8, 1))
            if len(new) == 1:
                here = columns(new[0])
        final = y[0]
        for r in range(1, 8):
            final = jnp.where(sub == r, y[r], final)
        done[pl.ds(pl.multiple_of(8 * t, 8), 8), :] = final
        return here, tuple(new) + (jnp.zeros(shape, F32),)

    carry = columns(tiles[0]), tuple(tiles)
    for start in range(0, n, group):
        here, tiles = lax.fori_loop(start, start + group, turn, carry)
        carry = here, tiles[: n - start - group]
    return [done[0:8, :]] + [pltpu.roll(done[8 * t : 8 * t + 8, :], 8 * t, 1) for t in range(1, n)]


def factor_body(core, mine, other, out, halves, t, done):
    size = t.shape[0]
    n = size // NB
    block = lambda i: slice(i * NB, (i + 1) * NB)
    halves[core[0]] = mine[...]
    halves[1 - core[0]] = other[...]
    trace = jnp.float32(0.0)
    for half in range(2):
        for at, (i, j) in enumerate(PACKED[half]):
            value = halves[half, :, block(at)]
            t[block(i), block(j)] = value
            if i == j:
                trace = trace + jnp.sum(jnp.where(eye(NB), value, 0.0))
    amount = jnp.float32(0.0001) * trace / jnp.float32(size)
    lower = lax.broadcasted_iota(jnp.int32, (NB, NB), 1) <= lax.broadcasted_iota(jnp.int32, (NB, NB), 0)
    for p in range(n):
        here, before = block(p), slice(0, p * NB)
        diagonal = t[here, here] + jnp.where(eye(NB), amount, 0.0)
        tiles = eliminate([diagonal[8 * i : 8 * i + 8] for i in range(NB // 8)], done)
        inverse = jnp.where(lower, jnp.concatenate(tiles, 0), 0.0)
        out[here, here] = inverse
        if p:
            left = dot(inverse, t[here, before], ((1,), (0,)), HIGHEST)
            out[here, before] = left
        if p < n - 1:
            rest = slice((p + 1) * NB, size)
            out[here, rest] = jnp.zeros((NB, size - (p + 1) * NB), F32)
            right = dot(inverse, t[here, rest], ((1,), (0,)), HIGHEST)
            for q in range(p + 1, n):
                off = (q - p - 1) * NB
                use = right[:, off : off + NB]
                t[block(q), q * NB :] = t[block(q), q * NB :] - dot(use, right[:, off:], ROWS, HIGHEST)
                t[block(q), here] = -dot(use, inverse, ROWS, HIGHEST)
                if p:
                    t[block(q), before] = t[block(q), before] - dot(use, left, ROWS, HIGHEST)


def factor_inverse(core, mine, other):
    size = mine.shape[0] * 4
    return pl.pallas_call(
        factor_body,
        grid=(1,),
        in_specs=[SMEM, whole(*mine.shape), whole(*mine.shape)],
        out_specs=whole(size, size),
        out_shape=jax.ShapeDtypeStruct((size, size), F32),
        scratch_shapes=[
            pltpu.VMEM((2,) + mine.shape, F32),
            pltpu.VMEM((size, size), F32),
            pltpu.VMEM((NB, NB), F32),
        ],
        name="factor_inverse",
        cost_estimate=cost(1, 1),
        compiler_params=limit(24),
    )(core, mine, other)


def basis_body(inverse, sketch, *refs):
    refs[-1][...] = dot(sketch[...], inverse[...], COLS, HIGHEST)


def basis_of(inverse, sketch, tokens):
    rows, size = sketch.shape
    return pl.pallas_call(
        basis_body,
        grid=(1,),
        in_specs=[whole(size, size), whole(rows, size)] + [ANY] * len(tokens),
        out_specs=whole(rows, size),
        out_shape=jax.ShapeDtypeStruct((rows, size), F32),
        name="basis",
        cost_estimate=cost(1, 1),
        compiler_params=limit(24),
    )(inverse, sketch, *tokens)


def turned_body(place, inverse, *refs):
    shares, turned = refs[:-1], refs[-1]
    rows, size = shares[0].shape
    quarter = size // 4
    for i in range(4):
        take = inverse[pl.ds(pl.multiple_of(place[i] * quarter, quarter), quarter), :]
        high = take.astype(BF16)
        low = (take - high.astype(F32)).astype(BF16)
        for d, share in enumerate(shares):
            value = dot(high, share[...], COLS) + dot(low, share[...], COLS)
            start = pl.multiple_of(place[4 + d] * rows, rows)
            turned[i * quarter : (i + 1) * quarter, pl.ds(start, rows)] = value.astype(BF16)


def turned_basis(place, inverse, shares):
    rows, size = shares[0].shape
    n = len(shares)
    return pl.pallas_call(
        turned_body,
        grid=(1,),
        in_specs=[SMEM, whole(size, size)] + [whole(rows, size)] * n,
        out_specs=whole(size, n * rows),
        out_shape=jax.ShapeDtypeStruct((size, n * rows), BF16),
        name="turned_basis",
        cost_estimate=cost(4 * n * rows * size * size, 4 * n * rows * size),
        compiler_params=limit(24),
    )(place, inverse, *shares)


def project_body(turned, w, *refs):
    send, own = refs[-2:]
    half = send.shape[0]
    value = jnp.dot(turned[...], w[...], preferred_element_type=F32)
    send[...] = value[:half].astype(BF16)
    own[...] = value[half:]


def project(turned, w, tokens, start, width, tile):
    size, rows = turned.shape
    steps = width // tile
    first = start // tile
    out = lambda g: (0, g)
    return pl.pallas_call(
        project_body,
        grid=(steps,),
        in_specs=[
            pl.BlockSpec((size, rows), lambda g: (0, 0), pipeline_mode=pl.Buffered(1)),
            pl.BlockSpec((rows, tile), lambda g: (0, first + g)),
        ]
        + [ANY] * len(tokens),
        out_specs=[pl.BlockSpec((size // 2, tile), out), pl.BlockSpec((size // 2, tile), out)],
        out_shape=[
            jax.ShapeDtypeStruct((size // 2, width), BF16),
            jax.ShapeDtypeStruct((size // 2, width), F32),
        ],
        name="project",
        cost_estimate=cost(40 * rows * size * width, 2 * rows * width),
        compiler_params=limit(40),
    )(turned, w, *tokens)


def finish_body(scale, start, mine, core_term, chip_term, *refs):
    out, turned, arrival = refs[-3:]
    total = mine[...] + core_term[...].astype(F32) + chip_term[...].astype(F32)
    turned[...] = jnp.transpose(total * scale)
    copy = pltpu.make_async_copy(turned, out.at[pl.ds(start, turned.shape[0])], arrival)
    copy.start()
    copy.wait()


def finish(own, core_term, chip_term, out, start, full, scale):
    size, width = chip_term.shape
    held = [] if out is None else [out]
    return pl.pallas_call(
        functools.partial(finish_body, scale, start),
        grid=(1,),
        in_specs=[
            pl.BlockSpec((size, width), lambda g: (1, 0)),
            pl.BlockSpec((size, width), lambda g: (1, 0)),
            whole(size, width),
        ]
        + [ANY] * len(held),
        out_specs=ANY,
        out_shape=jax.ShapeDtypeStruct((full, size), F32),
        input_output_aliases={3: 0} if held else {},
        scratch_shapes=[pltpu.VMEM((width, size), F32), pltpu.SemaphoreType.DMA],
        name="finish",
        cost_estimate=cost(1, 1),
        compiler_params=limit(24),
    )(own, core_term, chip_term, *held)


def pass_body(mine, core_term, *refs):
    refs[-1][...] = (mine[...] + core_term[...].astype(F32)).astype(BF16)


def pass_on(own, core_term, tokens):
    size, width = own.shape[0] // 2, own.shape[1]
    return pl.pallas_call(
        pass_body,
        grid=(1,),
        in_specs=[whole(size, width), whole(size, width)] + [ANY] * len(tokens),
        out_specs=whole(size, width),
        out_shape=jax.ShapeDtypeStruct((size, width), BF16),
        name="pass_on",
        cost_estimate=cost(1, 1),
        compiler_params=limit(24),
    )(own, core_term, *tokens)


def rotate(x, n, by):
    return lax.ppermute(x, "col", [(i, (i + by) % n) for i in range(n)])


def swap_col(x, bit):
    return lax.ppermute(x, "col", [(i, i ^ bit) for i in range(4)])


def swap(x, bit):
    return lax.ppermute(x, "row", [(i, i ^ bit) for i in range(4)])


def half_of(x, which):
    rows = x.shape[0] // 2
    return lax.dynamic_slice_in_dim(x, which * rows, rows, 0)


def stack_by(which, mine, other):
    return jnp.where(which == 0, jnp.concatenate([mine, other]), jnp.concatenate([other, mine]))


def pieces_of(share):
    n = share // NB
    return [2 * NB] * ((n - 2) // 2) + [NB] * (n - (n - 2) // 2 * 2) if n > 2 else [NB] * n


def sketch_phase(counts, log_ctx, ctx_sum, omega, col):
    rows, width = counts.shape
    part, small = row_sums(counts)
    part = jnp.concatenate([part.reshape(rows // NB, NB), jnp.broadcast_to(ctx_sum, (8, NB))])
    part = part + swap_col(part, 1)
    part = part + swap_col(part, 2)
    logs = jnp.log(part)
    base = logs[-1, 0] - jnp.log(F32(5.0)) - logs[:-8]
    base = base.reshape(rows // NB, 1, NB)
    order = jnp.stack([col ^ 1, col ^ 3, col ^ 2, col])
    w, offset, pieces, passed, arrived = None, 0, [], [], []
    for k, tile in enumerate(pieces_of(rows // 4)):
        tokens = passed[k - 2 : k - 1] if k >= 2 else []
        tokens = tokens + (arrived[k - 3 : k - 2] if k >= 3 else [])
        w, send, keep = weigh(small, base, log_ctx, omega, w, order, offset, tile, tokens)
        offset += tile
        near = swap_col(send, 1)
        passed.append((keep[0] + near[1].astype(F32)).astype(BF16))
        arrived.append(swap_col(passed[k], 2))
        pieces.append([(keep, 1), (near, 0), (arrived[k], None)])
    return w, pieces


def sketch_phase_any(counts, log_ctx, ctx_sum, omega, col):
    row_part = jnp.sum(counts.astype(F32), axis=1)
    row_total, ctx_total = lax.psum((row_part, ctx_sum), "col")
    value = jnp.log(counts.astype(F32)) + (
        jnp.log(ctx_total) - jnp.log(F32(5.0)) - jnp.log(row_total)[:, None] - log_ctx
    )
    w = jnp.maximum(value, 0.0).astype(BF16)
    partial = jnp.dot(w, omega, preferred_element_type=F32)
    return w, [[(lax.psum_scatter(partial, "col", scatter_dimension=0, tiled=True), None)]]


def shards(counts, ctx_counts, omega):
    rows, width = counts.shape
    n = lax.axis_size("col")
    row = lax.axis_index("row")
    col = lax.axis_index("col")
    core, chip = row % 2, row // 2
    ctx_weight = ctx_counts.astype(F32) ** 0.75
    ctx_sum = jnp.sum(ctx_weight)
    log_ctx = jnp.log(ctx_weight)[None, :]
    direct = n == 4 and rows % (4 * NB) == 0
    phase = sketch_phase if direct else sketch_phase_any
    w, pieces = phase(counts, log_ctx, ctx_sum, omega, col)
    sketch, sketch_b, half, other_half = gram_of(core.reshape(1), pieces)
    half = half + swap(other_half, 1)
    quarter = half_of(half, chip) + swap(half_of(half, 1 - chip), 2)
    if direct:
        quarter = quarter + swap_col(quarter, 1)
        quarter = quarter + swap_col(quarter, 2)
        shares = [sketch_b] + [rotate(sketch_b, n, d) for d in range(1, n)]
        sources = [(col - d) % n for d in range(n)]
    else:
        quarter = lax.psum(quarter, "col")
        shares = [lax.all_gather(sketch_b, "col", tiled=True)]
        sources = [jnp.int32(0)]
    half = stack_by(chip, quarter, swap(quarter, 2))
    inverse = factor_inverse(core.reshape(1), half, swap(half, 1))
    place = jnp.stack([row ^ 3, row ^ 1, row ^ 2, row] + sources)
    turned = turned_basis(place, inverse, shares)
    widths = (1, 2, 3, 3, 4, 2, 1) if width % (16 * NB) == 0 else (1,) * 8
    unit = width // sum(widths)
    scale = float(1.0 / (rows * lax.axis_size("row")) ** 0.5)
    quarter = omega.shape[1] // 4
    out, start = None, 0
    sent, passed, arrived = [], [], []
    for j, pieces in enumerate(widths):
        piece = pieces * unit
        tokens = sent[-1:] + (passed[-2:-1] if j >= 2 else []) + (arrived[-3:-2] if j >= 3 else [])
        send, mine = project(turned, w, tokens, start, piece, unit)
        core_term = swap(send, 1)
        if j == len(widths) - 1:
            basis = basis_of(inverse, sketch, [send])
            chip_send = pass_on(mine, core_term, [arrived[-2], basis])
        else:
            chip_send = (mine[:quarter] + core_term[:quarter].astype(F32)).astype(BF16)
        chip_term = swap(chip_send, 2)
        sent.append(send)
        passed.append(chip_send)
        arrived.append(chip_term)
        out = finish(mine, core_term, chip_term, out, start, width, scale)
        start += piece
    return (basis, out)


def solution(mesh):
    in_specs = (P(("grp", "row"), "col"), P(("grp", "col")), P("col", None))
    out_specs = (P(("grp", "row", "col"), None), P(("grp", "col"), "row"))
    return jax.shard_map(shards, mesh=mesh, in_specs=in_specs, out_specs=out_specs, check_vma=False)
```

profile of v0, /device:TPU:8, one launch (start us, length us, event | category | flops | bytes accessed | tf_op | source)
XLA Modules:
  0.0 256.0 jit_solution(2132384171869346176)
XLA Ops:
  0.6 27.6 %row_sums.1 = (f32[16,1,128]{2,1,0:T(1,128)S(1)}, s8[2048,8192]{1,0:T(32,128)(4,1)}) custom-call(s32[2048,8192]{1,0:T(8,128)} %counts.1), custom_call_target="tpu_custom_call" | custom-call | flops 33554432000 | bytes 1 | tf_op jit(solution)/shard_map/row_sums/pallas_call | solution.py:60
  29.6 3.7 %collective-permute-done = f32[24,128]{1,0:T(8,128)S(1)} collective-permute-done((f32[24,128]{1,0:T(8,128)S(1)}, f32[24,128]{1,0:T(8,128)S(1)}, u32[]{:S(2)}, u32[]{:S(2)}) %collective-permute-start) | collective-permute-done | bytes 12320 | tf_op jit(solution)/shard_map/ppermute | solution.py:462
  33.9 2.7 %collective-permute-start.1 = (f32[24,128]{1,0:T(8,128)S(1)}, f32[24,128]{1,0:T(8,128)S(1)}, u32[]{:S(2)}, u32[]{:S(2)}) collective-permute-start(f32[24,128]{1,0:T(8,128)S(1)} %pad_add_fusion), channel_id=1, source_target_pairs={{0,2},{1,3},{2,0},{3,1},{4,6},{5,7},{6,4},{7,5},{8,10},{9,11},{10,... | collective-permute-start | bytes 36872 | tf_op jit(solution)/shard_map/ppermute | solution.py:462
  39.8 3.4 %copy-done.21 = bf16[8192,512]{1,0:T(8,128)(2,1)S(1)} copy-done((bf16[8192,512]{1,0:T(8,128)(2,1)S(1)}, bf16[8192,512]{1,0:T(8,128)(2,1)}, u32[]{:S(2)}) %copy-start.21) | copy-done | bytes 8388632
  43.2 16.0 %weigh_and_sketch.3 = (bf16[2048,8192]{1,0:T(8,128)(2,1)}, bf16[2,256,512]{2,1,0:T(8,128)(2,1)S(1)}, f32[2,256,512]{2,1,0:T(8,128)S(1)}) custom-call(s32[4]{0:T(128)S(1)} %pad_add_fusion.1.order, s8[2048,8192]{1,0:T(32,128)(4,1)} %get-tuple-element.31.small, f32[16,1,128]{2,1,0:T(1,128)S(1)} %bitcast.28, f32[1,8192]{1,0:T(1,128)S(1)} %bitcast.23, ...), custom_call_target="tpu_custom_call" | custom-call | flops 171798691840 | bytes 50331648 | tf_op jit(solution)/shard_map/weigh_and_sketch/pallas_call | solution.py:111
  59.2 9.7 %weigh_and_sketch.4 = (bf16[2048,8192]{1,0:T(8,128)(2,1)}, bf16[2,128,512]{2,1,0:T(8,128)(2,1)S(1)}, f32[2,128,512]{2,1,0:T(8,128)S(1)}) custom-call(s32[4]{0:T(128)S(1)} %pad_add_fusion.1.order, s8[2048,8192]{1,0:T(32,128)(4,1)} %get-tuple-element.31.small, f32[16,1,128]{2,1,0:T(1,128)S(1)} %bitcast.29, ...), custom_call_target="tpu_custom_call", output_to_operand_aliasing={{0}: (5, {})} | custom-call | flops 85899345920 | bytes 25165824 | tf_op jit(solution)/shard_map/weigh_and_sketch/pallas_call | solution.py:111
  72.0 9.7 %weigh_and_sketch.5 = (bf16[2048,8192]{1,0:T(8,128)(2,1)}, bf16[2,128,512]{2,1,0:T(8,128)(2,1)S(1)}, f32[2,128,512]{2,1,0:T(8,128)S(1)}) custom-call(s32[4]{0:T(128)S(1)} %pad_add_fusion.1.order, s8[2048,8192]{1,0:T(32,128)(4,1)} %get-tuple-element.31.small, f32[16,1,128]{2,1,0:T(1,128)S(1)} %bitcast.30, ...), custom_call_target="tpu_custom_call", output_to_operand_aliasing={{0}: (5, {})} | custom-call | flops 85899345920 | bytes 25165824 | tf_op jit(solution)/shard_map/weigh_and_sketch/pallas_call | solution.py:111
  81.8 2.6 %collective-permute-start.5 = (bf16[128,512]{1,0:T(8,128)(2,1)S(1)}, bf16[128,512]{1,0:T(8,128)(2,1)S(1)}, u32[]{:S(2)}, u32[]{:S(2)}) collective-permute-start(bf16[128,512]{1,0:T(8,128)(2,1)S(1)} %fusion.1), channel_id=1, source_target_pairs={{0,2},{1,3},{2,0},{3,1},{4,6},{5,7},{6,4},{7,5},{8,10},{9,11},{10,... | collective-permute-start | bytes 393224 | tf_op jit(solution)/shard_map/ppermute | solution.py:462
  84.8 6.2 %collective-permute-done.6.refs_7_ = bf16[2,128,512]{2,1,0:T(8,128)(2,1)S(1)} collective-permute-done((bf16[2,128,512]{2,1,0:T(8,128)(2,1)S(1)}, bf16[2,128,512]{2,1,0:T(8,128)(2,1)S(1)}, u32[]{:S(2)}, u32[]{:S(2)}) %collective-permute-start.6) | collective-permute-done | bytes 262176 | tf_op jit(solution)/shard_map/ppermute | solution.py:462
  91.0 2.5 collective-permute-start.7
  93.5 3.1 %collective-permute-done.5.refs_5_ = bf16[128,512]{1,0:T(8,128)(2,1)S(1)} collective-permute-done((bf16[128,512]{1,0:T(8,128)(2,1)S(1)}, bf16[128,512]{1,0:T(8,128)(2,1)S(1)}, u32[]{:S(2)}, u32[]{:S(2)}) %collective-permute-start.5) | collective-permute-done | bytes 131104 | tf_op jit(solution)/shard_map/ppermute | solution.py:462
  96.6 5.1 %collective-permute-done.3.refs_2_ = bf16[256,512]{1,0:T(8,128)(2,1)S(1)} collective-permute-done((bf16[256,512]{1,0:T(8,128)(2,1)S(1)}, bf16[256,512]{1,0:T(8,128)(2,1)S(1)}, u32[]{:S(2)}, u32[]{:S(2)}) %collective-permute-start.3) | collective-permute-done | bytes 262176 | tf_op jit(solution)/shard_map/ppermute | solution.py:462
  103.7 4.5 %gram.1 = (f32[512,512]{1,0:T(8,128)}, bf16[512,512]{1,0:T(8,128)(2,1)}, f32[128,640]{1,0:T(8,128)}, f32[128,640]{1,0:T(8,128)}) custom-call(s32[1]{0:T(128)} %bitcast.core, f32[2,256,512]{2,1,0:T(8,128)} %copy-done.16, bf16[2,256,512]{2,1,0:T(8,128)(2,1)} %copy-done.23, bf16[256,512]{1,0:T(8,128)(2,1)} %copy-done.27, f32[2,128,512]{2,1,0:T(8,128)} %copy-done.19, ...), custom_call_target="tpu_custom_call" | custom-call | flops 1610612736 | bytes 2097152 | tf_op jit(solution)/shard_map/gram/pallas_call | solution.py:186
  112.8 4.7 %collective-permute-done.9 = f32[64,640]{1,0:T(8,128)S(1)} collective-permute-done((f32[64,640]{1,0:T(8,128)S(1)}, f32[64,640]{1,0:T(8,128)S(1)}, u32[]{:S(2)}, u32[]{:S(2)}) %collective-permute-start.9) | collective-permute-done | bytes 163872 | tf_op jit(solution)/shard_map/ppermute | solution.py:466
  117.5 3.3 %collective-permute-start.10 = (f32[64,640]{1,0:T(8,128)S(1)}, f32[64,640]{1,0:T(8,128)S(1)}, u32[]{:S(2)}, u32[]{:S(2)}) collective-permute-start(f32[64,640]{1,0:T(8,128)S(1)} %dynamic-slice_add_fusion), channel_id=1, source_target_pairs={{0,1},{1,0},{2,3},{3,2},{4,5},{5,4},{6,7},{7,6},{8,9},{9,8},{10,11... | collective-permute-start | bytes 491528 | tf_op jit(solution)/shard_map/ppermute | solution.py:462
  120.9 3.7 %collective-permute-done.10 = f32[64,640]{1,0:T(8,128)S(1)} collective-permute-done((f32[64,640]{1,0:T(8,128)S(1)}, f32[64,640]{1,0:T(8,128)S(1)}, u32[]{:S(2)}, u32[]{:S(2)}) %collective-permute-start.10) | collective-permute-done | bytes 163872 | tf_op jit(solution)/shard_map/ppermute | solution.py:462
  126.5 5.5 %collective-permute-done.11 = f32[64,640]{1,0:T(8,128)S(1)} collective-permute-done((f32[64,640]{1,0:T(8,128)S(1)}, f32[64,640]{1,0:T(8,128)S(1)}, u32[]{:S(2)}, u32[]{:S(2)}) %collective-permute-start.11) | collective-permute-done | bytes 163872 | tf_op jit(solution)/shard_map/ppermute | solution.py:462
  135.0 4.3 %collective-permute-start.15 = (bf16[512,512]{1,0:T(8,128)(2,1)}, bf16[512,512]{1,0:T(8,128)(2,1)S(1)}, u32[]{:S(2)}, u32[]{:S(2)}) collective-permute-start(bf16[512,512]{1,0:T(8,128)(2,1)} %get-tuple-element.44.refs_0_), channel_id=1, source_target_pairs={{0,2},{1,3},{2,0},{3,1},{4,6},{5,7},{6,4},{7,5},{8,10},{9,11},{10,... | collective-permute-start | bytes 1572872 | tf_op jit(solution)/shard_map/ppermute | solution.py:458
  141.0 27.4 %factor_inverse.1.inverse = f32[512,512]{1,0:T(8,128)S(1)} custom-call(s32[1]{0:T(128)} %bitcast.core, f32[128,640]{1,0:T(8,128)S(1)} %maximum_select_fusion.mine, f32[128,640]{1,0:T(8,128)S(1)} %collective-permute-done.13.other), custom_call_target="tpu_custom_call" | custom-call | flops 1 | bytes 1 | tf_op jit(solution)/shard_map/factor_inverse/pallas_call | solution.py:312
  168.4 11.1 %collective-permute-done.15.refs_2_ = bf16[512,512]{1,0:T(8,128)(2,1)S(1)} collective-permute-done((bf16[512,512]{1,0:T(8,128)(2,1)}, bf16[512,512]{1,0:T(8,128)(2,1)S(1)}, u32[]{:S(2)}, u32[]{:S(2)}) %collective-permute-start.15) | collective-permute-done | bytes 524320 | tf_op jit(solution)/shard_map/ppermute | solution.py:458
  179.6 3.8 %collective-permute-done.16.refs_3_ = bf16[512,512]{1,0:T(8,128)(2,1)S(1)} collective-permute-done((bf16[512,512]{1,0:T(8,128)(2,1)}, bf16[512,512]{1,0:T(8,128)(2,1)S(1)}, u32[]{:S(2)}, u32[]{:S(2)}) %collective-permute-start.16) | collective-permute-done | bytes 524320 | tf_op jit(solution)/shard_map/ppermute | solution.py:458
  183.3 6.1 %turned_basis.1.turned = bf16[512,2048]{1,0:T(8,128)(2,1)S(1)} custom-call(s32[8]{0:T(128)S(1)} %stack.55.place, f32[512,512]{1,0:T(8,128)S(1)} %factor_inverse.1.inverse, bf16[512,512]{1,0:T(8,128)(2,1)S(1)} %copy-done.22, bf16[512,512]{1,0:T(8,128)(2,1)S(1)} %collective-permute-done.14.refs_1_, bf16[512,512]{1,0:T(8,128)(2,1)S(1)} %collective-permute-done.15.refs_2_, ...), custom_call_target="tpu_custom_call" | custom-call | flops 2147483648 | bytes 4194304 | tf_op jit(solution)/shard_map/turned_basis/pallas_call | solution.py:364
  190.4 2.8 %project.7 = (bf16[256,512]{1,0:T(8,128)(2,1)S(1)}, f32[256,512]{1,0:T(8,128)S(1)}) custom-call(bf16[512,2048]{1,0:T(8,128)(2,1)S(1)} %turned_basis.1.turned, bf16[2048,8192]{1,0:T(8,128)(2,1)} %get-tuple-element.45.w), custom_call_target="tpu_custom_call" | custom-call | flops 21474836480 | bytes 2097152 | tf_op jit(solution)/shard_map/project/pallas_call | solution.py:389
  193.3 4.3 %project.8 = (bf16[256,1024]{1,0:T(8,128)(2,1)S(1)}, f32[256,1024]{1,0:T(8,128)S(1)}) custom-call(bf16[512,2048]{1,0:T(8,128)(2,1)S(1)} %turned_basis.1.turned, bf16[2048,8192]{1,0:T(8,128)(2,1)} %get-tuple-element.45.w, bf16[256,512]{1,0:T(8,128)(2,1)S(1)} %get-tuple-element.46.refs_0_), custom_call_target="tpu_custom_call" | custom-call | flops 42949672960 | bytes 4194304 | tf_op jit(solution)/shard_map/project/pallas_call | solution.py:389
  198.7 5.8 %project.9 = (bf16[256,1536]{1,0:T(8,128)(2,1)S(1)}, f32[256,1536]{1,0:T(8,128)S(1)}) custom-call(bf16[512,2048]{1,0:T(8,128)(2,1)S(1)} %turned_basis.1.turned, bf16[2048,8192]{1,0:T(8,128)(2,1)} %get-tuple-element.45.w, bf16[256,1024]{1,0:T(8,128)(2,1)S(1)} %get-tuple-element.47.refs_0_, bf16[128,512]{1,0:T(8,128)(2,1)S(1)} %add_convert_fusion.6.refs_1_), custom_call_target="tpu_custom_call" | custom-call | flops 64424509440 | bytes 6291456 | tf_op jit(solution)/shard_map/project/pallas_call | solution.py:389
  207.2 5.8 %project.10 = (bf16[256,1536]{1,0:T(8,128)(2,1)S(1)}, f32[256,1536]{1,0:T(8,128)S(1)}) custom-call(bf16[512,2048]{1,0:T(8,128)(2,1)S(1)} %turned_basis.1.turned, bf16[2048,8192]{1,0:T(8,128)(2,1)} %get-tuple-element.45.w, bf16[256,1536]{1,0:T(8,128)(2,1)S(1)} %get-tuple-element.49.refs_0_, bf16[128,1024]{1,0:T(8,128)(2,1)S(1)} %add_convert_fusion.4.refs_1_, ...), custom_call_target="tpu_custom_call" | custom-call | flops 64424509440 | bytes 6291456 | tf_op jit(solution)/shard_map/project/pallas_call | solution.py:389
  214.2 7.2 %project.11 = (bf16[256,2048]{1,0:T(8,128)(2,1)S(1)}, f32[256,2048]{1,0:T(8,128)S(1)}) custom-call(bf16[512,2048]{1,0:T(8,128)(2,1)S(1)} %turned_basis.1.turned, bf16[2048,8192]{1,0:T(8,128)(2,1)} %get-tuple-element.45.w, bf16[256,1536]{1,0:T(8,128)(2,1)S(1)} %get-tuple-element.51.refs_0_, bf16[128,1536]{1,0:T(8,128)(2,1)S(1)} %add_convert_fusion.2.refs_1_, ...), custom_call_target="tpu_custom_call" | custom-call | flops 85899345920 | bytes 8388608 | tf_op jit(solution)/shard_map/project/pallas_call | solution.py:389
  224.8 4.5 %project.12 = (bf16[256,1024]{1,0:T(8,128)(2,1)S(1)}, f32[256,1024]{1,0:T(8,128)S(1)}) custom-call(bf16[512,2048]{1,0:T(8,128)(2,1)S(1)} %turned_basis.1.turned, bf16[2048,8192]{1,0:T(8,128)(2,1)} %get-tuple-element.45.w, bf16[256,2048]{1,0:T(8,128)(2,1)S(1)} %get-tuple-element.53.refs_0_, bf16[128,1536]{1,0:T(8,128)(2,1)S(1)} %add_convert_fusion.1.refs_1_, ...), custom_call_target="tpu_custom_call" | custom-call | flops 42949672960 | bytes 4194304 | tf_op jit(solution)/shard_map/project/pallas_call | solution.py:389
  230.0 3.4 %collective-permute-done.25.refs_2_.chip_term = bf16[128,1536]{1,0:T(8,128)(2,1)S(1)} collective-permute-done((bf16[128,1536]{1,0:T(8,128)(2,1)S(1)}, bf16[128,1536]{1,0:T(8,128)(2,1)S(1)}, u32[]{:S(2)}, u32[]{:S(2)}) %collective-permute-start.25) | collective-permute-done | bytes 393248 | tf_op jit(solution)/shard_map/ppermute | solution.py:466
  233.5 2.8 %project.13 = (bf16[256,512]{1,0:T(8,128)(2,1)S(1)}, f32[256,512]{1,0:T(8,128)S(1)}) custom-call(bf16[512,2048]{1,0:T(8,128)(2,1)S(1)} %turned_basis.1.turned, bf16[2048,8192]{1,0:T(8,128)(2,1)} %get-tuple-element.45.w, bf16[256,1024]{1,0:T(8,128)(2,1)S(1)} %get-tuple-element.55.refs_0_, bf16[128,2048]{1,0:T(8,128)(2,1)S(1)} %add_convert_fusion.refs_1_, ...), custom_call_target="tpu_custom_call" | custom-call | flops 21474836480 | bytes 2097152 | tf_op jit(solution)/shard_map/project/pallas_call | solution.py:389
  238.1 2.8 %basis.1.refs_1_ = f32[512,512]{1,0:T(8,128)} custom-call(f32[512,512]{1,0:T(8,128)S(1)} %copy-done.1, f32[512,512]{1,0:T(8,128)S(1)} %copy-done.13, bf16[256,512]{1,0:T(8,128)(2,1)S(1)} %get-tuple-element.57.refs_0_), custom_call_target="tpu_custom_call" | custom-call | flops 1 | bytes 1 | tf_op jit(solution)/shard_map/basis/pallas_call | solution.py:335
  240.9 3.8 %collective-permute-done.27.refs_0_.chip_term = bf16[128,2048]{1,0:T(8,128)(2,1)S(1)} collective-permute-done((bf16[128,2048]{1,0:T(8,128)(2,1)S(1)}, bf16[128,2048]{1,0:T(8,128)(2,1)S(1)}, u32[]{:S(2)}, u32[]{:S(2)}) %collective-permute-start.27) | collective-permute-done | bytes 524320 | tf_op jit(solution)/shard_map/ppermute | solution.py:466
  (136 shorter events, 43.9 us)
Async XLA Ops:
  29.5 3.8 %collective-permute-start = (f32[24,128]{1,0:T(8,128)S(1)}, f32[24,128]{1,0:T(8,128)S(1)}, u32[]{:S(2)}, u32[]{:S(2)}) collective-permute-start(f32[24,128]{1,0:T(8,128)S(1)} %concatenate.9), channel_id=1, source_target_pairs={{0,1},{1,0},{2,3},{3,2},{4,5},{5,4},{6,7},{7,6},{8,9},{9,8},{10,11... | collective-permute-start | bytes 36872 | tf_op jit(solution)/shard_map/ppermute | solution.py:462
  33.9 4.7 %collective-permute-start.1 = (f32[24,128]{1,0:T(8,128)S(1)}, f32[24,128]{1,0:T(8,128)S(1)}, u32[]{:S(2)}, u32[]{:S(2)}) collective-permute-start(f32[24,128]{1,0:T(8,128)S(1)} %pad_add_fusion), channel_id=1, source_target_pairs={{0,2},{1,3},{2,0},{3,1},{4,6},{5,7},{6,4},{7,5},{8,10},{9,11},{10,... | collective-permute-start | bytes 36872 | tf_op jit(solution)/shard_map/ppermute | solution.py:462
  59.1 12.8 %collective-permute-start.2 = (bf16[2,256,512]{2,1,0:T(8,128)(2,1)S(1)}, bf16[2,256,512]{2,1,0:T(8,128)(2,1)S(1)}, u32[]{:S(2)}, u32[]{:S(2)}) collective-permute-start(bf16[2,256,512]{2,1,0:T(8,128)(2,1)S(1)} %get-tuple-element.34), channel_id=1, source_target_pairs={{0,1},{1,0},{2,3},{3,2},{4,5},{5,4},{6,7},{7,6},{8,9},{9,8},{10,11... | collective-permute-start | bytes 1572872 | tf_op jit(solution)/shard_map/ppermute | solution.py:462
  68.9 12.8 %collective-permute-start.4 = (bf16[2,128,512]{2,1,0:T(8,128)(2,1)S(1)}, bf16[2,128,512]{2,1,0:T(8,128)(2,1)S(1)}, u32[]{:S(2)}, u32[]{:S(2)}) collective-permute-start(bf16[2,128,512]{2,1,0:T(8,128)(2,1)S(1)} %get-tuple-element.37), channel_id=1, source_target_pairs={{0,1},{1,0},{2,3},{3,2},{4,5},{5,4},{6,7},{7,6},{8,9},{9,8},{10,11... | collective-permute-start | bytes 786440 | tf_op jit(solution)/shard_map/ppermute | solution.py:462
  81.7 9.2 %collective-permute-start.6 = (bf16[2,128,512]{2,1,0:T(8,128)(2,1)S(1)}, bf16[2,128,512]{2,1,0:T(8,128)(2,1)S(1)}, u32[]{:S(2)}, u32[]{:S(2)}) collective-permute-start(bf16[2,128,512]{2,1,0:T(8,128)(2,1)S(1)} %get-tuple-element.40), channel_id=1, source_target_pairs={{0,1},{1,0},{2,3},{3,2},{4,5},{5,4},{6,7},{7,6},{8,9},{9,8},{10,11... | collective-permute-start | bytes 786440 | tf_op jit(solution)/shard_map/ppermute | solution.py:462
  81.8 14.9 %collective-permute-start.5 = (bf16[128,512]{1,0:T(8,128)(2,1)S(1)}, bf16[128,512]{1,0:T(8,128)(2,1)S(1)}, u32[]{:S(2)}, u32[]{:S(2)}) collective-permute-start(bf16[128,512]{1,0:T(8,128)(2,1)S(1)} %fusion.1), channel_id=1, source_target_pairs={{0,2},{1,3},{2,0},{3,1},{4,6},{5,7},{6,4},{7,5},{8,10},{9,11},{10,... | collective-permute-start | bytes 393224 | tf_op jit(solution)/shard_map/ppermute | solution.py:462
  84.4 17.3 %collective-permute-start.3 = (bf16[256,512]{1,0:T(8,128)(2,1)S(1)}, bf16[256,512]{1,0:T(8,128)(2,1)S(1)}, u32[]{:S(2)}, u32[]{:S(2)}) collective-permute-start(bf16[256,512]{1,0:T(8,128)(2,1)S(1)} %fusion.refs_1_), channel_id=1, source_target_pairs={{0,2},{1,3},{2,0},{3,1},{4,6},{5,7},{6,4},{7,5},{8,10},{9,11},{10,... | collective-permute-start | bytes 786440 | tf_op jit(solution)/shard_map/ppermute | solution.py:462
  91.0 12.1 %collective-permute-start.7 = (bf16[128,512]{1,0:T(8,128)(2,1)S(1)}, bf16[128,512]{1,0:T(8,128)(2,1)S(1)}, u32[]{:S(2)}, u32[]{:S(2)}) collective-permute-start(bf16[128,512]{1,0:T(8,128)(2,1)S(1)} %fusion.2), channel_id=1, source_target_pairs={{0,2},{1,3},{2,0},{3,1},{4,6},{5,7},{6,4},{7,5},{8,10},{9,11},{10,... | collective-permute-start | bytes 393224 | tf_op jit(solution)/shard_map/ppermute | solution.py:462
  108.3 75.1 %copy-start.22 = (bf16[512,512]{1,0:T(8,128)(2,1)S(1)}, bf16[512,512]{1,0:T(8,128)(2,1)}, u32[]{:S(2)}) copy-start(bf16[512,512]{1,0:T(8,128)(2,1)} %get-tuple-element.44.refs_0_) | copy-start | bytes 1572868
  108.3 1.9 collective-permute-start.8
  111.2 6.3 %collective-permute-start.9 = (f32[64,640]{1,0:T(8,128)S(1)}, f32[64,640]{1,0:T(8,128)S(1)}, u32[]{:S(2)}, u32[]{:S(2)}) collective-permute-start(f32[64,640]{1,0:T(8,128)S(1)} %constant_dynamic-slice_fusion), channel_id=1, source_target_pairs={{0,8},{4,12},{8,0},{12,4},{1,9},{5,13},{9,1},{13,5},{2,10},{6,14},... | collective-permute-start | bytes 491528 | tf_op jit(solution)/shard_map/ppermute | solution.py:466
  117.5 7.0 %collective-permute-start.10 = (f32[64,640]{1,0:T(8,128)S(1)}, f32[64,640]{1,0:T(8,128)S(1)}, u32[]{:S(2)}, u32[]{:S(2)}) collective-permute-start(f32[64,640]{1,0:T(8,128)S(1)} %dynamic-slice_add_fusion), channel_id=1, source_target_pairs={{0,1},{1,0},{2,3},{3,2},{4,5},{5,4},{6,7},{7,6},{8,9},{9,8},{10,11... | collective-permute-start | bytes 491528 | tf_op jit(solution)/shard_map/ppermute | solution.py:462
  124.6 7.4 %collective-permute-start.11 = (f32[64,640]{1,0:T(8,128)S(1)}, f32[64,640]{1,0:T(8,128)S(1)}, u32[]{:S(2)}, u32[]{:S(2)}) collective-permute-start(f32[64,640]{1,0:T(8,128)S(1)} %add.88), channel_id=1, source_target_pairs={{0,2},{1,3},{2,0},{3,1},{4,6},{5,7},{6,4},{7,5},{8,10},{9,11},{10,... | collective-permute-start | bytes 491528 | tf_op jit(solution)/shard_map/ppermute | solution.py:462
  132.0 7.2 %collective-permute-start.12 = (f32[64,640]{1,0:T(8,128)S(1)}, f32[64,640]{1,0:T(8,128)S(1)}, u32[]{:S(2)}, u32[]{:S(2)}) collective-permute-start(f32[64,640]{1,0:T(8,128)S(1)} %add.89), channel_id=1, source_target_pairs={{0,8},{4,12},{8,0},{12,4},{1,9},{5,13},{9,1},{13,5},{2,10},{6,14},... | collective-permute-start | bytes 491528 | tf_op jit(solution)/shard_map/ppermute | solution.py:466
  133.6 34.8 %collective-permute-start.14 = (bf16[512,512]{1,0:T(8,128)(2,1)}, bf16[512,512]{1,0:T(8,128)(2,1)S(1)}, u32[]{:S(2)}, u32[]{:S(2)}) collective-permute-start(bf16[512,512]{1,0:T(8,128)(2,1)} %get-tuple-element.44.refs_0_), channel_id=1, source_target_pairs={{0,1},{1,2},{2,3},{3,0},{4,5},{5,6},{6,7},{7,4},{8,9},{9,10},{10,1... | collective-permute-start | bytes 1572872 | tf_op jit(solution)/shard_map/ppermute | solution.py:458
  135.0 44.6 %collective-permute-start.15 = (bf16[512,512]{1,0:T(8,128)(2,1)}, bf16[512,512]{1,0:T(8,128)(2,1)S(1)}, u32[]{:S(2)}, u32[]{:S(2)}) collective-permute-start(bf16[512,512]{1,0:T(8,128)(2,1)} %get-tuple-element.44.refs_0_), channel_id=1, source_target_pairs={{0,2},{1,3},{2,0},{3,1},{4,6},{5,7},{6,4},{7,5},{8,10},{9,11},{10,... | collective-permute-start | bytes 1572872 | tf_op jit(solution)/shard_map/ppermute | solution.py:458
  139.2 44.1 %collective-permute-start.16 = (bf16[512,512]{1,0:T(8,128)(2,1)}, bf16[512,512]{1,0:T(8,128)(2,1)S(1)}, u32[]{:S(2)}, u32[]{:S(2)}) collective-permute-start(bf16[512,512]{1,0:T(8,128)(2,1)} %get-tuple-element.44.refs_0_), channel_id=1, source_target_pairs={{0,3},{1,0},{2,1},{3,2},{4,7},{5,4},{6,5},{7,6},{8,11},{9,8},{10,9... | collective-permute-start | bytes 1572872 | tf_op jit(solution)/shard_map/ppermute | solution.py:458
  139.3 1.7 collective-permute-start.13
  193.2 4.9 %collective-permute-start.17 = (bf16[256,512]{1,0:T(8,128)(2,1)S(1)}, bf16[256,512]{1,0:T(8,128)(2,1)S(1)}, u32[]{:S(2)}, u32[]{:S(2)}) collective-permute-start(bf16[256,512]{1,0:T(8,128)(2,1)S(1)} %get-tuple-element.46.refs_0_), channel_id=1, source_target_pairs={{0,4},{4,0},{8,12},{12,8},{1,5},{5,1},{9,13},{13,9},{2,6},{6,2},{1... | collective-permute-start | bytes 786440 | tf_op jit(solution)/shard_map/ppermute | solution.py:466
  197.6 7.0 %collective-permute-start.18 = (bf16[256,1024]{1,0:T(8,128)(2,1)S(1)}, bf16[256,1024]{1,0:T(8,128)(2,1)S(1)}, u32[]{:S(2)}, u32[]{:S(2)}) collective-permute-start(bf16[256,1024]{1,0:T(8,128)(2,1)S(1)} %get-tuple-element.47.refs_0_), channel_id=1, source_target_pairs={{0,4},{4,0},{8,12},{12,8},{1,5},{5,1},{9,13},{13,9},{2,6},{6,2},{1... | collective-permute-start | bytes 1572872 | tf_op jit(solution)/shard_map/ppermute | solution.py:466
  198.1 9.0 %collective-permute-start.19 = (bf16[128,512]{1,0:T(8,128)(2,1)S(1)}, bf16[128,512]{1,0:T(8,128)(2,1)S(1)}, u32[]{:S(2)}, u32[]{:S(2)}) collective-permute-start(bf16[128,512]{1,0:T(8,128)(2,1)S(1)} %add_convert_fusion.6.refs_1_), channel_id=1, source_target_pairs={{0,8},{4,12},{8,0},{12,4},{1,9},{5,13},{9,1},{13,5},{2,10},{6,14},... | collective-permute-start | bytes 393224 | tf_op jit(solution)/shard_map/ppermute | solution.py:466
  204.5 8.6 %collective-permute-start.20 = (bf16[256,1536]{1,0:T(8,128)(2,1)S(1)}, bf16[256,1536]{1,0:T(8,128)(2,1)S(1)}, u32[]{:S(2)}, u32[]{:S(2)}) collective-permute-start(bf16[256,1536]{1,0:T(8,128)(2,1)S(1)} %get-tuple-element.49.refs_0_), channel_id=1, source_target_pairs={{0,4},{4,0},{8,12},{12,8},{1,5},{5,1},{9,13},{13,9},{2,6},{6,2},{1... | collective-permute-start | bytes 2359304 | tf_op jit(solution)/shard_map/ppermute | solution.py:466
  205.7 8.5 %collective-permute-start.21 = (bf16[128,1024]{1,0:T(8,128)(2,1)S(1)}, bf16[128,1024]{1,0:T(8,128)(2,1)S(1)}, u32[]{:S(2)}, u32[]{:S(2)}) collective-permute-start(bf16[128,1024]{1,0:T(8,128)(2,1)S(1)} %add_convert_fusion.4.refs_1_), channel_id=1, source_target_pairs={{0,8},{4,12},{8,0},{12,4},{1,9},{5,13},{9,1},{13,5},{2,10},{6,14},... | collective-permute-start | bytes 786440 | tf_op jit(solution)/shard_map/ppermute | solution.py:466
  213.0 8.4 %collective-permute-start.22 = (bf16[256,1536]{1,0:T(8,128)(2,1)S(1)}, bf16[256,1536]{1,0:T(8,128)(2,1)S(1)}, u32[]{:S(2)}, u32[]{:S(2)}) collective-permute-start(bf16[256,1536]{1,0:T(8,128)(2,1)S(1)} %get-tuple-element.51.refs_0_), channel_id=1, source_target_pairs={{0,4},{4,0},{8,12},{12,8},{1,5},{5,1},{9,13},{13,9},{2,6},{6,2},{1... | collective-permute-start | bytes 2359304 | tf_op jit(solution)/shard_map/ppermute | solution.py:466
  213.2 11.6 %collective-permute-start.23 = (bf16[128,1536]{1,0:T(8,128)(2,1)S(1)}, bf16[128,1536]{1,0:T(8,128)(2,1)S(1)}, u32[]{:S(2)}, u32[]{:S(2)}) collective-permute-start(bf16[128,1536]{1,0:T(8,128)(2,1)S(1)} %add_convert_fusion.2.refs_1_), channel_id=1, source_target_pairs={{0,8},{4,12},{8,0},{12,4},{1,9},{5,13},{9,1},{13,5},{2,10},{6,14},... | collective-permute-start | bytes 1179656 | tf_op jit(solution)/shard_map/ppermute | solution.py:466
  221.3 8.0 %collective-permute-start.24 = (bf16[256,2048]{1,0:T(8,128)(2,1)S(1)}, bf16[256,2048]{1,0:T(8,128)(2,1)S(1)}, u32[]{:S(2)}, u32[]{:S(2)}) collective-permute-start(bf16[256,2048]{1,0:T(8,128)(2,1)S(1)} %get-tuple-element.53.refs_0_), channel_id=1, source_target_pairs={{0,4},{4,0},{8,12},{12,8},{1,5},{5,1},{9,13},{13,9},{2,6},{6,2},{1... | collective-permute-start | bytes 3145736 | tf_op jit(solution)/shard_map/ppermute | solution.py:466
  221.5 12.0 %collective-permute-start.25 = (bf16[128,1536]{1,0:T(8,128)(2,1)S(1)}, bf16[128,1536]{1,0:T(8,128)(2,1)S(1)}, u32[]{:S(2)}, u32[]{:S(2)}) collective-permute-start(bf16[128,1536]{1,0:T(8,128)(2,1)S(1)} %add_convert_fusion.1.refs_1_), channel_id=1, source_target_pairs={{0,8},{4,12},{8,0},{12,4},{1,9},{5,13},{9,1},{13,5},{2,10},{6,14},... | collective-permute-start | bytes 1179656 | tf_op jit(solution)/shard_map/ppermute | solution.py:466
  229.2 7.2 %collective-permute-start.29 = (bf16[256,1024]{1,0:T(8,128)(2,1)S(1)}, bf16[256,1024]{1,0:T(8,128)(2,1)S(1)}, u32[]{:S(2)}, u32[]{:S(2)}) collective-permute-start(bf16[256,1024]{1,0:T(8,128)(2,1)S(1)} %get-tuple-element.55.refs_0_), channel_id=1, source_target_pairs={{0,4},{4,0},{8,12},{12,8},{1,5},{5,1},{9,13},{13,9},{2,6},{6,2},{1... | collective-permute-start | bytes 1572872 | tf_op jit(solution)/shard_map/ppermute | solution.py:466
  229.5 15.2 %collective-permute-start.27 = (bf16[128,2048]{1,0:T(8,128)(2,1)S(1)}, bf16[128,2048]{1,0:T(8,128)(2,1)S(1)}, u32[]{:S(2)}, u32[]{:S(2)}) collective-permute-start(bf16[128,2048]{1,0:T(8,128)(2,1)S(1)} %add_convert_fusion.refs_1_), channel_id=1, source_target_pairs={{0,8},{4,12},{8,0},{12,4},{1,9},{5,13},{9,1},{13,5},{2,10},{6,14},... | collective-permute-start | bytes 1572872 | tf_op jit(solution)/shard_map/ppermute | solution.py:466
  236.3 4.5 %collective-permute-start.26 = (bf16[256,512]{1,0:T(8,128)(2,1)S(1)}, bf16[256,512]{1,0:T(8,128)(2,1)S(1)}, u32[]{:S(2)}, u32[]{:S(2)}) collective-permute-start(bf16[256,512]{1,0:T(8,128)(2,1)S(1)} %get-tuple-element.57.refs_0_), channel_id=1, source_target_pairs={{0,4},{4,0},{8,12},{12,8},{1,5},{5,1},{9,13},{13,9},{2,6},{6,2},{1... | collective-permute-start | bytes 786440 | tf_op jit(solution)/shard_map/ppermute | solution.py:466
  236.5 17.4 %collective-permute-start.30 = (bf16[128,1024]{1,0:T(8,128)(2,1)S(1)}, bf16[128,1024]{1,0:T(8,128)(2,1)S(1)}, u32[]{:S(2)}, u32[]{:S(2)}) collective-permute-start(bf16[128,1024]{1,0:T(8,128)(2,1)S(1)} %add_convert_fusion.3), channel_id=1, source_target_pairs={{0,8},{4,12},{8,0},{12,4},{1,9},{5,13},{9,1},{13,5},{2,10},{6,14},... | collective-permute-start | bytes 786440 | tf_op jit(solution)/shard_map/ppermute | solution.py:466
  246.0 8.9 %collective-permute-start.28 = (bf16[128,512]{1,0:T(8,128)(2,1)S(1)}, bf16[128,512]{1,0:T(8,128)(2,1)S(1)}, u32[]{:S(2)}, u32[]{:S(2)}) collective-permute-start(bf16[128,512]{1,0:T(8,128)(2,1)S(1)} %pass_on.1), channel_id=1, source_target_pairs={{0,8},{4,12},{8,0},{12,4},{1,9},{5,13},{9,1},{13,5},{2,10},{6,14},... | collective-permute-start | bytes 393224 | tf_op jit(solution)/shard_map/ppermute | solution.py:466
  (29 other events, 249.0 us)
where the time goes:
time: 257 us; the launch traced here: 256 us
  Pallas kernels  144 us (56%)
  waiting for transfers between devices  63.9 us (25%)
  starting transfers between devices  33.3 us (13%)
  local copies, waits for them, and re-layouts  9.27 us (4%)
  other arithmetic  2.98 us (1%)
    pallas_call x3, Pallas kernels, weigh(): pl.pallas_call(weigh_body, grid_spec=pltpu.PrefetchScalarGridSpec(num_sca...  35.3 us
    pallas_call x7, Pallas kernels, project(): pl.pallas_call(project_body, grid=(steps,), in_specs=[pl.BlockSpec((size,...  33.2 us
    ppermute x10, waiting for transfers between devices, swap_col(): return lax.ppermute(x, 'col', [(i, i ^ bit) for i in range(4)])  31.6 us
    pallas_call x1, Pallas kernels, row_sums(): pl.pallas_call(totals_body, grid=(rows // tile,), in_specs=[pl.BlockSpec(...  27.6 us
    pallas_call x1, Pallas kernels, factor_inverse(): pl.pallas_call(factor_body, grid=(1,), in_specs=[SMEM, whole(*mine.shape)...  27.4 us
    ppermute x18, waiting for transfers between devices, swap(): return lax.ppermute(x, 'row', [(i, i ^ bit) for i in range(4)])  17.4 us
    ppermute x10, starting transfers between devices, swap_col(): return lax.ppermute(x, 'col', [(i, i ^ bit) for i in range(4)])  15.6 us
    ppermute x3, waiting for transfers between devices, rotate(): return lax.ppermute(x, 'col', [(i, (i + by) % n) for i in range(n)])  14.9 us
  transfers between devices with their start and end apart: 31, of which 18 were waited for; matrix products, arithmetic and copies ran while one was open for 0% of the time, Pallas kernels for 34%

commit v1 on v0

--- a/solution.py
+++ b/solution.py
@@ -39,9 +39,11 @@
     return lax.broadcasted_iota(jnp.int32, (n, n), 0) == lax.broadcasted_iota(jnp.int32, (n, n), 1)
 
 
-def totals_body(counts, out, small):
+def totals_body(counts, ctx_counts, out, small):
     tile, width = counts.shape
-    for at in range(tile // NB):
+    n = tile // NB
+    step = pl.program_id(0)
+    for at in range(n):
         parts = []
         for r in range(at * NB, (at + 1) * NB, 32):
             acc = None
@@ -51,37 +53,40 @@
                 acc = value if acc is None else acc + value
             parts.append(jnp.sum(acc.astype(F32), axis=1, keepdims=True))
         column = jnp.concatenate(parts, 0)
-        out[at] = jnp.sum(jnp.where(eye(NB), column, 0.0), axis=0, keepdims=True)
-
-
-def row_sums(counts):
+        out[step * n + at] = jnp.sum(jnp.where(eye(NB), column, 0.0), axis=0, keepdims=True)
+
+    @pl.when(step == 0)
+    def _():
+        count = ctx_counts[...].astype(F32)
+        weight = jnp.sqrt(count) * jnp.sqrt(jnp.sqrt(count))
+        out[out.shape[0] - 1] = jnp.broadcast_to(jnp.sum(weight, axis=1, keepdims=True), (1, NB))
+
+
+def row_sums(counts, ctx_counts):
     rows, width = counts.shape
     tile = 2 * NB
     return pl.pallas_call(
         totals_body,
         grid=(rows // tile,),
-        in_specs=[pl.BlockSpec((tile, width), lambda g: (g, 0))],
-        out_specs=[
-            pl.BlockSpec((tile // NB, 1, NB), lambda g: (g, 0, 0)),
-            pl.BlockSpec((tile, width), lambda g: (g, 0)),
-        ],
+        in_specs=[pl.BlockSpec((tile, width), lambda g: (g, 0)), whole(1, width)],
+        out_specs=[whole(rows // NB + 1, 1, NB), pl.BlockSpec((tile, width), lambda g: (g, 0))],
         out_shape=[
-            jax.ShapeDtypeStruct((rows // NB, 1, NB), F32),
+            jax.ShapeDtypeStruct((rows // NB + 1, 1, NB), F32),
             jax.ShapeDtypeStruct((rows, width), jnp.int8),
         ],
         name="row_sums",
         cost_estimate=cost(2000 * rows * width, 1),
-        compiler_params=limit(50),
-    )(counts)
-
-
-def weigh_body(order, small, base, log_ctx, omega, *refs):
-    w, send, keep = refs[-3:]
+        compiler_params=limit(45),
+    )(counts, ctx_counts)
+
+
+def weigh_body(split, order, small, row_total, ctx_total, ctx_counts, omega, *refs):
+    w, keep, *sends = refs[-4:] if split else refs[-3:]
     tile, width = w.shape
     step = min(2048, width)
-    column = jnp.concatenate(
-        [jnp.sum(jnp.where(eye(NB), base[i], 0.0), axis=1, keepdims=True) for i in range(tile // NB)]
-    )
+    row_log = [jnp.log(ctx_total[0]) - jnp.log(F32(5.0)) - jnp.log(row_total[i]) for i in range(tile // NB)]
+    column = jnp.concatenate([jnp.sum(jnp.where(eye(NB), x, 0.0), axis=1, keepdims=True) for x in row_log])
+    log_ctx = 0.75 * jnp.log(ctx_counts[...].astype(F32))
     acc = jnp.zeros((tile, omega.shape[1]), F32)
     for c in range(0, width, step):
         here = slice(c, c + step)
@@ -92,50 +97,66 @@
             w[rows, here] = jnp.maximum(value, 0.0).astype(BF16)
         acc = acc + jnp.dot(w[:, here], omega[here, :], preferred_element_type=F32)
 
-    @pl.when(pl.program_id(0) < 2)
-    def _():
-        send[0] = acc.astype(BF16)
+    if split:
+        for g in range(2):
+
+            @pl.when(pl.program_id(0) == g)
+            def _(g=g):
+                sends[g][...] = acc.astype(BF16)
+
+    else:
+
+        @pl.when(pl.program_id(0) < 2)
+        def _():
+            sends[0][0] = acc.astype(BF16)
 
     @pl.when(pl.program_id(0) >= 2)
     def _():
         keep[0] = acc
 
 
-def weigh(small, base, log_ctx, omega, w, order, offset, tile, tokens):
+def weigh(small, totals, ctx_counts, omega, w, order, offset, tile, tokens, split):
     n = order.shape[0]
     rows, width = small.shape
     size = omega.shape[1]
     share = rows // n
     place = lambda g, o: (o[g] * (share // tile) + offset // tile, 0)
     held = ([] if w is None else [w]) + tokens
-    return pl.pallas_call(
-        weigh_body,
+    if split:
+        sends = [jax.ShapeDtypeStruct((tile, size), BF16)] * 2
+        send_specs = [whole(tile, size)] * 2
+    else:
+        sends = [jax.ShapeDtypeStruct((2, tile, size), BF16)]
+        send_specs = [pl.BlockSpec((1, tile, size), lambda g, o: (jnp.minimum(g, 1), 0, 0))]
+    return pl.pallas_call(
+        functools.partial(weigh_body, split),
         grid_spec=pltpu.PrefetchScalarGridSpec(
             num_scalar_prefetch=1,
             grid=(n,),
             in_specs=[
                 pl.BlockSpec((tile, width), place),
                 pl.BlockSpec((tile // NB, 1, NB), lambda g, o: place(g, o) + (0,)),
+                pl.BlockSpec((1, 1, NB), lambda g, o: (rows // NB, 0, 0)),
                 pl.BlockSpec((1, width), lambda g, o: (0, 0)),
                 VMEM,
             ]
             + [ANY] * len(held),
             out_specs=[
                 pl.BlockSpec((tile, width), place),
-                pl.BlockSpec((1, tile, size), lambda g, o: (jnp.minimum(g, 1), 0, 0)),
                 pl.BlockSpec((1, tile, size), lambda g, o: (jnp.maximum(g - 2, 0), 0, 0)),
-            ],
+            ]
+            + send_specs,
         ),
         out_shape=[
             jax.ShapeDtypeStruct((rows, width), BF16),
-            jax.ShapeDtypeStruct((2, tile, size), BF16),
             jax.ShapeDtypeStruct((2, tile, size), F32),
-        ],
-        input_output_aliases={} if w is None else {5: 0},
+        ]
+        + sends,
+        input_output_aliases={} if w is None else {6: 0},
         name="weigh_and_sketch",
         cost_estimate=cost(40 * n * tile * width * size, 6 * n * tile * width),
         compiler_params=limit(44),
-    )(order, small, base, log_ctx, omega, *held)
+    )(order, small, totals, totals, ctx_counts, omega, *held)
 
 
 PACKED = (((0, 0), (0, 1), (0, 2), (0, 3), (3, 3)), ((1, 1), (1, 2), (1, 3), (2, 2), (2, 3)))
@@ -406,7 +427,8 @@
 
 
 def finish_body(scale, start, mine, core_term, chip_term, *refs):
-    out, turned, arrival = refs[-3:]
+    out, tick, turned, arrival = refs[-4:]
+    tick[...] = jnp.zeros_like(tick)
     total = mine[...] + core_term[...].astype(F32) + chip_term[...].astype(F32)
     turned[...] = jnp.transpose(total * scale)
     copy = pltpu.make_async_copy(turned, out.at[pl.ds(start, turned.shape[0])], arrival)
@@ -414,7 +436,7 @@
     copy.wait()
 
 
-def finish(own, core_term, chip_term, out, start, full, scale):
+def finish(own, core_term, chip_term, out, start, full, scale, tokens):
     size, width = chip_term.shape
     held = [] if out is None else [out]
     return pl.pallas_call(
@@ -425,15 +447,15 @@
             pl.BlockSpec((size, width), lambda g: (1, 0)),
             whole(size, width),
         ]
-        + [ANY] * len(held),
-        out_specs=ANY,
-        out_shape=jax.ShapeDtypeStruct((full, size), F32),
+        + [ANY] * len(held + tokens),
+        out_specs=[ANY, whole(8, NB)],
+        out_shape=[jax.ShapeDtypeStruct((full, size), F32), jax.ShapeDtypeStruct((8, NB), F32)],
         input_output_aliases={3: 0} if held else {},
         scratch_shapes=[pltpu.VMEM((width, size), F32), pltpu.SemaphoreType.DMA],
         name="finish",
         cost_estimate=cost(1, 1),
         compiler_params=limit(24),
-    )(own, core_term, chip_term, *held)
+    )(own, core_term, chip_term, *held, *tokens)
 
 
 def pass_body(mine, core_term, *refs):
@@ -480,32 +502,39 @@
     return [2 * NB] * ((n - 2) // 2) + [NB] * (n - (n - 2) // 2 * 2) if n > 2 else [NB] * n
 
 
-def sketch_phase(counts, log_ctx, ctx_sum, omega, col):
+def sketch_phase(counts, ctx_counts, omega, col):
     rows, width = counts.shape
-    part, small = row_sums(counts)
-    part = jnp.concatenate([part.reshape(rows // NB, NB), jnp.broadcast_to(ctx_sum, (8, NB))])
-    part = part + swap_col(part, 1)
-    part = part + swap_col(part, 2)
-    logs = jnp.log(part)
-    base = logs[-1, 0] - jnp.log(F32(5.0)) - logs[:-8]
-    base = base.reshape(rows // NB, 1, NB)
+    ctx_counts = ctx_counts.reshape(1, width)
+    totals, small = row_sums(counts, ctx_counts)
+    totals = totals + swap_col(totals, 1)
+    totals = totals + swap_col(totals, 2)
     order = jnp.stack([col ^ 1, col ^ 3, col ^ 2, col])
+    tiles = pieces_of(rows // 4)
     w, offset, pieces, passed, arrived = None, 0, [], [], []
-    for k, tile in enumerate(pieces_of(rows // 4)):
+    for k, tile in enumerate(tiles):
+        last = k == len(tiles) - 1
         tokens = passed[k - 2 : k - 1] if k >= 2 else []
         tokens = tokens + (arrived[k - 3 : k - 2] if k >= 3 else [])
-        w, send, keep = weigh(small, base, log_ctx, omega, w, order, offset, tile, tokens)
+        w, keep, *sends = weigh(small, totals, ctx_counts, omega, w, order, offset, tile, tokens, last)
         offset += tile
-        near = swap_col(send, 1)
-        passed.append((keep[0] + near[1].astype(F32)).astype(BF16))
+        if last:
+            theirs, mine = swap_col(sends[1], 1), swap_col(sends[0], 1)
+            passed.append(pass_on(keep.reshape(2 * tile, -1), theirs, arrived[: max(0, k - 1)]))
+            mine = (mine, None)
+        else:
+            near = swap_col(sends[0], 1)
+            passed.append((keep[0] + near[1].astype(F32)).astype(BF16))
+            mine = (near, 0)
         arrived.append(swap_col(passed[k], 2))
-        pieces.append([(keep, 1), (near, 0), (arrived[k], None)])
+        pieces.append([(keep, 1), mine, (arrived[k], None)])
     return w, pieces
 
 
-def sketch_phase_any(counts, log_ctx, ctx_sum, omega, col):
+def sketch_phase_any(counts, ctx_counts, omega, col):
     row_part = jnp.sum(counts.astype(F32), axis=1)
-    row_total, ctx_total = lax.psum((row_part, ctx_sum), "col")
+    ctx_weight = ctx_counts.astype(F32) ** 0.75
+    log_ctx = jnp.log(ctx_weight)[None, :]
+    row_total, ctx_total = lax.psum((row_part, jnp.sum(ctx_weight)), "col")
     value = jnp.log(counts.astype(F32)) + (
         jnp.log(ctx_total) - jnp.log(F32(5.0)) - jnp.log(row_total)[:, None] - log_ctx
     )
@@ -520,12 +549,9 @@
     row = lax.axis_index("row")
     col = lax.axis_index("col")
     core, chip = row % 2, row // 2
-    ctx_weight = ctx_counts.astype(F32) ** 0.75
-    ctx_sum = jnp.sum(ctx_weight)
-    log_ctx = jnp.log(ctx_weight)[None, :]
     direct = n == 4 and rows % (4 * NB) == 0
     phase = sketch_phase if direct else sketch_phase_any
-    w, pieces = phase(counts, log_ctx, ctx_sum, omega, col)
+    w, pieces = phase(counts, ctx_counts, omega, col)
     sketch, sketch_b, half, other_half = gram_of(core.reshape(1), pieces)
     half = half + swap(other_half, 1)
     quarter = half_of(half, chip) + swap(half_of(half, 1 - chip), 2)
@@ -547,23 +573,34 @@
     scale = float(1.0 / (rows * lax.axis_size("row")) ** 0.5)
     quarter = omega.shape[1] // 4
     out, start = None, 0
-    sent, passed, arrived = [], [], []
+    sent, passed, arrived, ended = [], [], [], []
+    terms = []
+
+    def end(tokens):
+        j = len(ended)
+        out = ended[-1][0] if ended else None
+        ended.append(finish(*terms[j][:2], arrived[j], out, terms[j][2], width, scale, tokens))
+
     for j, pieces in enumerate(widths):
         piece = pieces * unit
         tokens = sent[-1:] + (passed[-2:-1] if j >= 2 else []) + (arrived[-3:-2] if j >= 3 else [])
         send, mine = project(turned, w, tokens, start, piece, unit)
+        sent.append(send)
         core_term = swap(send, 1)
         if j == len(widths) - 1:
             basis = basis_of(inverse, sketch, [send])
-            chip_send = pass_on(mine, core_term, [arrived[-2], basis])
+            for _ in range(3):
+                end([])
+            chip_send = pass_on(mine, core_term, [arrived[-2], basis, ended[-1][1]])
         else:
             chip_send = (mine[:quarter] + core_term[:quarter].astype(F32)).astype(BF16)
-        chip_term = swap(chip_send, 2)
-        sent.append(send)
         passed.append(chip_send)
-        arrived.append(chip_term)
-        out = finish(mine, core_term, chip_term, out, start, width, scale)
+        arrived.append(swap(chip_send, 2))
+        terms.append((mine, core_term, start))
         start += piece
+    while len(ended) < len(widths):
+        end([])
+    out = ended[-1][0]
     return (basis, out)
 
 

time: 257 us -> 248 us (0.965)
  waiting for transfers between devices: 63.9 us -> 51 us
  Pallas kernels: 144 us -> 148 us
    ppermute x10 -> x11, waiting for transfers between devices: 31.6 us -> 23.3 us  [swap_col(): return lax.ppermute(x, 'col', [(i, i ^ bit) for i in range(4)])]
    ppermute x18, waiting for transfers between devices: 17.4 us -> 13.6 us  [swap(): return lax.ppermute(x, 'row', [(i, i ^ bit) for i in range(4)])]
    pallas_call x7, Pallas kernels: 7.37 us -> 10.9 us  [finish(): pl.pallas_call(functools.partial(finish_body, scale, start), grid=(1,), i...]
    ppermute x10 -> x11, starting transfers between devices: 15.6 us -> 19 us  [swap_col(): return lax.ppermute(x, 'col', [(i, i ^ bit) for i in range(4)])]
    unnamed x60 -> x62, local copies, waits for them, and re-layouts: 8.01 us -> 9.42 us
  transfers between devices with their start and end apart: 31 -> 32, of which waited for: 18 -> 15; matrix products, arithmetic and copies ran while one was open for 0% -> 0% of each run, Pallas kernels for 34% -> 36%
where the time goes in v1:
time: 248 us; the launch traced here: 247 us
  Pallas kernels  148 us (60%)
  waiting for transfers between devices  51 us (21%)
  starting transfers between devices  35.5 us (14%)
  local copies, waits for them, and re-layouts  9.53 us (4%)
    pallas_call x3, Pallas kernels, weigh(): pl.pallas_call(functools.partial(weigh_body, split), grid_spec=pltpu.Pref...  35.1 us
    pallas_call x7, Pallas kernels, project(): pl.pallas_call(project_body, grid=(steps,), in_specs=[pl.BlockSpec((size,...  33.2 us
    pallas_call x1, Pallas kernels, row_sums(): pl.pallas_call(totals_body, grid=(rows // tile,), in_specs=[pl.BlockSpec(...  27.5 us
    pallas_call x1, Pallas kernels, factor_inverse(): pl.pallas_call(factor_body, grid=(1,), in_specs=[SMEM, whole(*mine.shape)...  27.4 us
    ppermute x11, waiting for transfers between devices, swap_col(): return lax.ppermute(x, 'col', [(i, i ^ bit) for i in range(4)])  23.3 us
    ppermute x11, starting transfers between devices, swap_col(): return lax.ppermute(x, 'col', [(i, i ^ bit) for i in range(4)])  19 us
    ppermute x3, waiting for transfers between devices, rotate(): return lax.ppermute(x, 'col', [(i, (i + by) % n) for i in range(n)])  14.1 us
    ppermute x18, waiting for transfers between devices, swap(): return lax.ppermute(x, 'row', [(i, i ^ bit) for i in range(4)])  13.6 us
  transfers between devices with their start and end apart: 32, of which 15 were waited for; matrix products, arithmetic and copies ran while one was open for 0% of the time, Pallas kernels for 36%

profile of v1, /device:TPU:8, one launch (start us, length us, event | category | flops | bytes accessed | tf_op | source)
XLA Modules:
  0.0 246.8 jit_solution(3813944342266464722)
XLA Ops:
  1.4 27.5 %row_sums.1 = (f32[17,1,128]{2,1,0:T(1,128)S(1)}, s8[2048,8192]{1,0:T(32,128)(4,1)}) custom-call(s32[2048,8192]{1,0:T(8,128)} %counts.1, s32[1,8192]{1,0:T(1,128)S(1)} %bitcast.20), custom_call_target="tpu_custom_call" | custom-call | flops 33554432000 | bytes 1 | tf_op jit(solution)/shard_map/row_sums/pallas_call | solution.py:68
  28.9 3.7 %collective-permute-done = f32[17,1,128]{2,1,0:T(1,128)S(1)} collective-permute-done((f32[17,1,128]{2,1,0:T(1,128)S(1)}, f32[17,1,128]{2,1,0:T(1,128)S(1)}, u32[]{:S(2)}, u32[]{:S(2)}) %collective-permute-start) | collective-permute-done | bytes 8736 | tf_op jit(solution)/shard_map/ppermute | solution.py:484
  32.5 2.7 %collective-permute-start.1 = (f32[17,1,128]{2,1,0:T(1,128)S(1)}, f32[17,1,128]{2,1,0:T(1,128)S(1)}, u32[]{:S(2)}, u32[]{:S(2)}) collective-permute-start(f32[17,1,128]{2,1,0:T(1,128)S(1)} %add.71), channel_id=1, source_target_pairs={{0,2},{1,3},{2,0},{3,1},{4,6},{5,7},{6,4},{7,5},{8,10},{9,11},{10,... | collective-permute-start | bytes 26120 | tf_op jit(solution)/shard_map/ppermute | solution.py:484
  37.2 3.4 %copy-done.22 = bf16[8192,512]{1,0:T(8,128)(2,1)S(1)} copy-done((bf16[8192,512]{1,0:T(8,128)(2,1)S(1)}, bf16[8192,512]{1,0:T(8,128)(2,1)}, u32[]{:S(2)}) %copy-start.22) | copy-done | bytes 8388632
  40.6 15.8 %weigh_and_sketch.3 = (bf16[2048,8192]{1,0:T(8,128)(2,1)}, f32[2,256,512]{2,1,0:T(8,128)S(1)}, bf16[2,256,512]{2,1,0:T(8,128)(2,1)S(1)}) custom-call(s32[4]{0:T(128)S(1)} %pad_add_fusion.order, s8[2048,8192]{1,0:T(32,128)(4,1)} %get-tuple-element.40.small, f32[17,1,128]{2,1,0:T(1,128)S(1)} %add.72.row_total.ctx_total, ...), custom_call_target="tpu_custom_call" | custom-call | flops 171798691840 | bytes 50331648 | tf_op jit(solution)/shard_map/weigh_and_sketch/pallas_call | solution.py:131
  56.4 9.6 %weigh_and_sketch.4 = (bf16[2048,8192]{1,0:T(8,128)(2,1)}, f32[2,128,512]{2,1,0:T(8,128)S(1)}, bf16[2,128,512]{2,1,0:T(8,128)(2,1)S(1)}) custom-call(s32[4]{0:T(128)S(1)} %pad_add_fusion.order, s8[2048,8192]{1,0:T(32,128)(4,1)} %get-tuple-element.40.small, f32[17,1,128]{2,1,0:T(1,128)S(1)} %add.72.row_total.ctx_total, ...), custom_call_target="tpu_custom_call", output_to_operand_aliasing={{0}: (6, {})} | custom-call | flops 85899345920 | bytes 25165824 | tf_op jit(solution)/shard_map/weigh_and_sketch/pallas_call | solution.py:131
  66.0 2.0 collective-permute-start.4
  69.3 5.4 %collective-permute-start.3 = (bf16[256,512]{1,0:T(8,128)(2,1)S(1)}, bf16[256,512]{1,0:T(8,128)(2,1)S(1)}, u32[]{:S(2)}, u32[]{:S(2)}) collective-permute-start(bf16[256,512]{1,0:T(8,128)(2,1)S(1)} %fusion.refs_1_), channel_id=1, source_target_pairs={{0,2},{1,3},{2,0},{3,1},{4,6},{5,7},{6,4},{7,5},{8,10},{9,11},{10,... | collective-permute-start | bytes 786440 | tf_op jit(solution)/shard_map/ppermute | solution.py:484
  74.8 9.6 %weigh_and_sketch.5 = (bf16[2048,8192]{1,0:T(8,128)(2,1)}, f32[2,128,512]{2,1,0:T(8,128)S(1)}, bf16[128,512]{1,0:T(8,128)(2,1)S(1)}, bf16[128,512]{1,0:T(8,128)(2,1)S(1)}) custom-call(s32[4]{0:T(128)S(1)} %pad_add_fusion.order, s8[2048,8192]{1,0:T(32,128)(4,1)} %get-tuple-element.40.small, ...), custom_call_target="tpu_custom_call", output_to_operand_aliasing={{0}: (6, {})} | custom-call | flops 85899345920 | bytes 25165824 | tf_op jit(solution)/shard_map/weigh_and_sketch/pallas_call | solution.py:131
  84.6 2.1 collective-permute-start.6
  86.6 2.8 %collective-permute-done.7.core_term = bf16[128,512]{1,0:T(8,128)(2,1)S(1)} collective-permute-done((bf16[128,512]{1,0:T(8,128)(2,1)S(1)}, bf16[128,512]{1,0:T(8,128)(2,1)S(1)}, u32[]{:S(2)}, u32[]{:S(2)}) %collective-permute-start.7) | collective-permute-done | bytes 131104 | tf_op jit(solution)/shard_map/ppermute | solution.py:484
  89.4 3.3 %collective-permute-start.8 = (bf16[128,512]{1,0:T(8,128)(2,1)S(1)}, bf16[128,512]{1,0:T(8,128)(2,1)S(1)}, u32[]{:S(2)}, u32[]{:S(2)}) collective-permute-start(bf16[128,512]{1,0:T(8,128)(2,1)S(1)} %pass_on.2), channel_id=1, source_target_pairs={{0,2},{1,3},{2,0},{3,1},{4,6},{5,7},{6,4},{7,5},{8,10},{9,11},{10,... | collective-permute-start | bytes 393224 | tf_op jit(solution)/shard_map/ppermute | solution.py:484
  92.7 3.0 %collective-permute-done.8.refs_8_ = bf16[128,512]{1,0:T(8,128)(2,1)S(1)} collective-permute-done((bf16[128,512]{1,0:T(8,128)(2,1)S(1)}, bf16[128,512]{1,0:T(8,128)(2,1)S(1)}, u32[]{:S(2)}, u32[]{:S(2)}) %collective-permute-start.8) | collective-permute-done | bytes 131104 | tf_op jit(solution)/shard_map/ppermute | solution.py:484
  96.4 4.6 %gram.1 = (f32[512,512]{1,0:T(8,128)}, bf16[512,512]{1,0:T(8,128)(2,1)}, f32[128,640]{1,0:T(8,128)}, f32[128,640]{1,0:T(8,128)}) custom-call(s32[1]{0:T(128)} %bitcast.core, f32[2,256,512]{2,1,0:T(8,128)} %copy-done.17, bf16[2,256,512]{2,1,0:T(8,128)(2,1)} %copy-done.26, bf16[256,512]{1,0:T(8,128)(2,1)} %copy-done.18, f32[2,128,512]{2,1,0:T(8,128)} %copy-done.21, ...), custom_call_target="tpu_custom_call" | custom-call | flops 1610612736 | bytes 2097152 | tf_op jit(solution)/shard_map/gram/pallas_call | solution.py:207
  105.4 4.9 %collective-permute-done.10 = f32[64,640]{1,0:T(8,128)S(1)} collective-permute-done((f32[64,640]{1,0:T(8,128)S(1)}, f32[64,640]{1,0:T(8,128)S(1)}, u32[]{:S(2)}, u32[]{:S(2)}) %collective-permute-start.10) | collective-permute-done | bytes 163872 | tf_op jit(solution)/shard_map/ppermute | solution.py:488
  110.4 5.3 %collective-permute-done.11 = f32[64,640]{1,0:T(8,128)S(1)} collective-permute-done((f32[64,640]{1,0:T(8,128)S(1)}, f32[64,640]{1,0:T(8,128)S(1)}, u32[]{:S(2)}, u32[]{:S(2)}) %collective-permute-start.11) | collective-permute-done | bytes 163872 | tf_op jit(solution)/shard_map/ppermute | solution.py:484
  115.8 3.3 %collective-permute-start.12 = (f32[64,640]{1,0:T(8,128)S(1)}, f32[64,640]{1,0:T(8,128)S(1)}, u32[]{:S(2)}, u32[]{:S(2)}) collective-permute-start(f32[64,640]{1,0:T(8,128)S(1)} %add.79), channel_id=1, source_target_pairs={{0,2},{1,3},{2,0},{3,1},{4,6},{5,7},{6,4},{7,5},{8,10},{9,11},{10,... | collective-permute-start | bytes 491528 | tf_op jit(solution)/shard_map/ppermute | solution.py:484
  119.1 5.5 %collective-permute-done.12 = f32[64,640]{1,0:T(8,128)S(1)} collective-permute-done((f32[64,640]{1,0:T(8,128)S(1)}, f32[64,640]{1,0:T(8,128)S(1)}, u32[]{:S(2)}, u32[]{:S(2)}) %collective-permute-start.12) | collective-permute-done | bytes 163872 | tf_op jit(solution)/shard_map/ppermute | solution.py:484
  126.1 3.7 %collective-permute-start.16 = (bf16[512,512]{1,0:T(8,128)(2,1)}, bf16[512,512]{1,0:T(8,128)(2,1)S(1)}, u32[]{:S(2)}, u32[]{:S(2)}) collective-permute-start(bf16[512,512]{1,0:T(8,128)(2,1)} %get-tuple-element.54.refs_0_), channel_id=1, source_target_pairs={{0,2},{1,3},{2,0},{3,1},{4,6},{5,7},{6,4},{7,5},{8,10},{9,11},{10,... | collective-permute-start | bytes 1572872 | tf_op jit(solution)/shard_map/ppermute | solution.py:480
  133.2 27.4 %factor_inverse.1.inverse = f32[512,512]{1,0:T(8,128)S(1)} custom-call(s32[1]{0:T(128)} %bitcast.core, f32[128,640]{1,0:T(8,128)S(1)} %maximum_select_fusion.mine, f32[128,640]{1,0:T(8,128)S(1)} %collective-permute-done.14.other), custom_call_target="tpu_custom_call" | custom-call | flops 1 | bytes 1 | tf_op jit(solution)/shard_map/factor_inverse/pallas_call | solution.py:333
  160.7 10.3 %collective-permute-done.16.refs_2_ = bf16[512,512]{1,0:T(8,128)(2,1)S(1)} collective-permute-done((bf16[512,512]{1,0:T(8,128)(2,1)}, bf16[512,512]{1,0:T(8,128)(2,1)S(1)}, u32[]{:S(2)}, u32[]{:S(2)}) %collective-permute-start.16) | collective-permute-done | bytes 524320 | tf_op jit(solution)/shard_map/ppermute | solution.py:480
  171.0 3.8 %collective-permute-done.17.refs_3_ = bf16[512,512]{1,0:T(8,128)(2,1)S(1)} collective-permute-done((bf16[512,512]{1,0:T(8,128)(2,1)}, bf16[512,512]{1,0:T(8,128)(2,1)S(1)}, u32[]{:S(2)}, u32[]{:S(2)}) %collective-permute-start.17) | collective-permute-done | bytes 524320 | tf_op jit(solution)/shard_map/ppermute | solution.py:480
  174.8 6.1 %turned_basis.1.turned = bf16[512,2048]{1,0:T(8,128)(2,1)S(1)} custom-call(s32[8]{0:T(128)S(1)} %stack.55.place, f32[512,512]{1,0:T(8,128)S(1)} %factor_inverse.1.inverse, bf16[512,512]{1,0:T(8,128)(2,1)S(1)} %copy-done.23, bf16[512,512]{1,0:T(8,128)(2,1)S(1)} %collective-permute-done.15.refs_1_, bf16[512,512]{1,0:T(8,128)(2,1)S(1)} %collective-permute-done.16.refs_2_, ...), custom_call_target="tpu_custom_call" | custom-call | flops 2147483648 | bytes 4194304 | tf_op jit(solution)/shard_map/turned_basis/pallas_call | solution.py:385
  181.8 2.8 %project.7 = (bf16[256,512]{1,0:T(8,128)(2,1)S(1)}, f32[256,512]{1,0:T(8,128)S(1)}) custom-call(bf16[512,2048]{1,0:T(8,128)(2,1)S(1)} %turned_basis.1.turned, bf16[2048,8192]{1,0:T(8,128)(2,1)} %get-tuple-element.55.w), custom_call_target="tpu_custom_call" | custom-call | flops 21474836480 | bytes 2097152 | tf_op jit(solution)/shard_map/project/pallas_call | solution.py:410
  184.7 4.3 %project.8 = (bf16[256,1024]{1,0:T(8,128)(2,1)S(1)}, f32[256,1024]{1,0:T(8,128)S(1)}) custom-call(bf16[512,2048]{1,0:T(8,128)(2,1)S(1)} %turned_basis.1.turned, bf16[2048,8192]{1,0:T(8,128)(2,1)} %get-tuple-element.55.w, bf16[256,512]{1,0:T(8,128)(2,1)S(1)} %get-tuple-element.56.refs_0_), custom_call_target="tpu_custom_call" | custom-call | flops 42949672960 | bytes 4194304 | tf_op jit(solution)/shard_map/project/pallas_call | solution.py:410
  190.8 5.8 %project.9 = (bf16[256,1536]{1,0:T(8,128)(2,1)S(1)}, f32[256,1536]{1,0:T(8,128)S(1)}) custom-call(bf16[512,2048]{1,0:T(8,128)(2,1)S(1)} %turned_basis.1.turned, bf16[2048,8192]{1,0:T(8,128)(2,1)} %get-tuple-element.55.w, bf16[256,1024]{1,0:T(8,128)(2,1)S(1)} %get-tuple-element.57.refs_0_, bf16[128,512]{1,0:T(8,128)(2,1)S(1)} %add_convert_fusion.6.refs_1_), custom_call_target="tpu_custom_call" | custom-call | flops 64424509440 | bytes 6291456 | tf_op jit(solution)/shard_map/project/pallas_call | solution.py:410
  199.2 5.8 %project.10 = (bf16[256,1536]{1,0:T(8,128)(2,1)S(1)}, f32[256,1536]{1,0:T(8,128)S(1)}) custom-call(bf16[512,2048]{1,0:T(8,128)(2,1)S(1)} %turned_basis.1.turned, bf16[2048,8192]{1,0:T(8,128)(2,1)} %get-tuple-element.55.w, bf16[256,1536]{1,0:T(8,128)(2,1)S(1)} %get-tuple-element.59.refs_0_, bf16[128,1024]{1,0:T(8,128)(2,1)S(1)} %add_convert_fusion.4.refs_1_, ...), custom_call_target="tpu_custom_call" | custom-call | flops 64424509440 | bytes 6291456 | tf_op jit(solution)/shard_map/project/pallas_call | solution.py:410
  206.3 7.2 %project.11 = (bf16[256,2048]{1,0:T(8,128)(2,1)S(1)}, f32[256,2048]{1,0:T(8,128)S(1)}) custom-call(bf16[512,2048]{1,0:T(8,128)(2,1)S(1)} %turned_basis.1.turned, bf16[2048,8192]{1,0:T(8,128)(2,1)} %get-tuple-element.55.w, bf16[256,1536]{1,0:T(8,128)(2,1)S(1)} %get-tuple-element.61.refs_0_, bf16[128,1536]{1,0:T(8,128)(2,1)S(1)} %add_convert_fusion.2.refs_1_, ...), custom_call_target="tpu_custom_call" | custom-call | flops 85899345920 | bytes 8388608 | tf_op jit(solution)/shard_map/project/pallas_call | solution.py:410
  216.8 4.5 %project.12 = (bf16[256,1024]{1,0:T(8,128)(2,1)S(1)}, f32[256,1024]{1,0:T(8,128)S(1)}) custom-call(bf16[512,2048]{1,0:T(8,128)(2,1)S(1)} %turned_basis.1.turned, bf16[2048,8192]{1,0:T(8,128)(2,1)} %get-tuple-element.55.w, bf16[256,2048]{1,0:T(8,128)(2,1)S(1)} %get-tuple-element.63.refs_0_, bf16[128,1536]{1,0:T(8,128)(2,1)S(1)} %add_convert_fusion.1.refs_1_, ...), custom_call_target="tpu_custom_call" | custom-call | flops 42949672960 | bytes 4194304 | tf_op jit(solution)/shard_map/project/pallas_call | solution.py:410
  222.1 3.5 %collective-permute-done.26.refs_2_.chip_term = bf16[128,1536]{1,0:T(8,128)(2,1)S(1)} collective-permute-done((bf16[128,1536]{1,0:T(8,128)(2,1)S(1)}, bf16[128,1536]{1,0:T(8,128)(2,1)S(1)}, u32[]{:S(2)}, u32[]{:S(2)}) %collective-permute-start.26) | collective-permute-done | bytes 393248 | tf_op jit(solution)/shard_map/ppermute | solution.py:488
  225.7 2.8 %project.13 = (bf16[256,512]{1,0:T(8,128)(2,1)S(1)}, f32[256,512]{1,0:T(8,128)S(1)}) custom-call(bf16[512,2048]{1,0:T(8,128)(2,1)S(1)} %turned_basis.1.turned, bf16[2048,8192]{1,0:T(8,128)(2,1)} %get-tuple-element.55.w, bf16[256,1024]{1,0:T(8,128)(2,1)S(1)} %get-tuple-element.65.refs_0_, bf16[128,2048]{1,0:T(8,128)(2,1)S(1)} %add_convert_fusion.refs_1_, ...), custom_call_target="tpu_custom_call" | custom-call | flops 21474836480 | bytes 2097152 | tf_op jit(solution)/shard_map/project/pallas_call | solution.py:410
  235.0 2.8 %basis.1.refs_1_ = f32[512,512]{1,0:T(8,128)} custom-call(f32[512,512]{1,0:T(8,128)S(1)} %copy-done.2, f32[512,512]{1,0:T(8,128)S(1)} %copy-done.13, bf16[256,512]{1,0:T(8,128)(2,1)S(1)} %get-tuple-element.67.refs_0_), custom_call_target="tpu_custom_call" | custom-call | flops 1 | bytes 1 | tf_op jit(solution)/shard_map/basis/pallas_call | solution.py:356
  (136 shorter events, 40.0 us)
Async XLA Ops:
  28.9 3.7 %collective-permute-start = (f32[17,1,128]{2,1,0:T(1,128)S(1)}, f32[17,1,128]{2,1,0:T(1,128)S(1)}, u32[]{:S(2)}, u32[]{:S(2)}) collective-permute-start(f32[17,1,128]{2,1,0:T(1,128)S(1)} %get-tuple-element.41), channel_id=1, source_target_pairs={{0,1},{1,0},{2,3},{3,2},{4,5},{5,4},{6,7},{7,6},{8,9},{9,8},{10,11... | collective-permute-start | bytes 26120 | tf_op jit(solution)/shard_map/ppermute | solution.py:484
  32.5 4.6 %collective-permute-start.1 = (f32[17,1,128]{2,1,0:T(1,128)S(1)}, f32[17,1,128]{2,1,0:T(1,128)S(1)}, u32[]{:S(2)}, u32[]{:S(2)}) collective-permute-start(f32[17,1,128]{2,1,0:T(1,128)S(1)} %add.71), channel_id=1, source_target_pairs={{0,2},{1,3},{2,0},{3,1},{4,6},{5,7},{6,4},{7,5},{8,10},{9,11},{10,... | collective-permute-start | bytes 26120 | tf_op jit(solution)/shard_map/ppermute | solution.py:484
  56.4 12.9 %collective-permute-start.2 = (bf16[2,256,512]{2,1,0:T(8,128)(2,1)S(1)}, bf16[2,256,512]{2,1,0:T(8,128)(2,1)S(1)}, u32[]{:S(2)}, u32[]{:S(2)}) collective-permute-start(bf16[2,256,512]{2,1,0:T(8,128)(2,1)S(1)} %get-tuple-element.43), channel_id=1, source_target_pairs={{0,1},{1,0},{2,3},{3,2},{4,5},{5,4},{6,7},{7,6},{8,9},{9,8},{10,11... | collective-permute-start | bytes 1572872 | tf_op jit(solution)/shard_map/ppermute | solution.py:484
  66.0 18.4 %collective-permute-start.4 = (bf16[2,128,512]{2,1,0:T(8,128)(2,1)S(1)}, bf16[2,128,512]{2,1,0:T(8,128)(2,1)S(1)}, u32[]{:S(2)}, u32[]{:S(2)}) collective-permute-start(bf16[2,128,512]{2,1,0:T(8,128)(2,1)S(1)} %get-tuple-element.46), channel_id=1, source_target_pairs={{0,1},{1,0},{2,3},{3,2},{4,5},{5,4},{6,7},{7,6},{8,9},{9,8},{10,11... | collective-permute-start | bytes 786440 | tf_op jit(solution)/shard_map/ppermute | solution.py:484
  69.3 20.0 %collective-permute-start.3 = (bf16[256,512]{1,0:T(8,128)(2,1)S(1)}, bf16[256,512]{1,0:T(8,128)(2,1)S(1)}, u32[]{:S(2)}, u32[]{:S(2)}) collective-permute-start(bf16[256,512]{1,0:T(8,128)(2,1)S(1)} %fusion.refs_1_), channel_id=1, source_target_pairs={{0,2},{1,3},{2,0},{3,1},{4,6},{5,7},{6,4},{7,5},{8,10},{9,11},{10,... | collective-permute-start | bytes 786440 | tf_op jit(solution)/shard_map/ppermute | solution.py:484
  84.4 5.0 %collective-permute-start.7 = (bf16[128,512]{1,0:T(8,128)(2,1)S(1)}, bf16[128,512]{1,0:T(8,128)(2,1)S(1)}, u32[]{:S(2)}, u32[]{:S(2)}) collective-permute-start(bf16[128,512]{1,0:T(8,128)(2,1)S(1)} %get-tuple-element.50), channel_id=1, source_target_pairs={{0,1},{1,0},{2,3},{3,2},{4,5},{5,4},{6,7},{7,6},{8,9},{9,8},{10,11... | collective-permute-start | bytes 393224 | tf_op jit(solution)/shard_map/ppermute | solution.py:484
  84.5 8.2 %collective-permute-start.5 = (bf16[128,512]{1,0:T(8,128)(2,1)S(1)}, bf16[128,512]{1,0:T(8,128)(2,1)S(1)}, u32[]{:S(2)}, u32[]{:S(2)}) collective-permute-start(bf16[128,512]{1,0:T(8,128)(2,1)S(1)} %fusion.1), channel_id=1, source_target_pairs={{0,2},{1,3},{2,0},{3,1},{4,6},{5,7},{6,4},{7,5},{8,10},{9,11},{10,... | collective-permute-start | bytes 393224 | tf_op jit(solution)/shard_map/ppermute | solution.py:484
  84.6 8.1 %collective-permute-start.6 = (bf16[128,512]{1,0:T(8,128)(2,1)S(1)}, bf16[128,512]{1,0:T(8,128)(2,1)S(1)}, u32[]{:S(2)}, u32[]{:S(2)}) collective-permute-start(bf16[128,512]{1,0:T(8,128)(2,1)S(1)} %get-tuple-element.49), channel_id=1, source_target_pairs={{0,1},{1,0},{2,3},{3,2},{4,5},{5,4},{6,7},{7,6},{8,9},{9,8},{10,11... | collective-permute-start | bytes 393224 | tf_op jit(solution)/shard_map/ppermute | solution.py:484
  89.4 6.3 %collective-permute-start.8 = (bf16[128,512]{1,0:T(8,128)(2,1)S(1)}, bf16[128,512]{1,0:T(8,128)(2,1)S(1)}, u32[]{:S(2)}, u32[]{:S(2)}) collective-permute-start(bf16[128,512]{1,0:T(8,128)(2,1)S(1)} %pass_on.2), channel_id=1, source_target_pairs={{0,2},{1,3},{2,0},{3,1},{4,6},{5,7},{6,4},{7,5},{8,10},{9,11},{10,... | collective-permute-start | bytes 393224 | tf_op jit(solution)/shard_map/ppermute | solution.py:484
  101.0 1.9 collective-permute-start.9
  103.9 6.3 %collective-permute-start.10 = (f32[64,640]{1,0:T(8,128)S(1)}, f32[64,640]{1,0:T(8,128)S(1)}, u32[]{:S(2)}, u32[]{:S(2)}) collective-permute-start(f32[64,640]{1,0:T(8,128)S(1)} %constant_dynamic-slice_fusion), channel_id=1, source_target_pairs={{0,8},{4,12},{8,0},{12,4},{1,9},{5,13},{9,1},{13,5},{2,10},{6,14},... | collective-permute-start | bytes 491528 | tf_op jit(solution)/shard_map/ppermute | solution.py:488
  110.3 5.5 %collective-permute-start.11 = (f32[64,640]{1,0:T(8,128)S(1)}, f32[64,640]{1,0:T(8,128)S(1)}, u32[]{:S(2)}, u32[]{:S(2)}) collective-permute-start(f32[64,640]{1,0:T(8,128)S(1)} %dynamic-slice_add_fusion), channel_id=1, source_target_pairs={{0,1},{1,0},{2,3},{3,2},{4,5},{5,4},{6,7},{7,6},{8,9},{9,8},{10,11... | collective-permute-start | bytes 491528 | tf_op jit(solution)/shard_map/ppermute | solution.py:484
  115.8 8.8 %collective-permute-start.12 = (f32[64,640]{1,0:T(8,128)S(1)}, f32[64,640]{1,0:T(8,128)S(1)}, u32[]{:S(2)}, u32[]{:S(2)}) collective-permute-start(f32[64,640]{1,0:T(8,128)S(1)} %add.79), channel_id=1, source_target_pairs={{0,2},{1,3},{2,0},{3,1},{4,6},{5,7},{6,4},{7,5},{8,10},{9,11},{10,... | collective-permute-start | bytes 491528 | tf_op jit(solution)/shard_map/ppermute | solution.py:484
  124.6 6.9 %collective-permute-start.13 = (f32[64,640]{1,0:T(8,128)S(1)}, f32[64,640]{1,0:T(8,128)S(1)}, u32[]{:S(2)}, u32[]{:S(2)}) collective-permute-start(f32[64,640]{1,0:T(8,128)S(1)} %add.80), channel_id=1, source_target_pairs={{0,8},{4,12},{8,0},{12,4},{1,9},{5,13},{9,1},{13,5},{2,10},{6,14},... | collective-permute-start | bytes 491528 | tf_op jit(solution)/shard_map/ppermute | solution.py:488
  126.1 34.5 %collective-permute-start.15 = (bf16[512,512]{1,0:T(8,128)(2,1)}, bf16[512,512]{1,0:T(8,128)(2,1)S(1)}, u32[]{:S(2)}, u32[]{:S(2)}) collective-permute-start(bf16[512,512]{1,0:T(8,128)(2,1)} %get-tuple-element.54.refs_0_), channel_id=1, source_target_pairs={{0,1},{1,2},{2,3},{3,0},{4,5},{5,6},{6,7},{7,4},{8,9},{9,10},{10,1... | collective-permute-start | bytes 1572872 | tf_op jit(solution)/shard_map/ppermute | solution.py:480
  126.1 44.9 %collective-permute-start.16 = (bf16[512,512]{1,0:T(8,128)(2,1)}, bf16[512,512]{1,0:T(8,128)(2,1)S(1)}, u32[]{:S(2)}, u32[]{:S(2)}) collective-permute-start(bf16[512,512]{1,0:T(8,128)(2,1)} %get-tuple-element.54.refs_0_), channel_id=1, source_target_pairs={{0,2},{1,3},{2,0},{3,1},{4,6},{5,7},{6,4},{7,5},{8,10},{9,11},{10,... | collective-permute-start | bytes 1572872 | tf_op jit(solution)/shard_map/ppermute | solution.py:480
  129.8 45.0 %collective-permute-start.17 = (bf16[512,512]{1,0:T(8,128)(2,1)}, bf16[512,512]{1,0:T(8,128)(2,1)S(1)}, u32[]{:S(2)}, u32[]{:S(2)}) collective-permute-start(bf16[512,512]{1,0:T(8,128)(2,1)} %get-tuple-element.54.refs_0_), channel_id=1, source_target_pairs={{0,3},{1,0},{2,1},{3,2},{4,7},{5,4},{6,5},{7,6},{8,11},{9,8},{10,9... | collective-permute-start | bytes 1572872 | tf_op jit(solution)/shard_map/ppermute | solution.py:480
  131.6 1.7 collective-permute-start.14
  184.6 4.9 %collective-permute-start.18 = (bf16[256,512]{1,0:T(8,128)(2,1)S(1)}, bf16[256,512]{1,0:T(8,128)(2,1)S(1)}, u32[]{:S(2)}, u32[]{:S(2)}) collective-permute-start(bf16[256,512]{1,0:T(8,128)(2,1)S(1)} %get-tuple-element.56.refs_0_), channel_id=1, source_target_pairs={{0,4},{4,0},{8,12},{12,8},{1,5},{5,1},{9,13},{13,9},{2,6},{6,2},{1... | collective-permute-start | bytes 786440 | tf_op jit(solution)/shard_map/ppermute | solution.py:488
  189.0 7.7 %collective-permute-start.19 = (bf16[256,1024]{1,0:T(8,128)(2,1)S(1)}, bf16[256,1024]{1,0:T(8,128)(2,1)S(1)}, u32[]{:S(2)}, u32[]{:S(2)}) collective-permute-start(bf16[256,1024]{1,0:T(8,128)(2,1)S(1)} %get-tuple-element.57.refs_0_), channel_id=1, source_target_pairs={{0,4},{4,0},{8,12},{12,8},{1,5},{5,1},{9,13},{13,9},{2,6},{6,2},{1... | collective-permute-start | bytes 1572872 | tf_op jit(solution)/shard_map/ppermute | solution.py:488
  190.3 8.9 %collective-permute-start.20 = (bf16[128,512]{1,0:T(8,128)(2,1)S(1)}, bf16[128,512]{1,0:T(8,128)(2,1)S(1)}, u32[]{:S(2)}, u32[]{:S(2)}) collective-permute-start(bf16[128,512]{1,0:T(8,128)(2,1)S(1)} %add_convert_fusion.6.refs_1_), channel_id=1, source_target_pairs={{0,8},{4,12},{8,0},{12,4},{1,9},{5,13},{9,1},{13,5},{2,10},{6,14},... | collective-permute-start | bytes 393224 | tf_op jit(solution)/shard_map/ppermute | solution.py:488
  196.6 8.5 %collective-permute-start.21 = (bf16[256,1536]{1,0:T(8,128)(2,1)S(1)}, bf16[256,1536]{1,0:T(8,128)(2,1)S(1)}, u32[]{:S(2)}, u32[]{:S(2)}) collective-permute-start(bf16[256,1536]{1,0:T(8,128)(2,1)S(1)} %get-tuple-element.59.refs_0_), channel_id=1, source_target_pairs={{0,4},{4,0},{8,12},{12,8},{1,5},{5,1},{9,13},{13,9},{2,6},{6,2},{1... | collective-permute-start | bytes 2359304 | tf_op jit(solution)/shard_map/ppermute | solution.py:488
  197.7 8.6 %collective-permute-start.22 = (bf16[128,1024]{1,0:T(8,128)(2,1)S(1)}, bf16[128,1024]{1,0:T(8,128)(2,1)S(1)}, u32[]{:S(2)}, u32[]{:S(2)}) collective-permute-start(bf16[128,1024]{1,0:T(8,128)(2,1)S(1)} %add_convert_fusion.4.refs_1_), channel_id=1, source_target_pairs={{0,8},{4,12},{8,0},{12,4},{1,9},{5,13},{9,1},{13,5},{2,10},{6,14},... | collective-permute-start | bytes 786440 | tf_op jit(solution)/shard_map/ppermute | solution.py:488
  205.0 8.7 %collective-permute-start.23 = (bf16[256,1536]{1,0:T(8,128)(2,1)S(1)}, bf16[256,1536]{1,0:T(8,128)(2,1)S(1)}, u32[]{:S(2)}, u32[]{:S(2)}) collective-permute-start(bf16[256,1536]{1,0:T(8,128)(2,1)S(1)} %get-tuple-element.61.refs_0_), channel_id=1, source_target_pairs={{0,4},{4,0},{8,12},{12,8},{1,5},{5,1},{9,13},{13,9},{2,6},{6,2},{1... | collective-permute-start | bytes 2359304 | tf_op jit(solution)/shard_map/ppermute | solution.py:488
  205.2 11.5 %collective-permute-start.24 = (bf16[128,1536]{1,0:T(8,128)(2,1)S(1)}, bf16[128,1536]{1,0:T(8,128)(2,1)S(1)}, u32[]{:S(2)}, u32[]{:S(2)}) collective-permute-start(bf16[128,1536]{1,0:T(8,128)(2,1)S(1)} %add_convert_fusion.2.refs_1_), channel_id=1, source_target_pairs={{0,8},{4,12},{8,0},{12,4},{1,9},{5,13},{9,1},{13,5},{2,10},{6,14},... | collective-permute-start | bytes 1179656 | tf_op jit(solution)/shard_map/ppermute | solution.py:488
  213.4 7.9 %collective-permute-start.25 = (bf16[256,2048]{1,0:T(8,128)(2,1)S(1)}, bf16[256,2048]{1,0:T(8,128)(2,1)S(1)}, u32[]{:S(2)}, u32[]{:S(2)}) collective-permute-start(bf16[256,2048]{1,0:T(8,128)(2,1)S(1)} %get-tuple-element.63.refs_0_), channel_id=1, source_target_pairs={{0,4},{4,0},{8,12},{12,8},{1,5},{5,1},{9,13},{13,9},{2,6},{6,2},{1... | collective-permute-start | bytes 3145736 | tf_op jit(solution)/shard_map/ppermute | solution.py:488
  213.8 11.9 %collective-permute-start.26 = (bf16[128,1536]{1,0:T(8,128)(2,1)S(1)}, bf16[128,1536]{1,0:T(8,128)(2,1)S(1)}, u32[]{:S(2)}, u32[]{:S(2)}) collective-permute-start(bf16[128,1536]{1,0:T(8,128)(2,1)S(1)} %add_convert_fusion.1.refs_1_), channel_id=1, source_target_pairs={{0,8},{4,12},{8,0},{12,4},{1,9},{5,13},{9,1},{13,5},{2,10},{6,14},... | collective-permute-start | bytes 1179656 | tf_op jit(solution)/shard_map/ppermute | solution.py:488
  221.2 7.4 %collective-permute-start.30 = (bf16[256,1024]{1,0:T(8,128)(2,1)S(1)}, bf16[256,1024]{1,0:T(8,128)(2,1)S(1)}, u32[]{:S(2)}, u32[]{:S(2)}) collective-permute-start(bf16[256,1024]{1,0:T(8,128)(2,1)S(1)} %get-tuple-element.65.refs_0_), channel_id=1, source_target_pairs={{0,4},{4,0},{8,12},{12,8},{1,5},{5,1},{9,13},{13,9},{2,6},{6,2},{1... | collective-permute-start | bytes 1572872 | tf_op jit(solution)/shard_map/ppermute | solution.py:488
  221.5 16.4 %collective-permute-start.28 = (bf16[128,2048]{1,0:T(8,128)(2,1)S(1)}, bf16[128,2048]{1,0:T(8,128)(2,1)S(1)}, u32[]{:S(2)}, u32[]{:S(2)}) collective-permute-start(bf16[128,2048]{1,0:T(8,128)(2,1)S(1)} %add_convert_fusion.refs_1_), channel_id=1, source_target_pairs={{0,8},{4,12},{8,0},{12,4},{1,9},{5,13},{9,1},{13,5},{2,10},{6,14},... | collective-permute-start | bytes 1572872 | tf_op jit(solution)/shard_map/ppermute | solution.py:488
  228.5 9.3 %collective-permute-start.27 = (bf16[256,512]{1,0:T(8,128)(2,1)S(1)}, bf16[256,512]{1,0:T(8,128)(2,1)S(1)}, u32[]{:S(2)}, u32[]{:S(2)}) collective-permute-start(bf16[256,512]{1,0:T(8,128)(2,1)S(1)} %get-tuple-element.67.refs_0_), channel_id=1, source_target_pairs={{0,4},{4,0},{8,12},{12,8},{1,5},{5,1},{9,13},{13,9},{2,6},{6,2},{1... | collective-permute-start | bytes 786440 | tf_op jit(solution)/shard_map/ppermute | solution.py:488
  228.7 14.8 %collective-permute-start.31 = (bf16[128,1024]{1,0:T(8,128)(2,1)S(1)}, bf16[128,1024]{1,0:T(8,128)(2,1)S(1)}, u32[]{:S(2)}, u32[]{:S(2)}) collective-permute-start(bf16[128,1024]{1,0:T(8,128)(2,1)S(1)} %add_convert_fusion.3), channel_id=1, source_target_pairs={{0,8},{4,12},{8,0},{12,4},{1,9},{5,13},{9,1},{13,5},{2,10},{6,14},... | collective-permute-start | bytes 786440 | tf_op jit(solution)/shard_map/ppermute | solution.py:488
  239.1 6.0 %collective-permute-start.29 = (bf16[128,512]{1,0:T(8,128)(2,1)S(1)}, bf16[128,512]{1,0:T(8,128)(2,1)S(1)}, u32[]{:S(2)}, u32[]{:S(2)}) collective-permute-start(bf16[128,512]{1,0:T(8,128)(2,1)S(1)} %pass_on.3), channel_id=1, source_target_pairs={{0,8},{4,12},{8,0},{12,4},{1,9},{5,13},{9,1},{13,5},{2,10},{6,14},... | collective-permute-start | bytes 393224 | tf_op jit(solution)/shard_map/ppermute | solution.py:488
  (31 other events, 286.0 us)

commit v2 on v1

--- a/solution.py
+++ b/solution.py
@@ -365,33 +365,47 @@
     )(inverse, sketch, *tokens)
 
 
-def turned_body(place, inverse, *refs):
-    shares, turned = refs[:-1], refs[-1]
-    rows, size = shares[0].shape
+def turned_body(n, place, inverse, *refs):
+    shares, (turned, high, low) = refs[:n], refs[-3:]
+    size = inverse.shape[0]
     quarter = size // 4
-    for i in range(4):
-        take = inverse[pl.ds(pl.multiple_of(place[i] * quarter, quarter), quarter), :]
-        high = take.astype(BF16)
-        low = (take - high.astype(F32)).astype(BF16)
-        for d, share in enumerate(shares):
-            value = dot(high, share[...], COLS) + dot(low, share[...], COLS)
-            start = pl.multiple_of(place[4 + d] * rows, rows)
-            turned[i * quarter : (i + 1) * quarter, pl.ds(start, rows)] = value.astype(BF16)
-
-
-def turned_basis(place, inverse, shares):
+    step = pl.program_id(0)
+
+    @pl.when(step == 0)
+    def _():
+        for i in range(4):
+            rows = slice(i * quarter, (i + 1) * quarter)
+            take = inverse[pl.ds(pl.multiple_of(place[i] * quarter, quarter), quarter), :]
+            high[rows, :] = take.astype(BF16)
+            low[rows, :] = (take - take.astype(BF16).astype(F32)).astype(BF16)
+
+    for d in range(n):
+
+        @pl.when(step == d)
+        def _(d=d):
+            value = dot(high[...], shares[d][...], COLS) + dot(low[...], shares[d][...], COLS)
+            turned[...] = value.astype(BF16)
+
+
+def turned_basis(place, inverse, shares, held, first, n_all):
     rows, size = shares[0].shape
     n = len(shares)
-    return pl.pallas_call(
-        turned_body,
-        grid=(1,),
-        in_specs=[SMEM, whole(size, size)] + [whole(rows, size)] * n,
-        out_specs=whole(size, n * rows),
-        out_shape=jax.ShapeDtypeStruct((size, n * rows), BF16),
+    held = [] if held is None else [held]
+    return pl.pallas_call(
+        functools.partial(turned_body, n),
+        grid_spec=pltpu.PrefetchScalarGridSpec(
+            num_scalar_prefetch=1,
+            grid=(n,),
+            in_specs=[whole(size, size)] + [whole(rows, size)] * n + [ANY] * len(held),
+            out_specs=pl.BlockSpec((size, rows), lambda g, p: (0, p[4 + first + g])),
+            scratch_shapes=[pltpu.VMEM((size, size), BF16)] * 2,
+        ),
+        out_shape=jax.ShapeDtypeStruct((size, n_all * rows), BF16),
+        input_output_aliases={2 + n: 0} if held else {},
         name="turned_basis",
         cost_estimate=cost(4 * n * rows * size * size, 4 * n * rows * size),
         compiler_params=limit(24),
-    )(place, inverse, *shares)
+    )(place, inverse, *shares, *held)
 
 
 def project_body(turned, w, *refs):
@@ -422,7 +436,7 @@
         ],
         name="project",
         cost_estimate=cost(40 * rows * size * width, 2 * rows * width),
-        compiler_params=limit(40),
+        compiler_params=limit(34),
     )(turned, w, *tokens)
 
 
@@ -558,7 +572,7 @@
     if direct:
         quarter = quarter + swap_col(quarter, 1)
         quarter = quarter + swap_col(quarter, 2)
-        shares = [sketch_b] + [rotate(sketch_b, n, d) for d in range(1, n)]
+        shares = [sketch_b] + [rotate(sketch_b, n, d) for d in (1, 2, 3)]
         sources = [(col - d) % n for d in range(n)]
     else:
         quarter = lax.psum(quarter, "col")
@@ -567,7 +581,11 @@
     half = stack_by(chip, quarter, swap(quarter, 2))
     inverse = factor_inverse(core.reshape(1), half, swap(half, 1))
     place = jnp.stack([row ^ 3, row ^ 1, row ^ 2, row] + sources)
-    turned = turned_basis(place, inverse, shares)
+    n_share = len(shares)
+    first = (n_share + 1) // 2
+    turned = turned_basis(place, inverse, shares[:first], None, 0, n_share)
+    if n_share > 1:
+        turned = turned_basis(place, inverse, shares[first:], turned, first, n_share)
     widths = (1, 2, 3, 3, 4, 2, 1) if width % (16 * NB) == 0 else (1,) * 8
     unit = width // sum(widths)
     scale = float(1.0 / (rows * lax.axis_size("row")) ** 0.5)

time: 248 us -> 242 us (0.976)
    pallas_call x1 -> x2, Pallas kernels: 6.06 us -> 4.37 us  [turned_basis(): pl.pallas_call(functools.partial(turned_body, n), grid_spec=pltpu.Prefetc...]
  transfers between devices with their start and end apart: 32 -> 32, of which waited for: 15 -> 15; matrix products, arithmetic and copies ran while one was open for 0% -> 0% of each run, Pallas kernels for 36% -> 38%
where the time goes in v2:
time: 242 us; the launch traced here: 241 us
  Pallas kernels  146 us (60%)
  waiting for transfers between devices  49.2 us (20%)
  starting transfers between devices  35.5 us (15%)
  local copies, waits for them, and re-layouts  7.49 us (3%)
    pallas_call x3, Pallas kernels, weigh(): pl.pallas_call(functools.partial(weigh_body, split), grid_spec=pltpu.Pref...  35.1 us
    pallas_call x7, Pallas kernels, project(): pl.pallas_call(project_body, grid=(steps,), in_specs=[pl.BlockSpec((size,...  33 us
    pallas_call x1, Pallas kernels, row_sums(): pl.pallas_call(totals_body, grid=(rows // tile,), in_specs=[pl.BlockSpec(...  27.5 us
    pallas_call x1, Pallas kernels, factor_inverse(): pl.pallas_call(factor_body, grid=(1,), in_specs=[SMEM, whole(*mine.shape)...  27.3 us
    ppermute x11, waiting for transfers between devices, swap_col(): return lax.ppermute(x, 'col', [(i, i ^ bit) for i in range(4)])  23.3 us
    ppermute x11, starting transfers between devices, swap_col(): return lax.ppermute(x, 'col', [(i, i ^ bit) for i in range(4)])  19 us
    ppermute x18, waiting for transfers between devices, swap(): return lax.ppermute(x, 'row', [(i, i ^ bit) for i in range(4)])  13.9 us
    ppermute x3, waiting for transfers between devices, rotate(): return lax.ppermute(x, 'col', [(i, (i + by) % n) for i in range(n)])  12 us
  transfers between devices with their start and end apart: 32, of which 15 were waited for; matrix products, arithmetic and copies ran while one was open for 0% of the time, Pallas kernels for 38%

profile of v2, /device:TPU:8, one launch (start us, length us, event | category | flops | bytes accessed | tf_op | source)
XLA Modules:
  0.0 241.1 jit_solution(1833674231808451157)
XLA Ops:
  1.4 27.5 %row_sums.1 = (f32[17,1,128]{2,1,0:T(1,128)S(1)}, s8[2048,8192]{1,0:T(32,128)(4,1)}) custom-call(s32[2048,8192]{1,0:T(8,128)} %counts.1, s32[1,8192]{1,0:T(1,128)S(1)} %bitcast.20), custom_call_target="tpu_custom_call" | custom-call | flops 33554432000 | bytes 1 | tf_op jit(solution)/shard_map/row_sums/pallas_call | solution.py:68
  28.9 3.7 %collective-permute-done = f32[17,1,128]{2,1,0:T(1,128)S(1)} collective-permute-done((f32[17,1,128]{2,1,0:T(1,128)S(1)}, f32[17,1,128]{2,1,0:T(1,128)S(1)}, u32[]{:S(2)}, u32[]{:S(2)}) %collective-permute-start) | collective-permute-done | bytes 8736 | tf_op jit(solution)/shard_map/ppermute | solution.py:498
  32.5 2.7 %collective-permute-start.1 = (f32[17,1,128]{2,1,0:T(1,128)S(1)}, f32[17,1,128]{2,1,0:T(1,128)S(1)}, u32[]{:S(2)}, u32[]{:S(2)}) collective-permute-start(f32[17,1,128]{2,1,0:T(1,128)S(1)} %add.71), channel_id=1, source_target_pairs={{0,2},{1,3},{2,0},{3,1},{4,6},{5,7},{6,4},{7,5},{8,10},{9,11},{10,... | collective-permute-start | bytes 26120 | tf_op jit(solution)/shard_map/ppermute | solution.py:498
  37.2 3.4 %copy-done.23 = bf16[8192,512]{1,0:T(8,128)(2,1)S(1)} copy-done((bf16[8192,512]{1,0:T(8,128)(2,1)S(1)}, bf16[8192,512]{1,0:T(8,128)(2,1)}, u32[]{:S(2)}) %copy-start.23) | copy-done | bytes 8388632
  40.6 15.8 %weigh_and_sketch.3 = (bf16[2048,8192]{1,0:T(8,128)(2,1)}, f32[2,256,512]{2,1,0:T(8,128)S(1)}, bf16[2,256,512]{2,1,0:T(8,128)(2,1)S(1)}) custom-call(s32[4]{0:T(128)S(1)} %pad_add_fusion.order, s8[2048,8192]{1,0:T(32,128)(4,1)} %get-tuple-element.40.small, f32[17,1,128]{2,1,0:T(1,128)S(1)} %add.72.row_total.ctx_total, ...), custom_call_target="tpu_custom_call" | custom-call | flops 171798691840 | bytes 50331648 | tf_op jit(solution)/shard_map/weigh_and_sketch/pallas_call | solution.py:131
  56.4 9.6 %weigh_and_sketch.4 = (bf16[2048,8192]{1,0:T(8,128)(2,1)}, f32[2,128,512]{2,1,0:T(8,128)S(1)}, bf16[2,128,512]{2,1,0:T(8,128)(2,1)S(1)}) custom-call(s32[4]{0:T(128)S(1)} %pad_add_fusion.order, s8[2048,8192]{1,0:T(32,128)(4,1)} %get-tuple-element.40.small, f32[17,1,128]{2,1,0:T(1,128)S(1)} %add.72.row_total.ctx_total, ...), custom_call_target="tpu_custom_call", output_to_operand_aliasing={{0}: (6, {})} | custom-call | flops 85899345920 | bytes 25165824 | tf_op jit(solution)/shard_map/weigh_and_sketch/pallas_call | solution.py:131
  69.3 5.4 %collective-permute-start.3 = (bf16[256,512]{1,0:T(8,128)(2,1)S(1)}, bf16[256,512]{1,0:T(8,128)(2,1)S(1)}, u32[]{:S(2)}, u32[]{:S(2)}) collective-permute-start(bf16[256,512]{1,0:T(8,128)(2,1)S(1)} %fusion.refs_1_), channel_id=1, source_target_pairs={{0,2},{1,3},{2,0},{3,1},{4,6},{5,7},{6,4},{7,5},{8,10},{9,11},{10,... | collective-permute-start | bytes 786440 | tf_op jit(solution)/shard_map/ppermute | solution.py:498
  74.8 9.6 %weigh_and_sketch.5 = (bf16[2048,8192]{1,0:T(8,128)(2,1)}, f32[2,128,512]{2,1,0:T(8,128)S(1)}, bf16[128,512]{1,0:T(8,128)(2,1)S(1)}, bf16[128,512]{1,0:T(8,128)(2,1)S(1)}) custom-call(s32[4]{0:T(128)S(1)} %pad_add_fusion.order, s8[2048,8192]{1,0:T(32,128)(4,1)} %get-tuple-element.40.small, ...), custom_call_target="tpu_custom_call", output_to_operand_aliasing={{0}: (6, {})} | custom-call | flops 85899345920 | bytes 25165824 | tf_op jit(solution)/shard_map/weigh_and_sketch/pallas_call | solution.py:131
  84.6 2.1 collective-permute-start.6
  86.6 2.8 %collective-permute-done.7.core_term = bf16[128,512]{1,0:T(8,128)(2,1)S(1)} collective-permute-done((bf16[128,512]{1,0:T(8,128)(2,1)S(1)}, bf16[128,512]{1,0:T(8,128)(2,1)S(1)}, u32[]{:S(2)}, u32[]{:S(2)}) %collective-permute-start.7) | collective-permute-done | bytes 131104 | tf_op jit(solution)/shard_map/ppermute | solution.py:498
  89.4 3.3 %collective-permute-start.8 = (bf16[128,512]{1,0:T(8,128)(2,1)S(1)}, bf16[128,512]{1,0:T(8,128)(2,1)S(1)}, u32[]{:S(2)}, u32[]{:S(2)}) collective-permute-start(bf16[128,512]{1,0:T(8,128)(2,1)S(1)} %pass_on.2), channel_id=1, source_target_pairs={{0,2},{1,3},{2,0},{3,1},{4,6},{5,7},{6,4},{7,5},{8,10},{9,11},{10,... | collective-permute-start | bytes 393224 | tf_op jit(solution)/shard_map/ppermute | solution.py:498
  92.7 3.0 %collective-permute-done.8.refs_8_ = bf16[128,512]{1,0:T(8,128)(2,1)S(1)} collective-permute-done((bf16[128,512]{1,0:T(8,128)(2,1)S(1)}, bf16[128,512]{1,0:T(8,128)(2,1)S(1)}, u32[]{:S(2)}, u32[]{:S(2)}) %collective-permute-start.8) | collective-permute-done | bytes 131104 | tf_op jit(solution)/shard_map/ppermute | solution.py:498
  96.4 4.6 %gram.1 = (f32[512,512]{1,0:T(8,128)}, bf16[512,512]{1,0:T(8,128)(2,1)}, f32[128,640]{1,0:T(8,128)}, f32[128,640]{1,0:T(8,128)}) custom-call(s32[1]{0:T(128)} %bitcast.core, f32[2,256,512]{2,1,0:T(8,128)} %copy-done.18, bf16[2,256,512]{2,1,0:T(8,128)(2,1)} %copy-done.26, bf16[256,512]{1,0:T(8,128)(2,1)} %copy-done.19, f32[2,128,512]{2,1,0:T(8,128)} %copy-done.22, ...), custom_call_target="tpu_custom_call" | custom-call | flops 1610612736 | bytes 2097152 | tf_op jit(solution)/shard_map/gram/pallas_call | solution.py:207
  105.4 4.9 %collective-permute-done.10 = f32[64,640]{1,0:T(8,128)S(1)} collective-permute-done((f32[64,640]{1,0:T(8,128)S(1)}, f32[64,640]{1,0:T(8,128)S(1)}, u32[]{:S(2)}, u32[]{:S(2)}) %collective-permute-start.10) | collective-permute-done | bytes 163872 | tf_op jit(solution)/shard_map/ppermute | solution.py:502
  110.4 5.3 %collective-permute-done.11 = f32[64,640]{1,0:T(8,128)S(1)} collective-permute-done((f32[64,640]{1,0:T(8,128)S(1)}, f32[64,640]{1,0:T(8,128)S(1)}, u32[]{:S(2)}, u32[]{:S(2)}) %collective-permute-start.11) | collective-permute-done | bytes 163872 | tf_op jit(solution)/shard_map/ppermute | solution.py:498
  115.8 3.3 %collective-permute-start.12 = (f32[64,640]{1,0:T(8,128)S(1)}, f32[64,640]{1,0:T(8,128)S(1)}, u32[]{:S(2)}, u32[]{:S(2)}) collective-permute-start(f32[64,640]{1,0:T(8,128)S(1)} %add.79), channel_id=1, source_target_pairs={{0,2},{1,3},{2,0},{3,1},{4,6},{5,7},{6,4},{7,5},{8,10},{9,11},{10,... | collective-permute-start | bytes 491528 | tf_op jit(solution)/shard_map/ppermute | solution.py:498
  119.1 5.5 %collective-permute-done.12 = f32[64,640]{1,0:T(8,128)S(1)} collective-permute-done((f32[64,640]{1,0:T(8,128)S(1)}, f32[64,640]{1,0:T(8,128)S(1)}, u32[]{:S(2)}, u32[]{:S(2)}) %collective-permute-start.12) | collective-permute-done | bytes 163872 | tf_op jit(solution)/shard_map/ppermute | solution.py:498
  126.1 3.7 %collective-permute-start.15 = (bf16[512,512]{1,0:T(8,128)(2,1)}, bf16[512,512]{1,0:T(8,128)(2,1)S(1)}, u32[]{:S(2)}, u32[]{:S(2)}) collective-permute-start(bf16[512,512]{1,0:T(8,128)(2,1)} %get-tuple-element.54.refs_0_), channel_id=1, source_target_pairs={{0,2},{1,3},{2,0},{3,1},{4,6},{5,7},{6,4},{7,5},{8,10},{9,11},{10,... | collective-permute-start | bytes 1572872 | tf_op jit(solution)/shard_map/ppermute | solution.py:494
  133.2 27.3 %factor_inverse.1.inverse = f32[512,512]{1,0:T(8,128)S(1)} custom-call(s32[1]{0:T(128)} %bitcast.core, f32[128,640]{1,0:T(8,128)S(1)} %maximum_select_fusion.mine, f32[128,640]{1,0:T(8,128)S(1)} %collective-permute-done.14.other), custom_call_target="tpu_custom_call" | custom-call | flops 1 | bytes 1 | tf_op jit(solution)/shard_map/factor_inverse/pallas_call | solution.py:333
  160.6 2.2 turned_basis.2.refs_2_
  162.8 8.2 %collective-permute-done.15.refs_0_ = bf16[512,512]{1,0:T(8,128)(2,1)S(1)} collective-permute-done((bf16[512,512]{1,0:T(8,128)(2,1)}, bf16[512,512]{1,0:T(8,128)(2,1)S(1)}, u32[]{:S(2)}, u32[]{:S(2)}) %collective-permute-start.15) | collective-permute-done | bytes 524320 | tf_op jit(solution)/shard_map/ppermute | solution.py:494
  171.0 3.8 %collective-permute-done.16.refs_1_ = bf16[512,512]{1,0:T(8,128)(2,1)S(1)} collective-permute-done((bf16[512,512]{1,0:T(8,128)(2,1)}, bf16[512,512]{1,0:T(8,128)(2,1)S(1)}, u32[]{:S(2)}, u32[]{:S(2)}) %collective-permute-start.16) | collective-permute-done | bytes 524320 | tf_op jit(solution)/shard_map/ppermute | solution.py:494
  174.7 2.2 turned_basis.3.turned
  177.0 2.8 %project.7 = (bf16[256,512]{1,0:T(8,128)(2,1)S(1)}, f32[256,512]{1,0:T(8,128)S(1)}) custom-call(bf16[512,2048]{1,0:T(8,128)(2,1)S(1)} %turned_basis.3.turned, bf16[2048,8192]{1,0:T(8,128)(2,1)} %get-tuple-element.55.w), custom_call_target="tpu_custom_call" | custom-call | flops 21474836480 | bytes 2097152 | tf_op jit(solution)/shard_map/project/pallas_call | solution.py:424
  179.9 4.4 %project.8 = (bf16[256,1024]{1,0:T(8,128)(2,1)S(1)}, f32[256,1024]{1,0:T(8,128)S(1)}) custom-call(bf16[512,2048]{1,0:T(8,128)(2,1)S(1)} %turned_basis.3.turned, bf16[2048,8192]{1,0:T(8,128)(2,1)} %get-tuple-element.55.w, bf16[256,512]{1,0:T(8,128)(2,1)S(1)} %get-tuple-element.56.refs_0_), custom_call_target="tpu_custom_call" | custom-call | flops 42949672960 | bytes 4194304 | tf_op jit(solution)/shard_map/project/pallas_call | solution.py:424
  186.0 5.8 %project.9 = (bf16[256,1536]{1,0:T(8,128)(2,1)S(1)}, f32[256,1536]{1,0:T(8,128)S(1)}) custom-call(bf16[512,2048]{1,0:T(8,128)(2,1)S(1)} %turned_basis.3.turned, bf16[2048,8192]{1,0:T(8,128)(2,1)} %get-tuple-element.55.w, bf16[256,1024]{1,0:T(8,128)(2,1)S(1)} %get-tuple-element.57.refs_0_, bf16[128,512]{1,0:T(8,128)(2,1)S(1)} %add_convert_fusion.6.refs_1_), custom_call_target="tpu_custom_call" | custom-call | flops 64424509440 | bytes 6291456 | tf_op jit(solution)/shard_map/project/pallas_call | solution.py:424
  193.5 5.8 %project.10 = (bf16[256,1536]{1,0:T(8,128)(2,1)S(1)}, f32[256,1536]{1,0:T(8,128)S(1)}) custom-call(bf16[512,2048]{1,0:T(8,128)(2,1)S(1)} %turned_basis.3.turned, bf16[2048,8192]{1,0:T(8,128)(2,1)} %get-tuple-element.55.w, bf16[256,1536]{1,0:T(8,128)(2,1)S(1)} %get-tuple-element.59.refs_0_, bf16[128,1024]{1,0:T(8,128)(2,1)S(1)} %add_convert_fusion.4.refs_1_, ...), custom_call_target="tpu_custom_call" | custom-call | flops 64424509440 | bytes 6291456 | tf_op jit(solution)/shard_map/project/pallas_call | solution.py:424
  200.7 7.2 %project.11 = (bf16[256,2048]{1,0:T(8,128)(2,1)S(1)}, f32[256,2048]{1,0:T(8,128)S(1)}) custom-call(bf16[512,2048]{1,0:T(8,128)(2,1)S(1)} %turned_basis.3.turned, bf16[2048,8192]{1,0:T(8,128)(2,1)} %get-tuple-element.55.w, bf16[256,1536]{1,0:T(8,128)(2,1)S(1)} %get-tuple-element.61.refs_0_, bf16[128,1536]{1,0:T(8,128)(2,1)S(1)} %add_convert_fusion.2.refs_1_, ...), custom_call_target="tpu_custom_call" | custom-call | flops 85899345920 | bytes 8388608 | tf_op jit(solution)/shard_map/project/pallas_call | solution.py:424
  211.1 4.2 %project.12 = (bf16[256,1024]{1,0:T(8,128)(2,1)S(1)}, f32[256,1024]{1,0:T(8,128)S(1)}) custom-call(bf16[512,2048]{1,0:T(8,128)(2,1)S(1)} %turned_basis.3.turned, bf16[2048,8192]{1,0:T(8,128)(2,1)} %get-tuple-element.55.w, bf16[256,2048]{1,0:T(8,128)(2,1)S(1)} %get-tuple-element.63.refs_0_, bf16[128,1536]{1,0:T(8,128)(2,1)S(1)} %add_convert_fusion.1.refs_1_, ...), custom_call_target="tpu_custom_call" | custom-call | flops 42949672960 | bytes 4194304 | tf_op jit(solution)/shard_map/project/pallas_call | solution.py:424
  216.2 3.8 %collective-permute-done.26.refs_2_.chip_term = bf16[128,1536]{1,0:T(8,128)(2,1)S(1)} collective-permute-done((bf16[128,1536]{1,0:T(8,128)(2,1)S(1)}, bf16[128,1536]{1,0:T(8,128)(2,1)S(1)}, u32[]{:S(2)}, u32[]{:S(2)}) %collective-permute-start.26) | collective-permute-done | bytes 393248 | tf_op jit(solution)/shard_map/ppermute | solution.py:502
  220.0 2.8 %project.13 = (bf16[256,512]{1,0:T(8,128)(2,1)S(1)}, f32[256,512]{1,0:T(8,128)S(1)}) custom-call(bf16[512,2048]{1,0:T(8,128)(2,1)S(1)} %turned_basis.3.turned, bf16[2048,8192]{1,0:T(8,128)(2,1)} %get-tuple-element.55.w, bf16[256,1024]{1,0:T(8,128)(2,1)S(1)} %get-tuple-element.65.refs_0_, bf16[128,2048]{1,0:T(8,128)(2,1)S(1)} %add_convert_fusion.refs_1_, ...), custom_call_target="tpu_custom_call" | custom-call | flops 21474836480 | bytes 2097152 | tf_op jit(solution)/shard_map/project/pallas_call | solution.py:424
  229.5 2.8 %basis.1.refs_1_ = f32[512,512]{1,0:T(8,128)} custom-call(f32[512,512]{1,0:T(8,128)S(1)} %copy-done.1, f32[512,512]{1,0:T(8,128)S(1)} %copy-done.13, bf16[256,512]{1,0:T(8,128)(2,1)S(1)} %get-tuple-element.67.refs_0_), custom_call_target="tpu_custom_call" | custom-call | flops 1 | bytes 1 | tf_op jit(solution)/shard_map/basis/pallas_call | solution.py:356
  (137 shorter events, 40.1 us)
Async XLA Ops:
  28.9 3.7 %collective-permute-start = (f32[17,1,128]{2,1,0:T(1,128)S(1)}, f32[17,1,128]{2,1,0:T(1,128)S(1)}, u32[]{:S(2)}, u32[]{:S(2)}) collective-permute-start(f32[17,1,128]{2,1,0:T(1,128)S(1)} %get-tuple-element.41), channel_id=1, source_target_pairs={{0,1},{1,0},{2,3},{3,2},{4,5},{5,4},{6,7},{7,6},{8,9},{9,8},{10,11... | collective-permute-start | bytes 26120 | tf_op jit(solution)/shard_map/ppermute | solution.py:498
  32.5 4.6 %collective-permute-start.1 = (f32[17,1,128]{2,1,0:T(1,128)S(1)}, f32[17,1,128]{2,1,0:T(1,128)S(1)}, u32[]{:S(2)}, u32[]{:S(2)}) collective-permute-start(f32[17,1,128]{2,1,0:T(1,128)S(1)} %add.71), channel_id=1, source_target_pairs={{0,2},{1,3},{2,0},{3,1},{4,6},{5,7},{6,4},{7,5},{8,10},{9,11},{10,... | collective-permute-start | bytes 26120 | tf_op jit(solution)/shard_map/ppermute | solution.py:498
  56.4 12.9 %collective-permute-start.2 = (bf16[2,256,512]{2,1,0:T(8,128)(2,1)S(1)}, bf16[2,256,512]{2,1,0:T(8,128)(2,1)S(1)}, u32[]{:S(2)}, u32[]{:S(2)}) collective-permute-start(bf16[2,256,512]{2,1,0:T(8,128)(2,1)S(1)} %get-tuple-element.43), channel_id=1, source_target_pairs={{0,1},{1,0},{2,3},{3,2},{4,5},{5,4},{6,7},{7,6},{8,9},{9,8},{10,11... | collective-permute-start | bytes 1572872 | tf_op jit(solution)/shard_map/ppermute | solution.py:498
  66.0 18.4 %collective-permute-start.4 = (bf16[2,128,512]{2,1,0:T(8,128)(2,1)S(1)}, bf16[2,128,512]{2,1,0:T(8,128)(2,1)S(1)}, u32[]{:S(2)}, u32[]{:S(2)}) collective-permute-start(bf16[2,128,512]{2,1,0:T(8,128)(2,1)S(1)} %get-tuple-element.46), channel_id=1, source_target_pairs={{0,1},{1,0},{2,3},{3,2},{4,5},{5,4},{6,7},{7,6},{8,9},{9,8},{10,11... | collective-permute-start | bytes 786440 | tf_op jit(solution)/shard_map/ppermute | solution.py:498
  69.3 20.0 %collective-permute-start.3 = (bf16[256,512]{1,0:T(8,128)(2,1)S(1)}, bf16[256,512]{1,0:T(8,128)(2,1)S(1)}, u32[]{:S(2)}, u32[]{:S(2)}) collective-permute-start(bf16[256,512]{1,0:T(8,128)(2,1)S(1)} %fusion.refs_1_), channel_id=1, source_target_pairs={{0,2},{1,3},{2,0},{3,1},{4,6},{5,7},{6,4},{7,5},{8,10},{9,11},{10,... | collective-permute-start | bytes 786440 | tf_op jit(solution)/shard_map/ppermute | solution.py:498
  84.4 5.0 %collective-permute-start.7 = (bf16[128,512]{1,0:T(8,128)(2,1)S(1)}, bf16[128,512]{1,0:T(8,128)(2,1)S(1)}, u32[]{:S(2)}, u32[]{:S(2)}) collective-permute-start(bf16[128,512]{1,0:T(8,128)(2,1)S(1)} %get-tuple-element.50), channel_id=1, source_target_pairs={{0,1},{1,0},{2,3},{3,2},{4,5},{5,4},{6,7},{7,6},{8,9},{9,8},{10,11... | collective-permute-start | bytes 393224 | tf_op jit(solution)/shard_map/ppermute | solution.py:498
  84.5 8.2 %collective-permute-start.5 = (bf16[128,512]{1,0:T(8,128)(2,1)S(1)}, bf16[128,512]{1,0:T(8,128)(2,1)S(1)}, u32[]{:S(2)}, u32[]{:S(2)}) collective-permute-start(bf16[128,512]{1,0:T(8,128)(2,1)S(1)} %fusion.1), channel_id=1, source_target_pairs={{0,2},{1,3},{2,0},{3,1},{4,6},{5,7},{6,4},{7,5},{8,10},{9,11},{10,... | collective-permute-start | bytes 393224 | tf_op jit(solution)/shard_map/ppermute | solution.py:498
  84.6 8.1 %collective-permute-start.6 = (bf16[128,512]{1,0:T(8,128)(2,1)S(1)}, bf16[128,512]{1,0:T(8,128)(2,1)S(1)}, u32[]{:S(2)}, u32[]{:S(2)}) collective-permute-start(bf16[128,512]{1,0:T(8,128)(2,1)S(1)} %get-tuple-element.49), channel_id=1, source_target_pairs={{0,1},{1,0},{2,3},{3,2},{4,5},{5,4},{6,7},{7,6},{8,9},{9,8},{10,11... | collective-permute-start | bytes 393224 | tf_op jit(solution)/shard_map/ppermute | solution.py:498
  89.4 6.3 %collective-permute-start.8 = (bf16[128,512]{1,0:T(8,128)(2,1)S(1)}, bf16[128,512]{1,0:T(8,128)(2,1)S(1)}, u32[]{:S(2)}, u32[]{:S(2)}) collective-permute-start(bf16[128,512]{1,0:T(8,128)(2,1)S(1)} %pass_on.2), channel_id=1, source_target_pairs={{0,2},{1,3},{2,0},{3,1},{4,6},{5,7},{6,4},{7,5},{8,10},{9,11},{10,... | collective-permute-start | bytes 393224 | tf_op jit(solution)/shard_map/ppermute | solution.py:498
  101.0 1.9 collective-permute-start.9
  103.9 6.3 %collective-permute-start.10 = (f32[64,640]{1,0:T(8,128)S(1)}, f32[64,640]{1,0:T(8,128)S(1)}, u32[]{:S(2)}, u32[]{:S(2)}) collective-permute-start(f32[64,640]{1,0:T(8,128)S(1)} %constant_dynamic-slice_fusion), channel_id=1, source_target_pairs={{0,8},{4,12},{8,0},{12,4},{1,9},{5,13},{9,1},{13,5},{2,10},{6,14},... | collective-permute-start | bytes 491528 | tf_op jit(solution)/shard_map/ppermute | solution.py:502
  110.3 5.5 %collective-permute-start.11 = (f32[64,640]{1,0:T(8,128)S(1)}, f32[64,640]{1,0:T(8,128)S(1)}, u32[]{:S(2)}, u32[]{:S(2)}) collective-permute-start(f32[64,640]{1,0:T(8,128)S(1)} %dynamic-slice_add_fusion), channel_id=1, source_target_pairs={{0,1},{1,0},{2,3},{3,2},{4,5},{5,4},{6,7},{7,6},{8,9},{9,8},{10,11... | collective-permute-start | bytes 491528 | tf_op jit(solution)/shard_map/ppermute | solution.py:498
  115.8 8.8 %collective-permute-start.12 = (f32[64,640]{1,0:T(8,128)S(1)}, f32[64,640]{1,0:T(8,128)S(1)}, u32[]{:S(2)}, u32[]{:S(2)}) collective-permute-start(f32[64,640]{1,0:T(8,128)S(1)} %add.79), channel_id=1, source_target_pairs={{0,2},{1,3},{2,0},{3,1},{4,6},{5,7},{6,4},{7,5},{8,10},{9,11},{10,... | collective-permute-start | bytes 491528 | tf_op jit(solution)/shard_map/ppermute | solution.py:498
  124.6 6.9 %collective-permute-start.13 = (f32[64,640]{1,0:T(8,128)S(1)}, f32[64,640]{1,0:T(8,128)S(1)}, u32[]{:S(2)}, u32[]{:S(2)}) collective-permute-start(f32[64,640]{1,0:T(8,128)S(1)} %add.80), channel_id=1, source_target_pairs={{0,8},{4,12},{8,0},{12,4},{1,9},{5,13},{9,1},{13,5},{2,10},{6,14},... | collective-permute-start | bytes 491528 | tf_op jit(solution)/shard_map/ppermute | solution.py:502
  126.1 34.5 %collective-permute-start.17 = (bf16[512,512]{1,0:T(8,128)(2,1)}, bf16[512,512]{1,0:T(8,128)(2,1)S(1)}, u32[]{:S(2)}, u32[]{:S(2)}) collective-permute-start(bf16[512,512]{1,0:T(8,128)(2,1)} %get-tuple-element.54.refs_0_), channel_id=1, source_target_pairs={{0,1},{1,2},{2,3},{3,0},{4,5},{5,6},{6,7},{7,4},{8,9},{9,10},{10,1... | collective-permute-start | bytes 1572872 | tf_op jit(solution)/shard_map/ppermute | solution.py:494
  126.1 44.9 %collective-permute-start.15 = (bf16[512,512]{1,0:T(8,128)(2,1)}, bf16[512,512]{1,0:T(8,128)(2,1)S(1)}, u32[]{:S(2)}, u32[]{:S(2)}) collective-permute-start(bf16[512,512]{1,0:T(8,128)(2,1)} %get-tuple-element.54.refs_0_), channel_id=1, source_target_pairs={{0,2},{1,3},{2,0},{3,1},{4,6},{5,7},{6,4},{7,5},{8,10},{9,11},{10,... | collective-permute-start | bytes 1572872 | tf_op jit(solution)/shard_map/ppermute | solution.py:494
  129.8 45.0 %collective-permute-start.16 = (bf16[512,512]{1,0:T(8,128)(2,1)}, bf16[512,512]{1,0:T(8,128)(2,1)S(1)}, u32[]{:S(2)}, u32[]{:S(2)}) collective-permute-start(bf16[512,512]{1,0:T(8,128)(2,1)} %get-tuple-element.54.refs_0_), channel_id=1, source_target_pairs={{0,3},{1,0},{2,1},{3,2},{4,7},{5,4},{6,5},{7,6},{8,11},{9,8},{10,9... | collective-permute-start | bytes 1572872 | tf_op jit(solution)/shard_map/ppermute | solution.py:494
  131.5 1.7 collective-permute-start.14
  179.8 4.9 %collective-permute-start.18 = (bf16[256,512]{1,0:T(8,128)(2,1)S(1)}, bf16[256,512]{1,0:T(8,128)(2,1)S(1)}, u32[]{:S(2)}, u32[]{:S(2)}) collective-permute-start(bf16[256,512]{1,0:T(8,128)(2,1)S(1)} %get-tuple-element.56.refs_0_), channel_id=1, source_target_pairs={{0,4},{4,0},{8,12},{12,8},{1,5},{5,1},{9,13},{13,9},{2,6},{6,2},{1... | collective-permute-start | bytes 786440 | tf_op jit(solution)/shard_map/ppermute | solution.py:502
  184.3 7.5 %collective-permute-start.19 = (bf16[256,1024]{1,0:T(8,128)(2,1)S(1)}, bf16[256,1024]{1,0:T(8,128)(2,1)S(1)}, u32[]{:S(2)}, u32[]{:S(2)}) collective-permute-start(bf16[256,1024]{1,0:T(8,128)(2,1)S(1)} %get-tuple-element.57.refs_0_), channel_id=1, source_target_pairs={{0,4},{4,0},{8,12},{12,8},{1,5},{5,1},{9,13},{13,9},{2,6},{6,2},{1... | collective-permute-start | bytes 1572872 | tf_op jit(solution)/shard_map/ppermute | solution.py:502
  185.4 8.1 %collective-permute-start.20 = (bf16[128,512]{1,0:T(8,128)(2,1)S(1)}, bf16[128,512]{1,0:T(8,128)(2,1)S(1)}, u32[]{:S(2)}, u32[]{:S(2)}) collective-permute-start(bf16[128,512]{1,0:T(8,128)(2,1)S(1)} %add_convert_fusion.6.refs_1_), channel_id=1, source_target_pairs={{0,8},{4,12},{8,0},{12,4},{1,9},{5,13},{9,1},{13,5},{2,10},{6,14},... | collective-permute-start | bytes 393224 | tf_op jit(solution)/shard_map/ppermute | solution.py:502
  191.8 7.8 %collective-permute-start.21 = (bf16[256,1536]{1,0:T(8,128)(2,1)S(1)}, bf16[256,1536]{1,0:T(8,128)(2,1)S(1)}, u32[]{:S(2)}, u32[]{:S(2)}) collective-permute-start(bf16[256,1536]{1,0:T(8,128)(2,1)S(1)} %get-tuple-element.59.refs_0_), channel_id=1, source_target_pairs={{0,4},{4,0},{8,12},{12,8},{1,5},{5,1},{9,13},{13,9},{2,6},{6,2},{1... | collective-permute-start | bytes 2359304 | tf_op jit(solution)/shard_map/ppermute | solution.py:502
  192.0 8.8 %collective-permute-start.22 = (bf16[128,1024]{1,0:T(8,128)(2,1)S(1)}, bf16[128,1024]{1,0:T(8,128)(2,1)S(1)}, u32[]{:S(2)}, u32[]{:S(2)}) collective-permute-start(bf16[128,1024]{1,0:T(8,128)(2,1)S(1)} %add_convert_fusion.4.refs_1_), channel_id=1, source_target_pairs={{0,8},{4,12},{8,0},{12,4},{1,9},{5,13},{9,1},{13,5},{2,10},{6,14},... | collective-permute-start | bytes 786440 | tf_op jit(solution)/shard_map/ppermute | solution.py:502
  199.3 8.6 %collective-permute-start.23 = (bf16[256,1536]{1,0:T(8,128)(2,1)S(1)}, bf16[256,1536]{1,0:T(8,128)(2,1)S(1)}, u32[]{:S(2)}, u32[]{:S(2)}) collective-permute-start(bf16[256,1536]{1,0:T(8,128)(2,1)S(1)} %get-tuple-element.61.refs_0_), channel_id=1, source_target_pairs={{0,4},{4,0},{8,12},{12,8},{1,5},{5,1},{9,13},{13,9},{2,6},{6,2},{1... | collective-permute-start | bytes 2359304 | tf_op jit(solution)/shard_map/ppermute | solution.py:502
  199.7 11.4 %collective-permute-start.24 = (bf16[128,1536]{1,0:T(8,128)(2,1)S(1)}, bf16[128,1536]{1,0:T(8,128)(2,1)S(1)}, u32[]{:S(2)}, u32[]{:S(2)}) collective-permute-start(bf16[128,1536]{1,0:T(8,128)(2,1)S(1)} %add_convert_fusion.2.refs_1_), channel_id=1, source_target_pairs={{0,8},{4,12},{8,0},{12,4},{1,9},{5,13},{9,1},{13,5},{2,10},{6,14},... | collective-permute-start | bytes 1179656 | tf_op jit(solution)/shard_map/ppermute | solution.py:502
  207.9 7.5 %collective-permute-start.25 = (bf16[256,2048]{1,0:T(8,128)(2,1)S(1)}, bf16[256,2048]{1,0:T(8,128)(2,1)S(1)}, u32[]{:S(2)}, u32[]{:S(2)}) collective-permute-start(bf16[256,2048]{1,0:T(8,128)(2,1)S(1)} %get-tuple-element.63.refs_0_), channel_id=1, source_target_pairs={{0,4},{4,0},{8,12},{12,8},{1,5},{5,1},{9,13},{13,9},{2,6},{6,2},{1... | collective-permute-start | bytes 3145736 | tf_op jit(solution)/shard_map/ppermute | solution.py:502
  208.1 12.0 %collective-permute-start.26 = (bf16[128,1536]{1,0:T(8,128)(2,1)S(1)}, bf16[128,1536]{1,0:T(8,128)(2,1)S(1)}, u32[]{:S(2)}, u32[]{:S(2)}) collective-permute-start(bf16[128,1536]{1,0:T(8,128)(2,1)S(1)} %add_convert_fusion.1.refs_1_), channel_id=1, source_target_pairs={{0,8},{4,12},{8,0},{12,4},{1,9},{5,13},{9,1},{13,5},{2,10},{6,14},... | collective-permute-start | bytes 1179656 | tf_op jit(solution)/shard_map/ppermute | solution.py:502
  215.3 7.7 %collective-permute-start.30 = (bf16[256,1024]{1,0:T(8,128)(2,1)S(1)}, bf16[256,1024]{1,0:T(8,128)(2,1)S(1)}, u32[]{:S(2)}, u32[]{:S(2)}) collective-permute-start(bf16[256,1024]{1,0:T(8,128)(2,1)S(1)} %get-tuple-element.65.refs_0_), channel_id=1, source_target_pairs={{0,4},{4,0},{8,12},{12,8},{1,5},{5,1},{9,13},{13,9},{2,6},{6,2},{1... | collective-permute-start | bytes 1572872 | tf_op jit(solution)/shard_map/ppermute | solution.py:502
  215.5 16.7 %collective-permute-start.28 = (bf16[128,2048]{1,0:T(8,128)(2,1)S(1)}, bf16[128,2048]{1,0:T(8,128)(2,1)S(1)}, u32[]{:S(2)}, u32[]{:S(2)}) collective-permute-start(bf16[128,2048]{1,0:T(8,128)(2,1)S(1)} %add_convert_fusion.refs_1_), channel_id=1, source_target_pairs={{0,8},{4,12},{8,0},{12,4},{1,9},{5,13},{9,1},{13,5},{2,10},{6,14},... | collective-permute-start | bytes 1572872 | tf_op jit(solution)/shard_map/ppermute | solution.py:502
  222.9 9.4 %collective-permute-start.27 = (bf16[256,512]{1,0:T(8,128)(2,1)S(1)}, bf16[256,512]{1,0:T(8,128)(2,1)S(1)}, u32[]{:S(2)}, u32[]{:S(2)}) collective-permute-start(bf16[256,512]{1,0:T(8,128)(2,1)S(1)} %get-tuple-element.67.refs_0_), channel_id=1, source_target_pairs={{0,4},{4,0},{8,12},{12,8},{1,5},{5,1},{9,13},{13,9},{2,6},{6,2},{1... | collective-permute-start | bytes 786440 | tf_op jit(solution)/shard_map/ppermute | solution.py:502
  223.0 14.8 %collective-permute-start.31 = (bf16[128,1024]{1,0:T(8,128)(2,1)S(1)}, bf16[128,1024]{1,0:T(8,128)(2,1)S(1)}, u32[]{:S(2)}, u32[]{:S(2)}) collective-permute-start(bf16[128,1024]{1,0:T(8,128)(2,1)S(1)} %add_convert_fusion.3), channel_id=1, source_target_pairs={{0,8},{4,12},{8,0},{12,4},{1,9},{5,13},{9,1},{13,5},{2,10},{6,14},... | collective-permute-start | bytes 786440 | tf_op jit(solution)/shard_map/ppermute | solution.py:502
  233.5 5.9 %collective-permute-start.29 = (bf16[128,512]{1,0:T(8,128)(2,1)S(1)}, bf16[128,512]{1,0:T(8,128)(2,1)S(1)}, u32[]{:S(2)}, u32[]{:S(2)}) collective-permute-start(bf16[128,512]{1,0:T(8,128)(2,1)S(1)} %pass_on.3), channel_id=1, source_target_pairs={{0,8},{4,12},{8,0},{12,4},{1,9},{5,13},{9,1},{13,5},{2,10},{6,14},... | collective-permute-start | bytes 393224 | tf_op jit(solution)/shard_map/ppermute | solution.py:502
  (31 other events, 302.5 us)

commit v3 on v2

--- a/solution.py
+++ b/solution.py
@@ -223,21 +223,17 @@
     )(core, *terms)
 
 
-def small_inverse(g):
+def small_factor(g):
     n = len(g)
     g = [list(r) for r in g]
     m = [[None] * n for _ in range(n)]
-    out = [[None] * n for _ in range(n)]
+    pairs = []
     for j in range(0, n, 2):
         k = j + 1
         a, b, c = g[j][j], g[k][j], g[k][k]
         over = 1.0 / (a * c - b * b)
         ca, cb, cc = a * over, b * over, c * over
-        ra, rb = lax.rsqrt(a), lax.rsqrt(ca)
-        for l in range(j):
-            out[j][l] = m[j][l] * ra
-            out[k][l] = (ca * m[k][l] - cb * m[j][l]) * rb
-        out[j][j], out[k][j], out[k][k] = ra, -cb * rb, ca * rb
+        pairs.append((a, ca, cb, cc))
         for i in range(k + 1, n):
             f = cc * g[i][j] - cb * g[i][k]
             h = ca * g[i][k] - cb * g[i][j]
@@ -246,7 +242,7 @@
             for l in range(j):
                 m[i][l] = m[i][l] - (f * m[j][l] + h * m[k][l])
             m[i][j], m[i][k] = -f, -h
-    return out
+    return m, pairs
 
 
 def total(terms):
@@ -269,9 +265,13 @@
         rows = [
             jnp.where(pivots, jnp.where(lane == k, 1.0, 0.0), spread(tiles[0][k : k + 1])) for k in range(8)
         ]
-        low = small_inverse(g)
-        y = [total([low[r][k] * rows[k] for k in range(r + 1)]) for r in range(8)]
-        z = [total([low[r][m] * y[r] for r in range(m, 8)]) for m in range(8)]
+        m, pairs = small_factor(g)
+        u = [total([rows[i]] + [m[i][l] * rows[l] for l in range(i // 2 * 2)]) for i in range(8)]
+        v, y = [], []
+        for j, (a, ca, cb, cc) in zip(range(0, 8, 2), pairs):
+            v += [cc * u[j] - cb * u[j + 1], ca * u[j + 1] - cb * u[j]]
+            y += [u[j] * lax.rsqrt(a), v[j + 1] * lax.rsqrt(ca)]
+        z = [total([v[l]] + [m[i][l] * v[i] for i in range(l // 2 * 2 + 2, 8)]) for l in range(8)]
         new = []
         for x in tiles[1:]:
             x = jnp.where(pivots, 0.0, x) - total([c * w for c, w in zip(columns(x), z)])
@@ -387,10 +387,10 @@
             turned[...] = value.astype(BF16)
 
 
-def turned_basis(place, inverse, shares, held, first, n_all):
+def turned_basis(place, inverse, shares, held, first, n_all, tokens):
     rows, size = shares[0].shape
     n = len(shares)
-    held = [] if held is None else [held]
+    held = ([] if held is None else [held]) + tokens
     return pl.pallas_call(
         functools.partial(turned_body, n),
         grid_spec=pltpu.PrefetchScalarGridSpec(
@@ -401,7 +401,7 @@
             scratch_shapes=[pltpu.VMEM((size, size), BF16)] * 2,
         ),
         out_shape=jax.ShapeDtypeStruct((size, n_all * rows), BF16),
-        input_output_aliases={2 + n: 0} if held else {},
+        input_output_aliases={2 + n: 0} if first else {},
         name="turned_basis",
         cost_estimate=cost(4 * n * rows * size * size, 4 * n * rows * size),
         compiler_params=limit(24),
@@ -583,9 +583,10 @@
     place = jnp.stack([row ^ 3, row ^ 1, row ^ 2, row] + sources)
     n_share = len(shares)
     first = (n_share + 1) // 2
-    turned = turned_basis(place, inverse, shares[:first], None, 0, n_share)
+    turned = turned_basis(place, inverse, shares[:first], None, 0, n_share, [])
+    basis = basis_of(inverse, sketch, [])
     if n_share > 1:
-        turned = turned_basis(place, inverse, shares[first:], turned, first, n_share)
+        turned = turned_basis(place, inverse, shares[first:], turned, first, n_share, [basis])
     widths = (1, 2, 3, 3, 4, 2, 1) if width % (16 * NB) == 0 else (1,) * 8
     unit = width // sum(widths)
     scale = float(1.0 / (rows * lax.axis_size("row")) ** 0.5)
@@ -606,10 +607,9 @@
         sent.append(send)
         core_term = swap(send, 1)
         if j == len(widths) - 1:
-            basis = basis_of(inverse, sketch, [send])
             for _ in range(3):
                 end([])
-            chip_send = pass_on(mine, core_term, [arrived[-2], basis, ended[-1][1]])
+            chip_send = pass_on(mine, core_term, [arrived[-2], ended[-1][1]])
         else:
             chip_send = (mine[:quarter] + core_term[:quarter].astype(F32)).astype(BF16)
         passed.append(chip_send)

time: 242 us -> 242 us (level)
    ppermute x3, waiting for transfers between devices: 12 us -> 7.28 us  [rotate(): return lax.ppermute(x, 'col', [(i, (i + by) % n) for i in range(n)])]
    ppermute x18, waiting for transfers between devices: 13.9 us -> 17.9 us  [swap(): return lax.ppermute(x, 'row', [(i, i ^ bit) for i in range(4)])]
    unnamed x62 -> x60, local copies, waits for them, and re-layouts: 7.38 us -> 5.55 us
  transfers between devices with their start and end apart: 32 -> 32, of which waited for: 15 -> 18; matrix products, arithmetic and copies ran while one was open for 0% -> 1% of each run, Pallas kernels for 38% -> 38%
where the time goes in v3:
time: 242 us; the launch traced here: 241 us
  Pallas kernels  146 us (60%)
  waiting for transfers between devices  47.1 us (19%)
  starting transfers between devices  37.8 us (16%)
  local copies, waits for them, and re-layouts  5.66 us (2%)
  other arithmetic  2.89 us (1%)
    pallas_call x3, Pallas kernels, weigh(): pl.pallas_call(functools.partial(weigh_body, split), grid_spec=pltpu.Pref...  35 us
    pallas_call x7, Pallas kernels, project(): pl.pallas_call(project_body, grid=(steps,), in_specs=[pl.BlockSpec((size,...  32.9 us
    pallas_call x1, Pallas kernels, factor_inverse(): pl.pallas_call(factor_body, grid=(1,), in_specs=[SMEM, whole(*mine.shape)...  27.9 us
    pallas_call x1, Pallas kernels, row_sums(): pl.pallas_call(totals_body, grid=(rows // tile,), in_specs=[pl.BlockSpec(...  27.5 us
    ppermute x11, waiting for transfers between devices, swap_col(): return lax.ppermute(x, 'col', [(i, i ^ bit) for i in range(4)])  21.9 us
    ppermute x11, starting transfers between devices, swap_col(): return lax.ppermute(x, 'col', [(i, i ^ bit) for i in range(4)])  20.5 us
    ppermute x18, waiting for transfers between devices, swap(): return lax.ppermute(x, 'row', [(i, i ^ bit) for i in range(4)])  17.9 us
    ppermute x18, starting transfers between devices, swap(): return lax.ppermute(x, 'row', [(i, i ^ bit) for i in range(4)])  12 us
  transfers between devices with their start and end apart: 32, of which 18 were waited for; matrix products, arithmetic and copies ran while one was open for 1% of the time, Pallas kernels for 38%

profile of v3, /device:TPU:8, one launch (start us, length us, event | category | flops | bytes accessed | tf_op | source)
XLA Modules:
  0.0 241.2 jit_solution(10608424579895600104)
XLA Ops:
  1.4 27.5 %row_sums.1 = (f32[17,1,128]{2,1,0:T(1,128)S(1)}, s8[2048,8192]{1,0:T(32,128)(4,1)}) custom-call(s32[2048,8192]{1,0:T(8,128)} %counts.1, s32[1,8192]{1,0:T(1,128)S(1)} %bitcast.20), custom_call_target="tpu_custom_call" | custom-call | flops 33554432000 | bytes 1 | tf_op jit(solution)/shard_map/row_sums/pallas_call | solution.py:68
  28.9 3.7 %collective-permute-done = f32[17,1,128]{2,1,0:T(1,128)S(1)} collective-permute-done((f32[17,1,128]{2,1,0:T(1,128)S(1)}, f32[17,1,128]{2,1,0:T(1,128)S(1)}, u32[]{:S(2)}, u32[]{:S(2)}) %collective-permute-start) | collective-permute-done | bytes 8736 | tf_op jit(solution)/shard_map/ppermute | solution.py:498
  32.5 2.7 %collective-permute-start.1 = (f32[17,1,128]{2,1,0:T(1,128)S(1)}, f32[17,1,128]{2,1,0:T(1,128)S(1)}, u32[]{:S(2)}, u32[]{:S(2)}) collective-permute-start(f32[17,1,128]{2,1,0:T(1,128)S(1)} %add.71), channel_id=1, source_target_pairs={{0,2},{1,3},{2,0},{3,1},{4,6},{5,7},{6,4},{7,5},{8,10},{9,11},{10,... | collective-permute-start | bytes 26120 | tf_op jit(solution)/shard_map/ppermute | solution.py:498
  37.2 3.4 %copy-done.21 = bf16[8192,512]{1,0:T(8,128)(2,1)S(1)} copy-done((bf16[8192,512]{1,0:T(8,128)(2,1)S(1)}, bf16[8192,512]{1,0:T(8,128)(2,1)}, u32[]{:S(2)}) %copy-start.21) | copy-done | bytes 8388632
  40.6 15.8 %weigh_and_sketch.3 = (bf16[2048,8192]{1,0:T(8,128)(2,1)}, f32[2,256,512]{2,1,0:T(8,128)S(1)}, bf16[2,256,512]{2,1,0:T(8,128)(2,1)S(1)}) custom-call(s32[4]{0:T(128)S(1)} %pad_add_fusion.order, s8[2048,8192]{1,0:T(32,128)(4,1)} %get-tuple-element.40.small, f32[17,1,128]{2,1,0:T(1,128)S(1)} %add.72.row_total.ctx_total, ...), custom_call_target="tpu_custom_call" | custom-call | flops 171798691840 | bytes 50331648 | tf_op jit(solution)/shard_map/weigh_and_sketch/pallas_call | solution.py:131
  56.4 9.6 %weigh_and_sketch.4 = (bf16[2048,8192]{1,0:T(8,128)(2,1)}, f32[2,128,512]{2,1,0:T(8,128)S(1)}, bf16[2,128,512]{2,1,0:T(8,128)(2,1)S(1)}) custom-call(s32[4]{0:T(128)S(1)} %pad_add_fusion.order, s8[2048,8192]{1,0:T(32,128)(4,1)} %get-tuple-element.40.small, f32[17,1,128]{2,1,0:T(1,128)S(1)} %add.72.row_total.ctx_total, ...), custom_call_target="tpu_custom_call", output_to_operand_aliasing={{0}: (6, {})} | custom-call | flops 85899345920 | bytes 25165824 | tf_op jit(solution)/shard_map/weigh_and_sketch/pallas_call | solution.py:131
  69.3 5.5 %collective-permute-start.3 = (bf16[256,512]{1,0:T(8,128)(2,1)S(1)}, bf16[256,512]{1,0:T(8,128)(2,1)S(1)}, u32[]{:S(2)}, u32[]{:S(2)}) collective-permute-start(bf16[256,512]{1,0:T(8,128)(2,1)S(1)} %fusion.refs_1_), channel_id=1, source_target_pairs={{0,2},{1,3},{2,0},{3,1},{4,6},{5,7},{6,4},{7,5},{8,10},{9,11},{10,... | collective-permute-start | bytes 786440 | tf_op jit(solution)/shard_map/ppermute | solution.py:498
  74.8 9.6 %weigh_and_sketch.5 = (bf16[2048,8192]{1,0:T(8,128)(2,1)}, f32[2,128,512]{2,1,0:T(8,128)S(1)}, bf16[128,512]{1,0:T(8,128)(2,1)S(1)}, bf16[128,512]{1,0:T(8,128)(2,1)S(1)}) custom-call(s32[4]{0:T(128)S(1)} %pad_add_fusion.order, s8[2048,8192]{1,0:T(32,128)(4,1)} %get-tuple-element.40.small, ...), custom_call_target="tpu_custom_call", output_to_operand_aliasing={{0}: (6, {})} | custom-call | flops 85899345920 | bytes 25165824 | tf_op jit(solution)/shard_map/weigh_and_sketch/pallas_call | solution.py:131
  86.6 2.8 %collective-permute-done.7.core_term = bf16[128,512]{1,0:T(8,128)(2,1)S(1)} collective-permute-done((bf16[128,512]{1,0:T(8,128)(2,1)S(1)}, bf16[128,512]{1,0:T(8,128)(2,1)S(1)}, u32[]{:S(2)}, u32[]{:S(2)}) %collective-permute-start.7) | collective-permute-done | bytes 131104 | tf_op jit(solution)/shard_map/ppermute | solution.py:498
  89.4 3.3 %collective-permute-start.8 = (bf16[128,512]{1,0:T(8,128)(2,1)S(1)}, bf16[128,512]{1,0:T(8,128)(2,1)S(1)}, u32[]{:S(2)}, u32[]{:S(2)}) collective-permute-start(bf16[128,512]{1,0:T(8,128)(2,1)S(1)} %pass_on.2), channel_id=1, source_target_pairs={{0,2},{1,3},{2,0},{3,1},{4,6},{5,7},{6,4},{7,5},{8,10},{9,11},{10,... | collective-permute-start | bytes 393224 | tf_op jit(solution)/shard_map/ppermute | solution.py:498
  92.7 3.0 %collective-permute-done.8.refs_8_ = bf16[128,512]{1,0:T(8,128)(2,1)S(1)} collective-permute-done((bf16[128,512]{1,0:T(8,128)(2,1)S(1)}, bf16[128,512]{1,0:T(8,128)(2,1)S(1)}, u32[]{:S(2)}, u32[]{:S(2)}) %collective-permute-start.8) | collective-permute-done | bytes 131104 | tf_op jit(solution)/shard_map/ppermute | solution.py:498
  96.4 4.5 %gram.1 = (f32[512,512]{1,0:T(8,128)}, bf16[512,512]{1,0:T(8,128)(2,1)}, f32[128,640]{1,0:T(8,128)}, f32[128,640]{1,0:T(8,128)}) custom-call(s32[1]{0:T(128)} %bitcast.core, f32[2,256,512]{2,1,0:T(8,128)} %copy-done.16, bf16[2,256,512]{2,1,0:T(8,128)(2,1)} %copy-done.25, bf16[256,512]{1,0:T(8,128)(2,1)} %copy-done.17, f32[2,128,512]{2,1,0:T(8,128)} %copy-done.20, ...), custom_call_target="tpu_custom_call" | custom-call | flops 1610612736 | bytes 2097152 | tf_op jit(solution)/shard_map/gram/pallas_call | solution.py:207
  105.3 4.9 %collective-permute-done.10 = f32[64,640]{1,0:T(8,128)S(1)} collective-permute-done((f32[64,640]{1,0:T(8,128)S(1)}, f32[64,640]{1,0:T(8,128)S(1)}, u32[]{:S(2)}, u32[]{:S(2)}) %collective-permute-start.10) | collective-permute-done | bytes 163872 | tf_op jit(solution)/shard_map/ppermute | solution.py:502
  111.8 3.9 %collective-permute-done.11 = f32[64,640]{1,0:T(8,128)S(1)} collective-permute-done((f32[64,640]{1,0:T(8,128)S(1)}, f32[64,640]{1,0:T(8,128)S(1)}, u32[]{:S(2)}, u32[]{:S(2)}) %collective-permute-start.11) | collective-permute-done | bytes 163872 | tf_op jit(solution)/shard_map/ppermute | solution.py:498
  115.8 3.3 %collective-permute-start.12 = (f32[64,640]{1,0:T(8,128)S(1)}, f32[64,640]{1,0:T(8,128)S(1)}, u32[]{:S(2)}, u32[]{:S(2)}) collective-permute-start(f32[64,640]{1,0:T(8,128)S(1)} %add.79), channel_id=1, source_target_pairs={{0,2},{1,3},{2,0},{3,1},{4,6},{5,7},{6,4},{7,5},{8,10},{9,11},{10,... | collective-permute-start | bytes 491528 | tf_op jit(solution)/shard_map/ppermute | solution.py:498
  119.0 5.5 %collective-permute-done.12 = f32[64,640]{1,0:T(8,128)S(1)} collective-permute-done((f32[64,640]{1,0:T(8,128)S(1)}, f32[64,640]{1,0:T(8,128)S(1)}, u32[]{:S(2)}, u32[]{:S(2)}) %collective-permute-start.12) | collective-permute-done | bytes 163872 | tf_op jit(solution)/shard_map/ppermute | solution.py:498
  126.1 3.7 %collective-permute-start.15 = (bf16[512,512]{1,0:T(8,128)(2,1)}, bf16[512,512]{1,0:T(8,128)(2,1)S(1)}, u32[]{:S(2)}, u32[]{:S(2)}) collective-permute-start(bf16[512,512]{1,0:T(8,128)(2,1)} %get-tuple-element.54.refs_0_), channel_id=1, source_target_pairs={{0,2},{1,3},{2,0},{3,1},{4,6},{5,7},{6,4},{7,5},{8,10},{9,11},{10,... | collective-permute-start | bytes 1572872 | tf_op jit(solution)/shard_map/ppermute | solution.py:494
  134.5 27.9 %factor_inverse.1.inverse = f32[512,512]{1,0:T(8,128)S(1)} custom-call(s32[1]{0:T(128)} %bitcast.core, f32[128,640]{1,0:T(8,128)S(1)} %maximum_select_fusion.mine, f32[128,640]{1,0:T(8,128)} %collective-permute-done.14.other), custom_call_target="tpu_custom_call" | custom-call | flops 1 | bytes 1 | tf_op jit(solution)/shard_map/factor_inverse/pallas_call | solution.py:333
  162.5 2.8 %basis.1.refs_3_ = f32[512,512]{1,0:T(8,128)} custom-call(f32[512,512]{1,0:T(8,128)S(1)} %factor_inverse.1.inverse, f32[512,512]{1,0:T(8,128)S(1)} %copy-done.11), custom_call_target="tpu_custom_call" | custom-call | flops 1 | bytes 1 | tf_op jit(solution)/shard_map/basis/pallas_call | solution.py:356
  165.3 2.2 turned_basis.2.refs_2_
  167.5 3.5 %collective-permute-done.15.refs_0_ = bf16[512,512]{1,0:T(8,128)(2,1)S(1)} collective-permute-done((bf16[512,512]{1,0:T(8,128)(2,1)}, bf16[512,512]{1,0:T(8,128)(2,1)S(1)}, u32[]{:S(2)}, u32[]{:S(2)}) %collective-permute-start.15) | collective-permute-done | bytes 524320 | tf_op jit(solution)/shard_map/ppermute | solution.py:494
  171.0 3.8 %collective-permute-done.16.refs_1_ = bf16[512,512]{1,0:T(8,128)(2,1)S(1)} collective-permute-done((bf16[512,512]{1,0:T(8,128)(2,1)}, bf16[512,512]{1,0:T(8,128)(2,1)S(1)}, u32[]{:S(2)}, u32[]{:S(2)}) %collective-permute-start.16) | collective-permute-done | bytes 524320 | tf_op jit(solution)/shard_map/ppermute | solution.py:494
  174.7 2.4 turned_basis.3.turned
  177.1 2.8 %project.7 = (bf16[256,512]{1,0:T(8,128)(2,1)S(1)}, f32[256,512]{1,0:T(8,128)S(1)}) custom-call(bf16[512,2048]{1,0:T(8,128)(2,1)S(1)} %turned_basis.3.turned, bf16[2048,8192]{1,0:T(8,128)(2,1)} %get-tuple-element.55.w), custom_call_target="tpu_custom_call" | custom-call | flops 21474836480 | bytes 2097152 | tf_op jit(solution)/shard_map/project/pallas_call | solution.py:424
  180.1 4.3 %project.8 = (bf16[256,1024]{1,0:T(8,128)(2,1)S(1)}, f32[256,1024]{1,0:T(8,128)S(1)}) custom-call(bf16[512,2048]{1,0:T(8,128)(2,1)S(1)} %turned_basis.3.turned, bf16[2048,8192]{1,0:T(8,128)(2,1)} %get-tuple-element.55.w, bf16[256,512]{1,0:T(8,128)(2,1)S(1)} %get-tuple-element.56.refs_0_), custom_call_target="tpu_custom_call" | custom-call | flops 42949672960 | bytes 4194304 | tf_op jit(solution)/shard_map/project/pallas_call | solution.py:424
  186.3 5.8 %project.9 = (bf16[256,1536]{1,0:T(8,128)(2,1)S(1)}, f32[256,1536]{1,0:T(8,128)S(1)}) custom-call(bf16[512,2048]{1,0:T(8,128)(2,1)S(1)} %turned_basis.3.turned, bf16[2048,8192]{1,0:T(8,128)(2,1)} %get-tuple-element.55.w, bf16[256,1024]{1,0:T(8,128)(2,1)S(1)} %get-tuple-element.57.refs_0_, bf16[128,512]{1,0:T(8,128)(2,1)S(1)} %add_convert_fusion.6.refs_1_), custom_call_target="tpu_custom_call" | custom-call | flops 64424509440 | bytes 6291456 | tf_op jit(solution)/shard_map/project/pallas_call | solution.py:424
  193.6 5.8 %project.10 = (bf16[256,1536]{1,0:T(8,128)(2,1)S(1)}, f32[256,1536]{1,0:T(8,128)S(1)}) custom-call(bf16[512,2048]{1,0:T(8,128)(2,1)S(1)} %turned_basis.3.turned, bf16[2048,8192]{1,0:T(8,128)(2,1)} %get-tuple-element.55.w, bf16[256,1536]{1,0:T(8,128)(2,1)S(1)} %get-tuple-element.59.refs_0_, bf16[128,1024]{1,0:T(8,128)(2,1)S(1)} %add_convert_fusion.4.refs_1_, ...), custom_call_target="tpu_custom_call" | custom-call | flops 64424509440 | bytes 6291456 | tf_op jit(solution)/shard_map/project/pallas_call | solution.py:424
  201.0 7.2 %project.11 = (bf16[256,2048]{1,0:T(8,128)(2,1)S(1)}, f32[256,2048]{1,0:T(8,128)S(1)}) custom-call(bf16[512,2048]{1,0:T(8,128)(2,1)S(1)} %turned_basis.3.turned, bf16[2048,8192]{1,0:T(8,128)(2,1)} %get-tuple-element.55.w, bf16[256,1536]{1,0:T(8,128)(2,1)S(1)} %get-tuple-element.61.refs_0_, bf16[128,1536]{1,0:T(8,128)(2,1)S(1)} %add_convert_fusion.2.refs_1_, ...), custom_call_target="tpu_custom_call" | custom-call | flops 85899345920 | bytes 8388608 | tf_op jit(solution)/shard_map/project/pallas_call | solution.py:424
  211.2 4.2 %project.12 = (bf16[256,1024]{1,0:T(8,128)(2,1)S(1)}, f32[256,1024]{1,0:T(8,128)S(1)}) custom-call(bf16[512,2048]{1,0:T(8,128)(2,1)S(1)} %turned_basis.3.turned, bf16[2048,8192]{1,0:T(8,128)(2,1)} %get-tuple-element.55.w, bf16[256,2048]{1,0:T(8,128)(2,1)S(1)} %get-tuple-element.63.refs_0_, bf16[128,1536]{1,0:T(8,128)(2,1)S(1)} %add_convert_fusion.1.refs_1_, ...), custom_call_target="tpu_custom_call" | custom-call | flops 42949672960 | bytes 4194304 | tf_op jit(solution)/shard_map/project/pallas_call | solution.py:424
  216.5 3.8 %collective-permute-done.26.refs_2_.chip_term = bf16[128,1536]{1,0:T(8,128)(2,1)S(1)} collective-permute-done((bf16[128,1536]{1,0:T(8,128)(2,1)S(1)}, bf16[128,1536]{1,0:T(8,128)(2,1)S(1)}, u32[]{:S(2)}, u32[]{:S(2)}) %collective-permute-start.26) | collective-permute-done | bytes 393248 | tf_op jit(solution)/shard_map/ppermute | solution.py:502
  220.3 2.8 %project.13 = (bf16[256,512]{1,0:T(8,128)(2,1)S(1)}, f32[256,512]{1,0:T(8,128)S(1)}) custom-call(bf16[512,2048]{1,0:T(8,128)(2,1)S(1)} %turned_basis.3.turned, bf16[2048,8192]{1,0:T(8,128)(2,1)} %get-tuple-element.55.w, bf16[256,1024]{1,0:T(8,128)(2,1)S(1)} %get-tuple-element.65.refs_0_, bf16[128,2048]{1,0:T(8,128)(2,1)S(1)} %add_convert_fusion.refs_1_, ...), custom_call_target="tpu_custom_call" | custom-call | flops 21474836480 | bytes 2097152 | tf_op jit(solution)/shard_map/project/pallas_call | solution.py:424
  229.0 2.5 %collective-permute-done.28.refs_0_.chip_term = bf16[128,2048]{1,0:T(8,128)(2,1)S(1)} collective-permute-done((bf16[128,2048]{1,0:T(8,128)(2,1)S(1)}, bf16[128,2048]{1,0:T(8,128)(2,1)S(1)}, u32[]{:S(2)}, u32[]{:S(2)}) %collective-permute-start.28) | collective-permute-done | bytes 524320 | tf_op jit(solution)/shard_map/ppermute | solution.py:502
  (135 shorter events, 45.3 us)
Async XLA Ops:
  28.9 3.7 %collective-permute-start = (f32[17,1,128]{2,1,0:T(1,128)S(1)}, f32[17,1,128]{2,1,0:T(1,128)S(1)}, u32[]{:S(2)}, u32[]{:S(2)}) collective-permute-start(f32[17,1,128]{2,1,0:T(1,128)S(1)} %get-tuple-element.41), channel_id=1, source_target_pairs={{0,1},{1,0},{2,3},{3,2},{4,5},{5,4},{6,7},{7,6},{8,9},{9,8},{10,11... | collective-permute-start | bytes 26120 | tf_op jit(solution)/shard_map/ppermute | solution.py:498
  32.5 4.6 %collective-permute-start.1 = (f32[17,1,128]{2,1,0:T(1,128)S(1)}, f32[17,1,128]{2,1,0:T(1,128)S(1)}, u32[]{:S(2)}, u32[]{:S(2)}) collective-permute-start(f32[17,1,128]{2,1,0:T(1,128)S(1)} %add.71), channel_id=1, source_target_pairs={{0,2},{1,3},{2,0},{3,1},{4,6},{5,7},{6,4},{7,5},{8,10},{9,11},{10,... | collective-permute-start | bytes 26120 | tf_op jit(solution)/shard_map/ppermute | solution.py:498
  56.4 12.9 %collective-permute-start.2 = (bf16[2,256,512]{2,1,0:T(8,128)(2,1)S(1)}, bf16[2,256,512]{2,1,0:T(8,128)(2,1)S(1)}, u32[]{:S(2)}, u32[]{:S(2)}) collective-permute-start(bf16[2,256,512]{2,1,0:T(8,128)(2,1)S(1)} %get-tuple-element.43), channel_id=1, source_target_pairs={{0,1},{1,0},{2,3},{3,2},{4,5},{5,4},{6,7},{7,6},{8,9},{9,8},{10,11... | collective-permute-start | bytes 1572872 | tf_op jit(solution)/shard_map/ppermute | solution.py:498
  66.0 18.4 %collective-permute-start.4 = (bf16[2,128,512]{2,1,0:T(8,128)(2,1)S(1)}, bf16[2,128,512]{2,1,0:T(8,128)(2,1)S(1)}, u32[]{:S(2)}, u32[]{:S(2)}) collective-permute-start(bf16[2,128,512]{2,1,0:T(8,128)(2,1)S(1)} %get-tuple-element.46), channel_id=1, source_target_pairs={{0,1},{1,0},{2,3},{3,2},{4,5},{5,4},{6,7},{7,6},{8,9},{9,8},{10,11... | collective-permute-start | bytes 786440 | tf_op jit(solution)/shard_map/ppermute | solution.py:498
  69.3 20.1 %collective-permute-start.3 = (bf16[256,512]{1,0:T(8,128)(2,1)S(1)}, bf16[256,512]{1,0:T(8,128)(2,1)S(1)}, u32[]{:S(2)}, u32[]{:S(2)}) collective-permute-start(bf16[256,512]{1,0:T(8,128)(2,1)S(1)} %fusion.refs_1_), channel_id=1, source_target_pairs={{0,2},{1,3},{2,0},{3,1},{4,6},{5,7},{6,4},{7,5},{8,10},{9,11},{10,... | collective-permute-start | bytes 786440 | tf_op jit(solution)/shard_map/ppermute | solution.py:498
  84.4 5.0 %collective-permute-start.7 = (bf16[128,512]{1,0:T(8,128)(2,1)S(1)}, bf16[128,512]{1,0:T(8,128)(2,1)S(1)}, u32[]{:S(2)}, u32[]{:S(2)}) collective-permute-start(bf16[128,512]{1,0:T(8,128)(2,1)S(1)} %get-tuple-element.50), channel_id=1, source_target_pairs={{0,1},{1,0},{2,3},{3,2},{4,5},{5,4},{6,7},{7,6},{8,9},{9,8},{10,11... | collective-permute-start | bytes 393224 | tf_op jit(solution)/shard_map/ppermute | solution.py:498
  84.5 8.2 %collective-permute-start.5 = (bf16[128,512]{1,0:T(8,128)(2,1)S(1)}, bf16[128,512]{1,0:T(8,128)(2,1)S(1)}, u32[]{:S(2)}, u32[]{:S(2)}) collective-permute-start(bf16[128,512]{1,0:T(8,128)(2,1)S(1)} %fusion.1), channel_id=1, source_target_pairs={{0,2},{1,3},{2,0},{3,1},{4,6},{5,7},{6,4},{7,5},{8,10},{9,11},{10,... | collective-permute-start | bytes 393224 | tf_op jit(solution)/shard_map/ppermute | solution.py:498
  84.6 8.1 %collective-permute-start.6 = (bf16[128,512]{1,0:T(8,128)(2,1)S(1)}, bf16[128,512]{1,0:T(8,128)(2,1)S(1)}, u32[]{:S(2)}, u32[]{:S(2)}) collective-permute-start(bf16[128,512]{1,0:T(8,128)(2,1)S(1)} %get-tuple-element.49), channel_id=1, source_target_pairs={{0,1},{1,0},{2,3},{3,2},{4,5},{5,4},{6,7},{7,6},{8,9},{9,8},{10,11... | collective-permute-start | bytes 393224 | tf_op jit(solution)/shard_map/ppermute | solution.py:498
  89.4 6.3 %collective-permute-start.8 = (bf16[128,512]{1,0:T(8,128)(2,1)S(1)}, bf16[128,512]{1,0:T(8,128)(2,1)S(1)}, u32[]{:S(2)}, u32[]{:S(2)}) collective-permute-start(bf16[128,512]{1,0:T(8,128)(2,1)S(1)} %pass_on.2), channel_id=1, source_target_pairs={{0,2},{1,3},{2,0},{3,1},{4,6},{5,7},{6,4},{7,5},{8,10},{9,11},{10,... | collective-permute-start | bytes 393224 | tf_op jit(solution)/shard_map/ppermute | solution.py:498
  100.9 1.9 collective-permute-start.9
  103.9 6.3 %collective-permute-start.10 = (f32[64,640]{1,0:T(8,128)S(1)}, f32[64,640]{1,0:T(8,128)S(1)}, u32[]{:S(2)}, u32[]{:S(2)}) collective-permute-start(f32[64,640]{1,0:T(8,128)S(1)} %constant_dynamic-slice_fusion), channel_id=1, source_target_pairs={{0,8},{4,12},{8,0},{12,4},{1,9},{5,13},{9,1},{13,5},{2,10},{6,14},... | collective-permute-start | bytes 491528 | tf_op jit(solution)/shard_map/ppermute | solution.py:502
  110.3 5.5 %collective-permute-start.11 = (f32[64,640]{1,0:T(8,128)S(1)}, f32[64,640]{1,0:T(8,128)S(1)}, u32[]{:S(2)}, u32[]{:S(2)}) collective-permute-start(f32[64,640]{1,0:T(8,128)S(1)} %dynamic-slice_add_fusion), channel_id=1, source_target_pairs={{0,1},{1,0},{2,3},{3,2},{4,5},{5,4},{6,7},{7,6},{8,9},{9,8},{10,11... | collective-permute-start | bytes 491528 | tf_op jit(solution)/shard_map/ppermute | solution.py:498
  115.8 8.8 %collective-permute-start.12 = (f32[64,640]{1,0:T(8,128)S(1)}, f32[64,640]{1,0:T(8,128)S(1)}, u32[]{:S(2)}, u32[]{:S(2)}) collective-permute-start(f32[64,640]{1,0:T(8,128)S(1)} %add.79), channel_id=1, source_target_pairs={{0,2},{1,3},{2,0},{3,1},{4,6},{5,7},{6,4},{7,5},{8,10},{9,11},{10,... | collective-permute-start | bytes 491528 | tf_op jit(solution)/shard_map/ppermute | solution.py:498
  124.6 6.9 %collective-permute-start.13 = (f32[64,640]{1,0:T(8,128)S(1)}, f32[64,640]{1,0:T(8,128)}, u32[]{:S(2)}, u32[]{:S(2)}) collective-permute-start(f32[64,640]{1,0:T(8,128)S(1)} %add.80), channel_id=1, source_target_pairs={{0,8},{4,12},{8,0},{12,4},{1,9},{5,13},{9,1},{13,5},{2,10},{6,14},... | collective-permute-start | bytes 491528 | tf_op jit(solution)/shard_map/ppermute | solution.py:502
  126.1 39.2 %collective-permute-start.17 = (bf16[512,512]{1,0:T(8,128)(2,1)}, bf16[512,512]{1,0:T(8,128)(2,1)S(1)}, u32[]{:S(2)}, u32[]{:S(2)}) collective-permute-start(bf16[512,512]{1,0:T(8,128)(2,1)} %get-tuple-element.54.refs_0_), channel_id=1, source_target_pairs={{0,1},{1,2},{2,3},{3,0},{4,5},{5,6},{6,7},{7,4},{8,9},{9,10},{10,1... | collective-permute-start | bytes 1572872 | tf_op jit(solution)/shard_map/ppermute | solution.py:494
  126.1 44.9 %collective-permute-start.15 = (bf16[512,512]{1,0:T(8,128)(2,1)}, bf16[512,512]{1,0:T(8,128)(2,1)S(1)}, u32[]{:S(2)}, u32[]{:S(2)}) collective-permute-start(bf16[512,512]{1,0:T(8,128)(2,1)} %get-tuple-element.54.refs_0_), channel_id=1, source_target_pairs={{0,2},{1,3},{2,0},{3,1},{4,6},{5,7},{6,4},{7,5},{8,10},{9,11},{10,... | collective-permute-start | bytes 1572872 | tf_op jit(solution)/shard_map/ppermute | solution.py:494
  129.8 45.0 %collective-permute-start.16 = (bf16[512,512]{1,0:T(8,128)(2,1)}, bf16[512,512]{1,0:T(8,128)(2,1)S(1)}, u32[]{:S(2)}, u32[]{:S(2)}) collective-permute-start(bf16[512,512]{1,0:T(8,128)(2,1)} %get-tuple-element.54.refs_0_), channel_id=1, source_target_pairs={{0,3},{1,0},{2,1},{3,2},{4,7},{5,4},{6,5},{7,6},{8,11},{9,8},{10,9... | collective-permute-start | bytes 1572872 | tf_op jit(solution)/shard_map/ppermute | solution.py:494
  132.7 1.8 collective-permute-start.14
  180.0 4.9 %collective-permute-start.18 = (bf16[256,512]{1,0:T(8,128)(2,1)S(1)}, bf16[256,512]{1,0:T(8,128)(2,1)S(1)}, u32[]{:S(2)}, u32[]{:S(2)}) collective-permute-start(bf16[256,512]{1,0:T(8,128)(2,1)S(1)} %get-tuple-element.56.refs_0_), channel_id=1, source_target_pairs={{0,4},{4,0},{8,12},{12,8},{1,5},{5,1},{9,13},{13,9},{2,6},{6,2},{1... | collective-permute-start | bytes 786440 | tf_op jit(solution)/shard_map/ppermute | solution.py:502
  184.4 7.8 %collective-permute-start.19 = (bf16[256,1024]{1,0:T(8,128)(2,1)S(1)}, bf16[256,1024]{1,0:T(8,128)(2,1)S(1)}, u32[]{:S(2)}, u32[]{:S(2)}) collective-permute-start(bf16[256,1024]{1,0:T(8,128)(2,1)S(1)} %get-tuple-element.57.refs_0_), channel_id=1, source_target_pairs={{0,4},{4,0},{8,12},{12,8},{1,5},{5,1},{9,13},{13,9},{2,6},{6,2},{1... | collective-permute-start | bytes 1572872 | tf_op jit(solution)/shard_map/ppermute | solution.py:502
  185.6 8.1 %collective-permute-start.20 = (bf16[128,512]{1,0:T(8,128)(2,1)S(1)}, bf16[128,512]{1,0:T(8,128)(2,1)S(1)}, u32[]{:S(2)}, u32[]{:S(2)}) collective-permute-start(bf16[128,512]{1,0:T(8,128)(2,1)S(1)} %add_convert_fusion.6.refs_1_), channel_id=1, source_target_pairs={{0,8},{4,12},{8,0},{12,4},{1,9},{5,13},{9,1},{13,5},{2,10},{6,14},... | collective-permute-start | bytes 393224 | tf_op jit(solution)/shard_map/ppermute | solution.py:502
  192.1 7.7 %collective-permute-start.21 = (bf16[256,1536]{1,0:T(8,128)(2,1)S(1)}, bf16[256,1536]{1,0:T(8,128)(2,1)S(1)}, u32[]{:S(2)}, u32[]{:S(2)}) collective-permute-start(bf16[256,1536]{1,0:T(8,128)(2,1)S(1)} %get-tuple-element.59.refs_0_), channel_id=1, source_target_pairs={{0,4},{4,0},{8,12},{12,8},{1,5},{5,1},{9,13},{13,9},{2,6},{6,2},{1... | collective-permute-start | bytes 2359304 | tf_op jit(solution)/shard_map/ppermute | solution.py:502
  192.2 8.8 %collective-permute-start.22 = (bf16[128,1024]{1,0:T(8,128)(2,1)S(1)}, bf16[128,1024]{1,0:T(8,128)(2,1)S(1)}, u32[]{:S(2)}, u32[]{:S(2)}) collective-permute-start(bf16[128,1024]{1,0:T(8,128)(2,1)S(1)} %add_convert_fusion.4.refs_1_), channel_id=1, source_target_pairs={{0,8},{4,12},{8,0},{12,4},{1,9},{5,13},{9,1},{13,5},{2,10},{6,14},... | collective-permute-start | bytes 786440 | tf_op jit(solution)/shard_map/ppermute | solution.py:502
  199.5 8.7 %collective-permute-start.23 = (bf16[256,1536]{1,0:T(8,128)(2,1)S(1)}, bf16[256,1536]{1,0:T(8,128)(2,1)S(1)}, u32[]{:S(2)}, u32[]{:S(2)}) collective-permute-start(bf16[256,1536]{1,0:T(8,128)(2,1)S(1)} %get-tuple-element.61.refs_0_), channel_id=1, source_target_pairs={{0,4},{4,0},{8,12},{12,8},{1,5},{5,1},{9,13},{13,9},{2,6},{6,2},{1... | collective-permute-start | bytes 2359304 | tf_op jit(solution)/shard_map/ppermute | solution.py:502
  199.8 11.4 %collective-permute-start.24 = (bf16[128,1536]{1,0:T(8,128)(2,1)S(1)}, bf16[128,1536]{1,0:T(8,128)(2,1)S(1)}, u32[]{:S(2)}, u32[]{:S(2)}) collective-permute-start(bf16[128,1536]{1,0:T(8,128)(2,1)S(1)} %add_convert_fusion.2.refs_1_), channel_id=1, source_target_pairs={{0,8},{4,12},{8,0},{12,4},{1,9},{5,13},{9,1},{13,5},{2,10},{6,14},... | collective-permute-start | bytes 1179656 | tf_op jit(solution)/shard_map/ppermute | solution.py:502
  208.2 7.4 %collective-permute-start.25 = (bf16[256,2048]{1,0:T(8,128)(2,1)S(1)}, bf16[256,2048]{1,0:T(8,128)(2,1)S(1)}, u32[]{:S(2)}, u32[]{:S(2)}) collective-permute-start(bf16[256,2048]{1,0:T(8,128)(2,1)S(1)} %get-tuple-element.63.refs_0_), channel_id=1, source_target_pairs={{0,4},{4,0},{8,12},{12,8},{1,5},{5,1},{9,13},{13,9},{2,6},{6,2},{1... | collective-permute-start | bytes 3145736 | tf_op jit(solution)/shard_map/ppermute | solution.py:502
  208.3 12.0 %collective-permute-start.26 = (bf16[128,1536]{1,0:T(8,128)(2,1)S(1)}, bf16[128,1536]{1,0:T(8,128)(2,1)S(1)}, u32[]{:S(2)}, u32[]{:S(2)}) collective-permute-start(bf16[128,1536]{1,0:T(8,128)(2,1)S(1)} %add_convert_fusion.1.refs_1_), channel_id=1, source_target_pairs={{0,8},{4,12},{8,0},{12,4},{1,9},{5,13},{9,1},{13,5},{2,10},{6,14},... | collective-permute-start | bytes 1179656 | tf_op jit(solution)/shard_map/ppermute | solution.py:502
  215.4 7.8 %collective-permute-start.30 = (bf16[256,1024]{1,0:T(8,128)(2,1)S(1)}, bf16[256,1024]{1,0:T(8,128)(2,1)S(1)}, u32[]{:S(2)}, u32[]{:S(2)}) collective-permute-start(bf16[256,1024]{1,0:T(8,128)(2,1)S(1)} %get-tuple-element.65.refs_0_), channel_id=1, source_target_pairs={{0,4},{4,0},{8,12},{12,8},{1,5},{5,1},{9,13},{13,9},{2,6},{6,2},{1... | collective-permute-start | bytes 1572872 | tf_op jit(solution)/shard_map/ppermute | solution.py:502
  215.7 15.8 %collective-permute-start.28 = (bf16[128,2048]{1,0:T(8,128)(2,1)S(1)}, bf16[128,2048]{1,0:T(8,128)(2,1)S(1)}, u32[]{:S(2)}, u32[]{:S(2)}) collective-permute-start(bf16[128,2048]{1,0:T(8,128)(2,1)S(1)} %add_convert_fusion.refs_1_), channel_id=1, source_target_pairs={{0,8},{4,12},{8,0},{12,4},{1,9},{5,13},{9,1},{13,5},{2,10},{6,14},... | collective-permute-start | bytes 1572872 | tf_op jit(solution)/shard_map/ppermute | solution.py:502
  223.2 5.8 %collective-permute-start.27 = (bf16[256,512]{1,0:T(8,128)(2,1)S(1)}, bf16[256,512]{1,0:T(8,128)(2,1)S(1)}, u32[]{:S(2)}, u32[]{:S(2)}) collective-permute-start(bf16[256,512]{1,0:T(8,128)(2,1)S(1)} %get-tuple-element.68), channel_id=1, source_target_pairs={{0,4},{4,0},{8,12},{12,8},{1,5},{5,1},{9,13},{13,9},{2,6},{6,2},{1... | collective-permute-start | bytes 786440 | tf_op jit(solution)/shard_map/ppermute | solution.py:502
  223.3 13.8 %collective-permute-start.31 = (bf16[128,1024]{1,0:T(8,128)(2,1)S(1)}, bf16[128,1024]{1,0:T(8,128)(2,1)S(1)}, u32[]{:S(2)}, u32[]{:S(2)}) collective-permute-start(bf16[128,1024]{1,0:T(8,128)(2,1)S(1)} %add_convert_fusion.3), channel_id=1, source_target_pairs={{0,8},{4,12},{8,0},{12,4},{1,9},{5,13},{9,1},{13,5},{2,10},{6,14},... | collective-permute-start | bytes 786440 | tf_op jit(solution)/shard_map/ppermute | solution.py:502
  231.6 8.0 %collective-permute-start.29 = (bf16[128,512]{1,0:T(8,128)(2,1)S(1)}, bf16[128,512]{1,0:T(8,128)(2,1)S(1)}, u32[]{:S(2)}, u32[]{:S(2)}) collective-permute-start(bf16[128,512]{1,0:T(8,128)(2,1)S(1)} %pass_on.3), channel_id=1, source_target_pairs={{0,8},{4,12},{8,0},{12,4},{1,9},{5,13},{9,1},{13,5},{2,10},{6,14},... | collective-permute-start | bytes 393224 | tf_op jit(solution)/shard_map/ppermute | solution.py:502
  (30 other events, 362.7 us)
